TPU v7x, 32 devices: a whole 2x2x4 slice. The times are simulated.
32 devices in a mesh: rows: 8 (over z, y), seq: 4 (over x, core).
Axes of the slice: x: 2, y: 2, z: 4, core: 2. Of those that a mesh axis runs over, the one named last changes fastest.
Arguments:
- residual_in: bfloat16 [8, 2048, 3200], P('rows', 'seq'), may hold values from -6 to 6
- norm_gain: float32 [3200], replicated, may hold values from 0.1 to 1.9
- qkv_weight: bfloat16 [3200, 6144], P(None, 'seq')
- qk_gain: float32 [2, 2048], P(None, 'seq')
- out_weight: bfloat16 [2048, 3200], P('seq'), may hold values from -0.125 to 0.125
- layer_scale: float32 [3200], replicated, may hold values from 1 to 6
- segment_ids: int32 [8, 2048], P('rows', 'seq'), may hold values from 0 to 2, as said below
- pad_mask: int32 [8, 2048], P('rows', 'seq'), may hold values from 0 to 1, as said below
- ln_weight: float32 [12800], replicated, may hold values from 0.1 to 1.9
- ln_bias: float32 [12800], replicated, may hold values from -3 to 3
- fc_weight: bfloat16 [12800, 6144], P('rows'), may hold values from -0.0546875 to 0.0546875
- fc_bias: float32 [6144], replicated, may hold values from -3 to 3
- owner: int32 [8], replicated, may hold values from 0 to 7, each once
Outputs:
- features: bfloat16 [8, 512, 6144], P('rows', 'seq')
Inputs may be any that keep to these rules, and one draw needn't show every extreme that they name: `segment_ids`: within a row, segment ids never fall and change only at multiples of 1024 tokens; picture tokens carry ids below 2, padding tokens carry 2 and stand at the end of the row; the first tile is never padding. pad_mask is 0 exactly where segment_ids equals 2. `owner`: each index of rows owns exactly one row.
All inputs are finite; a program needn't handle non-finite values.
Results may differ from a plain program's by a relative error of at most 0.025.
Values may be sent and summed in bfloat16 or wider, within the bound.
No kernel may reach another device: no remote copies, remote signals or barrier semaphores. Data moves between devices by JAX's collectives and lax.ppermute only.
A program may use at most 128 MiB of HBM per device.

v0:
```python
import jax
import jax.numpy as jnp
from jax import lax
from jax.sharding import PartitionSpec as P

D = 3200
HEAD_DIM = 128
HEADS = 16
GRID = 32


def attend_dense(query_norm, key_norm, value_half, row_segments, block_len, scale):
    length, heads_here = (query_norm.shape[0], query_norm.shape[1])
    block_count = length // block_len

    def one_block(packed):
        query_block, query_seg = packed
        scores = (
            jnp.einsum("qhd,khd->hqk", query_block, key_norm, preferred_element_type=jnp.float32)
            * scale
        )
        same_seg = (query_seg[:, None] == row_segments[None, :])[None]
        scores = jnp.where(same_seg, scores, -1e30)
        peak_val = jnp.max(scores, axis=-1, keepdims=True)
        exp_terms = jnp.exp(scores - peak_val)
        probs = (exp_terms / jnp.sum(exp_terms, axis=-1, keepdims=True)).astype(jnp.bfloat16)
        return jnp.einsum(
            "hqk,khd->qhd", probs, value_half, preferred_element_type=jnp.float32
        ).astype(jnp.bfloat16)

    blocks_out = lax.map(
        one_block,
        (
            query_norm.reshape(block_count, block_len, heads_here, HEAD_DIM),
            row_segments.reshape(block_count, block_len),
        ),
    )
    return blocks_out.reshape(length, heads_here * HEAD_DIM)


def per_device(
    residual_in,
    norm_gain,
    qkv_weight,
    qk_gain,
    out_weight,
    layer_scale,
    segment_ids,
    pad_mask,
    ln_weight,
    ln_bias,
    fc_weight,
    fc_bias,
    owner,
):
    tokens = residual_in[0].astype(jnp.float32)
    shard_rows = tokens.shape[0]
    normed = (
        tokens * lax.rsqrt(jnp.mean(tokens * tokens, axis=-1, keepdims=True) + 1e-06) * norm_gain
    ).astype(jnp.bfloat16)
    row_tokens, row_segments = (
        lax.all_gather(normed, "seq", axis=0, tiled=True),
        lax.all_gather(segment_ids[0].astype(jnp.bfloat16), "seq", axis=0, tiled=True),
    )
    length = row_tokens.shape[0]
    heads_here = qkv_weight.shape[1] // (3 * HEAD_DIM)
    projected = jnp.dot(row_tokens, qkv_weight, preferred_element_type=jnp.float32).reshape(
        length, heads_here, 3, HEAD_DIM
    )
    query_raw = projected[:, :, 0]
    key_raw = projected[:, :, 1]
    value_half = projected[:, :, 2].astype(jnp.bfloat16)
    query_sq, key_sq = lax.psum(
        (jnp.sum(query_raw * query_raw, axis=(1, 2)), jnp.sum(key_raw * key_raw, axis=(1, 2))),
        "seq",
    )
    norm_width = HEADS * HEAD_DIM
    gain_pair = qk_gain.reshape(2, heads_here, HEAD_DIM)
    query_norm = (
        query_raw * lax.rsqrt(query_sq / norm_width + 1e-06)[:, None, None] * gain_pair[0]
    ).astype(jnp.bfloat16)
    key_norm = (
        key_raw * lax.rsqrt(key_sq / norm_width + 1e-06)[:, None, None] * gain_pair[1]
    ).astype(jnp.bfloat16)
    block_len = min(512, length)
    scale = HEAD_DIM ** (-0.5)
    attended = attend_dense(query_norm, key_norm, value_half, row_segments, block_len, scale)
    piece = attended
    attn = lax.psum_scatter(
        jnp.dot(piece, out_weight, preferred_element_type=jnp.float32).astype(jnp.bfloat16),
        "seq",
        scatter_dimension=0,
        tiled=True,
    ).astype(jnp.float32)
    hidden = tokens + layer_scale * attn
    half_grid = GRID // 2
    lines = shard_rows // (2 * GRID)
    merged_count = shard_rows // 4
    merged = jnp.transpose(hidden.reshape(lines, 2, half_grid, 2, D), (0, 2, 1, 3, 4)).reshape(
        merged_count, 4 * D
    )
    centre = merged - jnp.mean(merged, axis=-1, keepdims=True)
    spread = jnp.mean(centre * centre, axis=-1, keepdims=True)
    merged_norm = (centre * lax.rsqrt(spread + 1e-05) * ln_weight + ln_bias).astype(jnp.bfloat16)
    merged_mask = (
        pad_mask[0]
        .reshape(lines, 2, half_grid, 2)[:, 0, :, 0]
        .reshape(merged_count)
        .astype(jnp.bfloat16)
    )
    row_count = lax.axis_size("rows")
    mask_spread = jnp.broadcast_to(merged_mask[:, None], (merged_count, row_count))
    slabs, slab_mask = (
        lax.all_to_all(merged_norm, "rows", split_axis=1, concat_axis=0, tiled=True),
        lax.all_to_all(mask_spread, "rows", split_axis=1, concat_axis=0, tiled=True),
    )
    owner_hot = (owner[None, :] == jnp.arange(row_count, dtype=jnp.int32)[:, None]).astype(
        jnp.bfloat16
    )
    ordered = jnp.einsum(
        "jp,pms->jms",
        owner_hot,
        slabs.reshape(row_count, merged_count, -1),
        preferred_element_type=jnp.float32,
    ).astype(jnp.bfloat16)
    ordered = ordered.reshape(row_count * merged_count, -1)
    ordered_mask = jnp.einsum(
        "jp,pms->jms",
        owner_hot,
        slab_mask.reshape(row_count, merged_count, 1),
        preferred_element_type=jnp.float32,
    )
    ordered_mask = ordered_mask.reshape(row_count * merged_count)
    piece = ordered
    summed = lax.psum_scatter(
        jnp.dot(piece, fc_weight, preferred_element_type=jnp.float32).astype(jnp.bfloat16),
        "rows",
        scatter_dimension=0,
        tiled=True,
    ).astype(jnp.float32)
    own_mask = lax.dynamic_slice_in_dim(
        ordered_mask, lax.axis_index("rows") * merged_count, merged_count, 0
    )
    result = jax.nn.gelu(summed + fc_bias, approximate=False) * own_mask[:, None]
    return result.astype(jnp.bfloat16)[None]


def solution(mesh):
    return jax.shard_map(
        per_device,
        mesh=mesh,
        in_specs=(
            P("rows", "seq", None),
            P(),
            P(None, "seq"),
            P(None, "seq"),
            P("seq", None),
            P(),
            P("rows", "seq"),
            P("rows", "seq"),
            P(),
            P(),
            P("rows", None),
            P(),
            P(),
        ),
        out_specs=P("rows", "seq", None),
        check_vma=False,
    )
```

profile of v0, /device:TPU:0, one launch (start us, length us, event | category | flops | bytes accessed | tf_op | source)
XLA Modules:
  0.0 767.4 jit_solution(11750310285934367138)
XLA Ops:
  6.5 2.8 fusion.27
  9.3 0.3 copy-done.3
  9.6 3.5 fusion.29
  13.2 0.6 copy-done.10
  13.8 6.1 all-gather
  20.0 81.1 %all-gather.3.cloned.1.call-done = bf16[2048,3200]{1,0:T(8,128)(2,1)} async-done(((bf16[512,3200]{1,0:T(8,128)(2,1)}), bf16[2048,3200]{1,0:T(8,128)(2,1)}) %all-gather.3.cloned.1.call-update) | async-done | bytes 13107216 | tf_op jit(solution)/shard_map/all_gather | solution.py:62
  101.1 28.5 %fusion.72 = f32[2048,1536]{0,1:T(8,128)} fusion(bf16[2048,3200]{1,0:T(8,128)(2,1)} %all-gather.3.cloned.1.call-done, bf16[3200,1536]{1,0:T(8,128)(2,1)} %param.17), kind=kOutput, calls=%fused_computation.93 | convolution fusion | flops 20132659200 | bytes 35520512 | tf_op jit(solution)/shard_map/dot_general | solution.py:67
  129.6 7.8 %fusion.70 = (f32[2048,4,1,128]{0,3,2,1:T(8,128)}, f32[2048,4,1,128]{0,3,2,1:T(8,128)}) fusion(f32[2048,4,3,128]{0,3,2,1:T(8,128)} %bitcast.92), kind=kLoop, calls=%fused_computation.91 | loop fusion | bytes 16777216 | tf_op jit(solution)/shard_map/slice | solution.py:71
  137.4 3.9 slice.30
  141.3 5.3 copy.48
  146.7 2.5 fusion.30
  149.2 5.4 copy.47
  154.6 2.5 multiply_reduce_fusion.1
  157.1 10.5 %all-reduce = (f32[2048]{0:T(1024)S(1)}, f32[2048]{0:T(1024)S(1)}) all-reduce(f32[2048]{0:T(1024)S(1)} %multiply_reduce_fusion.1, f32[2048]{0:T(1024)S(1)} %fusion.30), channel_id=1, replica_groups=mesh['rows'=8,'seq'=4] {'seq'}, use_global_device_ids=true, to_apply=%region_2.0 | all-reduce | flops 4096 | bytes 32768 | tf_op jit(solution)/shard_map/psum | solution.py:73
  167.7 4.0 copy.49
  171.6 4.2 fusion.32
  175.8 2.0 multiply_convert_fusion
  177.8 91.2 %while.10 = (s32[]{:T(128)}, bf16[4,512,4,128]{3,2,1,0:T(4,128)(2,1)}, bf16[4,512]{1,0:T(4,128)(2,1)S(1)}, bf16[2048]{0:T(1024)(128)(2,1)S(1)}, bf16[4,512,4,128...) while((s32[]{:T(128)}, ...), condition=%wide.region_8.9_spmd, body=%wide.region_5.8_spmd.sunk | while | flops 2173962240 | bytes 41967704 | solution.py:31
  177.8 1.6 broadcast_compare_fusion.2
  179.4 11.2 %fusion.88 = (f32[4,512]{1,0:T(4,128)S(1)}, f32[4,512,2048]{2,1,0:T(8,128)}) fusion(pred[512,2048]{1,0:T(8,128)(4,1)} %broadcast_compare_fusion.2, bf16[2048,4,128]{2,0,1:T(8,128)(2,1)} %get-tuple-element.154, bf16[4,512,4,128]{3,1,0,2:T(8,128)(2,1)} %get-tuple-element.153, s32[]{:T(128)} %get-tuple-element.141), kind=kOutput, calls=%fused_computation.90.clone.1 | convolution fusion | flops 1090521088 | bytes 20455936 | tf_op jit(solution)/shard_map/while/body/eval_jaxpr/sub | solution.py:25
  190.6 8.7 %fusion.89 = bf16[1,512,4,128]{3,1,2,0:T(8,128)(2,1)S(1)} fusion(bf16[2048,4,128]{2,0,1:T(8,128)(2,1)} %get-tuple-element.155, f32[4,512,2048]{2,1,0:T(8,128)} %get-tuple-element.131, f32[4,512]{1,0:T(4,128)S(1)} %get-tuple-element.132), kind=kOutput, calls=%fused_computation.11.clone.1 | convolution fusion | flops 1082392576 | bytes 19406848 | tf_op jit(solution)/shard_map/while/body/eval_jaxpr/hqk,khd->qhd/dot_general | solution.py:27
  199.4 1.3 copy_dynamic-update-slice_fusion.2
  200.7 1.6 broadcast_compare_fusion.2
  202.3 11.2 %fusion.88 = (f32[4,512]{1,0:T(4,128)S(1)}, f32[4,512,2048]{2,1,0:T(8,128)}) fusion(pred[512,2048]{1,0:T(8,128)(4,1)} %broadcast_compare_fusion.2, bf16[2048,4,128]{2,0,1:T(8,128)(2,1)} %get-tuple-element.154, bf16[4,512,4,128]{3,1,0,2:T(8,128)(2,1)} %get-tuple-element.153, s32[]{:T(128)} %get-tuple-element.141), kind=kOutput, calls=%fused_computation.90.clone.1 | convolution fusion | flops 1090521088 | bytes 20455936 | tf_op jit(solution)/shard_map/while/body/eval_jaxpr/sub | solution.py:25
  213.5 8.7 %fusion.89 = bf16[1,512,4,128]{3,1,2,0:T(8,128)(2,1)S(1)} fusion(bf16[2048,4,128]{2,0,1:T(8,128)(2,1)} %get-tuple-element.155, f32[4,512,2048]{2,1,0:T(8,128)} %get-tuple-element.131, f32[4,512]{1,0:T(4,128)S(1)} %get-tuple-element.132), kind=kOutput, calls=%fused_computation.11.clone.1 | convolution fusion | flops 1082392576 | bytes 19406848 | tf_op jit(solution)/shard_map/while/body/eval_jaxpr/hqk,khd->qhd/dot_general | solution.py:27
  222.2 1.2 copy_dynamic-update-slice_fusion.2
  223.5 1.6 broadcast_compare_fusion.2
  225.0 11.2 %fusion.88 = (f32[4,512]{1,0:T(4,128)S(1)}, f32[4,512,2048]{2,1,0:T(8,128)}) fusion(pred[512,2048]{1,0:T(8,128)(4,1)} %broadcast_compare_fusion.2, bf16[2048,4,128]{2,0,1:T(8,128)(2,1)} %get-tuple-element.154, bf16[4,512,4,128]{3,1,0,2:T(8,128)(2,1)} %get-tuple-element.153, s32[]{:T(128)} %get-tuple-element.141), kind=kOutput, calls=%fused_computation.90.clone.1 | convolution fusion | flops 1090521088 | bytes 20455936 | tf_op jit(solution)/shard_map/while/body/eval_jaxpr/sub | solution.py:25
  236.2 8.7 %fusion.89 = bf16[1,512,4,128]{3,1,2,0:T(8,128)(2,1)S(1)} fusion(bf16[2048,4,128]{2,0,1:T(8,128)(2,1)} %get-tuple-element.155, f32[4,512,2048]{2,1,0:T(8,128)} %get-tuple-element.131, f32[4,512]{1,0:T(4,128)S(1)} %get-tuple-element.132), kind=kOutput, calls=%fused_computation.11.clone.1 | convolution fusion | flops 1082392576 | bytes 19406848 | tf_op jit(solution)/shard_map/while/body/eval_jaxpr/hqk,khd->qhd/dot_general | solution.py:27
  245.0 1.2 copy_dynamic-update-slice_fusion.2
  246.2 1.6 broadcast_compare_fusion.2
  247.8 11.2 %fusion.88 = (f32[4,512]{1,0:T(4,128)S(1)}, f32[4,512,2048]{2,1,0:T(8,128)}) fusion(pred[512,2048]{1,0:T(8,128)(4,1)} %broadcast_compare_fusion.2, bf16[2048,4,128]{2,0,1:T(8,128)(2,1)} %get-tuple-element.154, bf16[4,512,4,128]{3,1,0,2:T(8,128)(2,1)} %get-tuple-element.153, s32[]{:T(128)} %get-tuple-element.141), kind=kOutput, calls=%fused_computation.90.clone.1 | convolution fusion | flops 1090521088 | bytes 20455936 | tf_op jit(solution)/shard_map/while/body/eval_jaxpr/sub | solution.py:25
  259.0 8.7 %fusion.89 = bf16[1,512,4,128]{3,1,2,0:T(8,128)(2,1)S(1)} fusion(bf16[2048,4,128]{2,0,1:T(8,128)(2,1)} %get-tuple-element.155, f32[4,512,2048]{2,1,0:T(8,128)} %get-tuple-element.131, f32[4,512]{1,0:T(4,128)S(1)} %get-tuple-element.132), kind=kOutput, calls=%fused_computation.11.clone.1 | convolution fusion | flops 1082392576 | bytes 19406848 | tf_op jit(solution)/shard_map/while/body/eval_jaxpr/hqk,khd->qhd/dot_general | solution.py:27
  267.8 1.2 copy_dynamic-update-slice_fusion.2
  269.0 12.5 %convolution_convert_fusion = bf16[2048,3200]{1,0:T(8,128)(2,1)} fusion(bf16[512,3200]{1,0:T(8,128)(2,1)S(1)} %copy-done, bf16[256,8,4,128]{3,2,1,0:T(4,128)(2,1)} %bitcast.23), kind=kOutput, calls=%fused_computation.24 | convolution fusion | flops 6717440000 | bytes 18481152 | tf_op jit(solution)/shard_map/dot_general | solution.py:90
  281.6 0.7 copy-done.4
  282.3 0.1 add.72
  282.4 0.1 mul.150
  282.5 102.8 %reduce-scatter.3.cloned.1.call-done = bf16[512,3200]{1,0:T(8,128)(2,1)} async-done(((bf16[2048,3200]{1,0:T(8,128)(2,1)}), bf16[512,3200]{1,0:T(8,128)(2,1)}) %reduce-scatter.3.cloned.1.call-update) | async-done | bytes 3276816 | tf_op jit(solution)/shard_map/reduce_scatter | solution.py:89
  385.3 6.5 convert_add_fusion
  391.8 8.3 %reshape.166 = f32[8,2,16,2,3200]{4,3,2,1,0:T(2,128)} reshape(f32[512,3200]{1,0:T(8,128)} %convert_add_fusion) | data formatting | bytes 13107200 | tf_op jit(solution)/shard_map/reshape | solution.py:99
  400.1 4.4 fusion.64
  404.4 0.4 copy-done.1
  404.8 3.6 multiply_reduce_fusion
  408.5 0.1 div.33
  408.5 7.8 %copy.76 = f32[8,2,16,2,3200]{4,3,1,2,0:T(2,128)} copy(f32[8,2,16,2,3200]{4,3,2,1,0:T(2,128)} %reshape.166) | data formatting | bytes 13107200 | tf_op jit(solution)/shard_map/reshape | solution.py:99
  416.3 0.1 rsqrt.29
  416.4 9.4 %reshape.167 = f32[128,8,1600]{2,1,0:T(8,128)} reshape(f32[8,16,2,2,3200]{4,3,2,1,0:T(2,128)} %bitcast.91) | data formatting | bytes 13107200 | tf_op jit(solution)/shard_map/reshape | solution.py:99
  425.9 4.9 add_convert_fusion
  430.8 5.9 copy.41
  436.6 79.8 %all_to_all.26 = bf16[128,8,1600]{0,2,1:T(8,128)(2,1)S(1)} all-to-all(bf16[128,8,1600]{0,2,1:T(8,128)(2,1)} %copy.41), channel_id=1, replica_groups=mesh['rows'=8,'seq'=4] {'rows'}, dimensions={1} | all-to-all | bytes 6553600 | tf_op jit(solution)/shard_map/all_to_all | solution.py:114
  516.4 2.0 fusion.52
  518.4 28.0 %convolution_convert_fusion.1 = bf16[1024,6144]{1,0:T(8,128)(2,1)} fusion(bf16[1600,6144]{1,0:T(8,128)(2,1)} %param.25, bf16[200,8,8,128]{3,2,1,0:T(8,128)(2,1)S(1)} %bitcast.94), kind=kOutput, calls=%fused_computation.25 | convolution fusion | flops 20138950656 | bytes 35520512 | tf_op jit(solution)/shard_map/dot_general | solution.py:136
  546.4 0.7 copy-done.9
  547.1 0.2 reshape_squeeze.5
  547.2 0.1 slice_reduce_fusion
  547.3 0.1 convert_element_type.80
  547.4 0.6 broadcast_in_dim.28
  548.0 3.3 all-to-all-start.1
  551.3 6.7 all-to-all-done.1
  558.1 0.1 convolution_bitcast_fusion
  558.2 0.1 dynamic_slice.11
  558.3 193.4 %reduce-scatter.5.cloned.1.call-done = bf16[128,6144]{1,0:T(8,128)(2,1)} async-done(((bf16[1024,6144]{1,0:T(8,128)(2,1)}), bf16[128,6144]{1,0:T(8,128)(2,1)}) %reduce-scatter.5.cloned.1.call-update) | async-done | bytes 1572880 | tf_op jit(solution)/shard_map/reduce_scatter | solution.py:135
  751.7 8.8 %fusion.57 = bf16[1,128,6144]{2,1,0:T(8,128)(2,1)} fusion(bf16[128,6144]{1,0:T(8,128)(2,1)} %reduce-scatter.5.cloned.1.call-done, f32[128]{0:T(128)S(1)} %dynamic_slice.11, f32[6144]{0:T(1024)S(1)} %copy-done.6), kind=kLoop, calls=%fused_computation.74 | loop fusion | flops 53477376 | bytes 3170816 | tf_op jit(solution)/shard_map/broadcast_in_dim | solution.py:145
  (41 shorter events, 0.4 us)
Async XLA Ops:
  6.5 262.5 %copy-start = (bf16[512,3200]{1,0:T(8,128)(2,1)S(1)}, bf16[512,3200]{1,0:T(8,128)(2,1)}, u32[]{:S(2)}) copy-start(bf16[512,3200]{1,0:T(8,128)(2,1)} %param.19) | copy-start | bytes 9830404
  6.5 94.5 %all-gather.3.cloned.1.call-start = ((), (), s32[]{:S(2)}) async-start(), calls=%async_computation.4 | async-start | bytes 16384000 | tf_op jit(solution)/shard_map/all_gather | solution.py:62
  6.5 3.1 copy-start.3
  13.1 0.7 copy-start.10
  13.1 6.8 copy-start.8
  13.1 372.1 %reduce-scatter.3.cloned.1.call-start = ((), (), s32[]{:S(2)}) async-start(), calls=%async_computation.5 | async-start | bytes 16384000 | tf_op jit(solution)/shard_map/reduce_scatter | solution.py:89
  171.6 4.2 copy-start.2
  281.5 0.8 copy-start.4
  281.5 0.9 copy-start.5
  281.5 103.8 %copy-start.7 = (f32[3200]{0:T(1024)S(1)}, f32[3200]{0:T(1024)}, u32[]{:S(2)}) copy-start(f32[3200]{0:T(1024)} %param.20) | copy-start | bytes 38404
  281.5 470.1 %reduce-scatter.5.cloned.1.call-start = ((), (), s32[]{:S(2)}) async-start(), calls=%async_computation.6 | async-start | bytes 14155776 | tf_op jit(solution)/shard_map/reduce_scatter | solution.py:135
  400.1 4.7 copy-start.1
  436.6 79.8 %copy-start.11 = (s32[8]{0:T(128)S(1)}, s32[8]{0:T(128)}, u32[]{:S(2)}) copy-start(s32[8]{0:T(128)} %param.27) | copy-start | bytes 100
  546.4 0.7 copy-start.9
  546.4 205.3 %copy-start.6 = (f32[6144]{0:T(1024)S(1)}, f32[6144]{0:T(1024)}, u32[]{:S(2)}) copy-start(f32[6144]{0:T(1024)} %param.26) | copy-start | bytes 73732
  548.0 10.1 %all-to-all-start.1 = ((bf16[128,8,1]{0,2,1:T(2,128)(2,1)}), bf16[128,8,1]{0,2,1:T(2,128)(2,1)S(1)}, u32[]{:S(2)}, u32[]{:S(2)}) async-start(bf16[128,8,1]{0,2,1:T(2,128)(2,1)} %broadcast_in_dim.28), calls=%async_computation.3 | async-start | bytes 8192 | tf_op jit(solution)/shard_map/all_to_all | solution.py:115
Sparse Core Ops, SparseCore 0:
  13.3 87.7 all-gather.2
  281.7 103.5 reduce-scatter.2
  546.5 205.1 reduce-scatter.4
where the time goes:
time: 776 us; the launch traced here: 767 us
  waiting for transfers between devices  384 us (49%)
  matrix products  151 us (19%)
  blocking collectives  96.4 us (12%)
  local copies, waits for them, and re-layouts  66.8 us (9%)
  other arithmetic  52.2 us (7%)
  between operations  13.7 us (2%)
    reduce_scatter x1, waiting for transfers between devices, per_device(): lax.psum_scatter(jnp.dot(piece, fc_weight, preferred_element_type=jnp.flo...  193 us
    reduce_scatter x1, waiting for transfers between devices, per_device(): lax.psum_scatter(jnp.dot(piece, out_weight, preferred_element_type=jnp.fl...  103 us
    all_gather x1, waiting for transfers between devices, per_device(): lax.all_gather(normed, 'seq', axis=0, tiled=True)  81.1 us
    all_to_all x1, blocking collectives, per_device(): lax.all_to_all(merged_norm, 'rows', split_axis=1, concat_axis=0, tiled=True)  79.8 us
    sub x4, matrix products, one_block(): exp_terms = jnp.exp(scores - peak_val)  44.8 us
    dot_general x4, matrix products, one_block(): jnp.einsum('hqk,khd->qhd', probs, value_half, preferred_element_type=jnp....  35 us
    dot_general x1, matrix products, per_device(): jnp.dot(row_tokens, qkv_weight, preferred_element_type=jnp.float32)  28.5 us
    dot_general x1, matrix products, per_device(): jnp.dot(piece, fc_weight, preferred_element_type=jnp.float32)  28 us
  transfers between devices with their start and end apart: 4, of which 4 were waited for; matrix products, arithmetic and copies ran while one was open for 0% of the time, Pallas kernels for 0%

commit v1 on v0

v1 whole, which is shorter than its diff:
```python
import functools
import math

import jax
import jax.numpy as jnp
import numpy as np
from jax import lax
from jax.experimental import pallas as pl
from jax.experimental.pallas import tpu as pltpu
from jax.sharding import PartitionSpec as P

D = 3200
HEAD_DIM = 128
HEADS = 16
GRID = 32
TILE = GRID * GRID
SUBS = 4
CHUNKS = 2
HALVES = 2
MIB = 1024 * 1024
BF16 = jnp.bfloat16
F32 = jnp.float32


def reorder_kernel(pick_ref, x_ref, out_ref):
    out_ref[...] = jnp.dot(pick_ref[...], x_ref[...], preferred_element_type=F32).astype(BF16)


def reorder(x, chunk):
    lines = chunk // (2 * GRID)
    source = np.arange(chunk).reshape(lines, 2, GRID // 2, 2).transpose(1, 3, 0, 2).reshape(chunk)
    pick = jnp.asarray(np.eye(chunk, dtype=np.float32)[source], BF16)
    return pl.pallas_call(
        reorder_kernel,
        grid=(x.shape[0] // chunk,),
        in_specs=[
            pl.BlockSpec((chunk, chunk), lambda i: (0, 0)),
            pl.BlockSpec((chunk, D), lambda i: (i, 0)),
        ],
        out_specs=pl.BlockSpec((chunk, D), lambda i: (i, 0)),
        out_shape=jax.ShapeDtypeStruct(x.shape, BF16),
        cost_estimate=pl.CostEstimate(
            flops=2 * x.shape[0] * chunk * D, bytes_accessed=4 * x.size, transcendentals=0
        ),
        compiler_params=pltpu.CompilerParams(vmem_limit_bytes=32 * MIB),
        name="reorder",
    )(pick, x)


def qkv_kernel(count, *refs):
    x_refs, gain_ref, w_ref = refs[:count], refs[count], refs[count + 1]
    out_refs = refs[count + 2 : 2 * count + 2]
    sq_refs = refs[2 * count + 2 : 3 * count + 2]
    normed, q_acc, k_acc = refs[3 * count + 2 :]
    head = pl.program_id(0)
    rows = x_refs[0].shape[0]
    step = 64

    @pl.when(head == 0)
    def _():
        for i in range(count):

            @pl.loop(0, rows // step)
            def _(b):
                part = pl.ds(pl.multiple_of(b * step, step), step)
                x = x_refs[i][part, :].astype(F32)
                inv = lax.rsqrt(jnp.mean(x * x, axis=-1, keepdims=True) + 1e-06)
                normed[i, part, :] = (x * inv * gain_ref[...]).astype(BF16)

        q_acc[...] = jnp.zeros_like(q_acc)
        k_acc[...] = jnp.zeros_like(k_acc)

    for i in range(count):
        product = jnp.dot(normed[i], w_ref[...], preferred_element_type=F32)
        out_refs[i][...] = product
        for first in range(0, product.shape[1], 3 * HEAD_DIM):
            q = product[:, first : first + HEAD_DIM]
            k = product[:, first + HEAD_DIM : first + 2 * HEAD_DIM]
            q_acc[i] += q * q
            k_acc[i] += k * k

    @pl.when(head == pl.num_programs(0) - 1)
    def _():
        for i in range(count):
            sq_refs[i][0:1, :] = jnp.sum(q_acc[i].T, axis=0, keepdims=True)
            sq_refs[i][1:2, :] = jnp.sum(k_acc[i].T, axis=0, keepdims=True)


def project(pieces, norm_gain, qkv_weight):
    count = len(pieces)
    rows = pieces[0].shape[0]
    width = qkv_weight.shape[1]
    heads = width // (3 * HEAD_DIM)
    block = 3 * HEAD_DIM * (2 if heads % 2 == 0 else 1)
    results = pl.pallas_call(
        functools.partial(qkv_kernel, count),
        grid=(width // block,),
        in_specs=[pl.BlockSpec((rows, D), lambda h: (0, 0))] * count
        + [
            pl.BlockSpec((1, D), lambda h: (0, 0)),
            pl.BlockSpec((D, block), lambda h: (0, h)),
        ],
        out_specs=[pl.BlockSpec((rows, block), lambda h: (0, h))] * count
        + [pl.BlockSpec((2, rows), lambda h: (0, 0))] * count,
        out_shape=[jax.ShapeDtypeStruct((rows, width), F32)] * count
        + [jax.ShapeDtypeStruct((2, rows), F32)] * count,
        scratch_shapes=[
            pltpu.VMEM((count, rows, D), BF16),
            pltpu.VMEM((count, rows, HEAD_DIM), F32),
            pltpu.VMEM((count, rows, HEAD_DIM), F32),
        ],
        cost_estimate=pl.CostEstimate(
            flops=2 * count * rows * D * width,
            bytes_accessed=2 * D * width + count * rows * (2 * D + 4 * width),
            transcendentals=0,
        ),
        compiler_params=pltpu.CompilerParams(vmem_limit_bytes=56 * MIB),
        name="qkv",
    )(*pieces, norm_gain.reshape(1, D), qkv_weight)
    return results[:count], results[count:]


def attend_kernel(plan, rows, first, chunk, group, *refs):
    count = len(plan)
    blocks = plan[-1][0] + 1
    seg_ref, sq_ref, gain_ref = refs[:3]
    p_refs = refs[3 : 3 + count]
    out_ref, q_scale, k_scale, q_all, k_all, v_all = refs[3 + count :]
    head = pl.program_id(0)
    factor = HEAD_DIM ** (-0.5) * math.log2(math.e)

    @pl.when(head == 0)
    def _():
        inv = lax.rsqrt(sq_ref[...] / (HEADS * HEAD_DIM) + 1e-06)
        for d in range(blocks):
            part = slice(d * rows, (d + 1) * rows)
            k_scale[part, :] = jnp.broadcast_to(inv[1:2, part], (HEAD_DIM, rows)).T
            q_wide = jnp.broadcast_to(inv[0:1, part] * factor, (HEAD_DIM, rows)).T
            q_scale[d * chunk : (d + 1) * chunk, :] = q_wide[first : first + chunk, :]
        v_all[:, HEAD_DIM:] = jnp.ones_like(v_all[:, HEAD_DIM:])

    for (d, start, size), p_ref in zip(plan, p_refs):
        part = slice(d * rows + start, d * rows + start + size)
        k = p_ref[:, HEAD_DIM : 2 * HEAD_DIM]
        k_all[part, :] = (k * k_scale[part, :] * gain_ref[1:2, :]).astype(BF16)
        v_all[part, :HEAD_DIM] = p_ref[:, 2 * HEAD_DIM :].astype(BF16)
        low, high = max(first, start), min(first + chunk, start + size)
        if low < high:
            part = slice(d * chunk + low - first, d * chunk + high - first)
            q = p_ref[low - start : high - start, :HEAD_DIM]
            q_all[part, :] = (q * q_scale[part, :] * gain_ref[0:1, :]).astype(BF16)

    groups = blocks // group
    keys = group * rows
    step = min(chunk, 128)

    def attend(d, begin, low, high):
        q = q_all[d * chunk + begin : d * chunk + begin + step, :]
        scores = lax.dot_general(
            q, k_all[low:high, :], (((1,), (1,)), ((), ())), preferred_element_type=F32
        )
        if groups > 2:
            own = d // group
            masked = []
            for g in range(groups):
                part = scores[:, g * keys : (g + 1) * keys]
                if g != own:
                    part = jnp.where(seg_ref[g] == seg_ref[own], part, -1e30)
                masked.append(part)
            scores = jnp.concatenate(masked, axis=1)
        peak = jnp.max(scores, axis=-1, keepdims=True)
        terms = jnp.exp2(scores - peak).astype(BF16)
        both = jnp.dot(terms, v_all[low:high, :], preferred_element_type=F32)
        out_ref[d, begin : begin + step, :] = (
            both[:, :HEAD_DIM] / both[:, HEAD_DIM:]
        ).astype(BF16)

    def attend_all(d, low, high):
        for begin in range(0, chunk, step):
            attend(d, begin, low, high)

    if groups != 2:
        for d in range(blocks):
            attend_all(d, 0, blocks * rows)
    else:
        joint = seg_ref[0] == seg_ref[1]

        @pl.when(joint)
        def _():
            for d in range(blocks):
                attend_all(d, 0, blocks * rows)

        @pl.when(jnp.logical_not(joint))
        def _():
            for d in range(blocks):
                own = d // group
                attend_all(d, own * keys, (own + 1) * keys)


def attend(pieces, plan, rows, squares, segments, qk_gain, first, chunk):
    blocks = plan[-1][0] + 1
    width = pieces[0].shape[1]
    heads = width // (3 * HEAD_DIM)
    total = blocks * rows
    group = max(1, min(blocks, TILE // rows))
    return pl.pallas_call(
        functools.partial(attend_kernel, plan, rows, first, chunk, group),
        grid=(heads,),
        in_specs=[
            pl.BlockSpec(memory_space=pltpu.SMEM),
            pl.BlockSpec((2, total), lambda h: (0, 0)),
            pl.BlockSpec((2, HEAD_DIM), lambda h: (0, h)),
        ]
        + [pl.BlockSpec((size, 3 * HEAD_DIM), lambda h: (0, h)) for _, _, size in plan],
        out_specs=pl.BlockSpec((blocks, chunk, HEAD_DIM), lambda h: (0, 0, h)),
        out_shape=jax.ShapeDtypeStruct((blocks, chunk, heads * HEAD_DIM), BF16),
        scratch_shapes=[
            pltpu.VMEM((blocks * chunk, HEAD_DIM), F32),
            pltpu.VMEM((total, HEAD_DIM), F32),
            pltpu.VMEM((blocks * chunk, HEAD_DIM), BF16),
            pltpu.VMEM((total, HEAD_DIM), BF16),
            pltpu.VMEM((total, 2 * HEAD_DIM), BF16),
        ],
        cost_estimate=pl.CostEstimate(
            flops=8 * heads * blocks * chunk * total * HEAD_DIM,
            bytes_accessed=4 * total * width,
            transcendentals=heads * blocks * chunk * total,
        ),
        compiler_params=pltpu.CompilerParams(vmem_limit_bytes=56 * MIB),
        name="attend",
    )(segments, squares, qk_gain, *pieces)


def per_device(
    residual_in,
    norm_gain,
    qkv_weight,
    qk_gain,
    out_weight,
    layer_scale,
    segment_ids,
    pad_mask,
    ln_weight,
    ln_bias,
    fc_weight,
    fc_bias,
    owner,
):
    x = residual_in[0]
    rows_here = x.shape[0]
    n_seq, n_rows = lax.axis_size("seq"), lax.axis_size("rows")
    row = lax.axis_index("rows")
    parts = n_rows // SUBS
    sub, part = row // parts, row % parts
    width = D // parts
    chunk = rows_here // CHUNKS
    merged = chunk // SUBS
    hid = fc_weight.shape[1]

    def over_seq(value, d):
        return lax.ppermute(value, "seq", [(i, i ^ d) for i in range(n_seq)])

    def over_sub(value, d):
        return lax.ppermute(value, "rows", [(i, i ^ (d * parts)) for i in range(n_rows)])

    def over_part(value, d):
        return lax.ppermute(value, "rows", [(i, i ^ d) for i in range(n_rows)])

    def spread(value, axis):
        count = 1
        while count < lax.axis_size(axis):
            steps = [(i, i ^ count) for i in range(lax.axis_size(axis))]
            value = jnp.concatenate([value, lax.ppermute(value, axis, steps)])
            count *= 2
        return value

    def pick(value, index, axis=0):
        return lax.dynamic_index_in_dim(value, index, axis, keepdims=False)

    fence = lax.optimization_barrier

    tokens = reorder(x, chunk)
    cuts = [0, rows_here * 3 // 4, rows_here]
    cut = [tokens[low:high] for low, high in zip(cuts, cuts[1:])]
    by_sub = tokens.reshape(CHUNKS, SUBS, merged, D)
    residual = {0: pick(by_sub, sub, 1)}
    to_send = {d: pick(by_sub, sub ^ d, 1) for d in range(1, SUBS)}
    share = out_weight.shape[0] // n_rows
    strip = lax.dynamic_slice_in_dim(out_weight, row * share, share, 0)
    group = max(1, min(n_seq, TILE // rows_here))
    projected, squares = {}, {}

    far = {d: over_seq(cut[0], d) for d in range(2, n_seq, 2)}
    near = over_seq(tokens, 1)
    strips = {d: over_seq(strip, d) for d in range(2, n_seq, 2)}
    for d in (1, 2):
        residual[d] = over_sub(to_send[d], d)
    given, given_s = project([tokens, near], norm_gain, qkv_weight)
    for d in range(2):
        projected[d, 0], squares[d, 0] = given[d], given_s[d]
    state = far, cut[1], strips, residual, to_send, squares, segment_ids, pad_mask, out_weight
    far, later, strips, residual, to_send, squares, segment_ids, pad_mask, out_weight = fence(state)

    coming = {d: over_seq(later, d) for d in range(2, n_seq, 2)}
    out_blocks = {0: out_weight, 1: over_seq(out_weight, 1)}
    for d in range(2, n_seq, 2):
        out_blocks[d] = lax.all_gather(strips[d], "rows", axis=0, tiled=True)
        far[d + 1] = over_seq(far[d], 1)
    for d in range(3, SUBS):
        residual[d] = over_sub(to_send[d], d)
    leads = spread(segment_ids[0, :1], "seq")[::group]
    masks = spread(pad_mask[0, :1], "rows")
    given, given_s = project([far[d] for d in range(2, n_seq)], norm_gain, qkv_weight)
    for d in range(2, n_seq):
        projected[d, 0], squares[d, 0] = given[d - 2], given_s[d - 2]
    far, residual, squares, leads, masks = fence((coming, residual, squares, leads, masks))

    for d in range(2, n_seq, 2):
        far[d + 1] = over_seq(far[d], 1)
    given, given_s = project([far[d] for d in range(2, n_seq)], norm_gain, qkv_weight)
    for d in range(2, n_seq):
        projected[d, 1], squares[d, 1] = given[d - 2], given_s[d - 2]
    plan, pieces = [], []
    for d, i in sorted(projected):
        plan.append((d, cuts[i], projected[d, i].shape[0]))
        pieces.append(projected[d, i])

    here = jnp.concatenate([squares[key] for key in sorted(squares)], axis=1)
    here = jnp.transpose(here.reshape(2, n_seq, rows_here), (1, 0, 2))
    total = here
    for e in range(1, n_seq):
        there = over_seq(here, e)
        total = total + jnp.stack([there[d ^ e] for d in range(n_seq)])
    total = jnp.transpose(total, (1, 0, 2)).reshape(2, n_seq * rows_here)

    for d in range(2, n_seq, 2):
        out_blocks[d + 1] = over_seq(out_blocks[d], 1)
    out_full = jnp.concatenate([out_blocks[d] for d in range(n_seq)], axis=0)

    sub_ln = lax.dynamic_slice_in_dim(ln_weight, sub * D, D, 0)
    sub_bias = lax.dynamic_slice_in_dim(ln_bias, sub * D, D, 0)
    source = jnp.argmax(owner[None, :] == jnp.arange(n_rows, dtype=jnp.int32)[:, None], axis=1)
    own_mask = pick(masks, pick(source, row) ^ row).astype(F32)
    wanted = []
    for f in range(parts):
        for g in range(SUBS):
            p = pick(source, (sub ^ g) * parts + (part ^ f))
            wanted.append((p % parts ^ part) * SUBS + (p // parts ^ sub))
    wanted_hot = (
        jnp.stack(wanted)[:, None] == jnp.arange(n_rows, dtype=jnp.int32)[None, :]
    ).astype(BF16)

    def heads_of(j, sums):
        return attend(pieces, plan, rows_here, sums, leads, qk_gain, j * chunk, chunk)

    def gather_rows(heads):
        groups = [heads[0]] + [over_seq(heads[d], d) for d in range(1, n_seq)]
        heads = jnp.concatenate(groups, axis=-1).reshape(SUBS, merged, HEADS * HEAD_DIM)
        mine = [pick(heads, sub)]
        for d in range(1, SUBS):
            mine.append(over_sub(pick(heads, sub ^ d), d))
        return jnp.concatenate(mine, axis=0)

    def to_slab(j, mine):
        attn = jnp.dot(mine, out_full, preferred_element_type=F32)
        stream = jnp.concatenate([residual[d][j] for d in range(SUBS)], axis=0).astype(F32)
        hidden = stream + layer_scale * attn
        mean_here = jnp.mean(hidden, axis=-1)
        centre = hidden - mean_here[:, None]
        spread_here = jnp.sum(centre * centre, axis=-1)
        stats = jnp.stack([mean_here, spread_here]).reshape(2, SUBS, merged)
        known = [stats]
        for e in range(1, SUBS):
            there = over_sub(stats, e)
            known.append(jnp.stack([there[:, d ^ e] for d in range(SUBS)], axis=1))
        mean = sum(k[0] for k in known) / SUBS
        var = sum(k[1] + D * (k[0] - mean) * (k[0] - mean) for k in known) / (SUBS * D)
        mean, var = mean.reshape(-1, 1), var.reshape(-1, 1)
        normed = (
            (hidden - mean) * lax.rsqrt(var + 1e-05) * sub_ln + sub_bias
        ).astype(BF16)
        by_part = jnp.stack([normed[:, i * width : (i + 1) * width] for i in range(parts)])
        slab = [pick(by_part, part)]
        for e in range(1, parts):
            slab.append(over_part(pick(by_part, part ^ e), e))
        return jnp.concatenate(slab, axis=0)

    def to_shares(slab):
        half = merged // HALVES
        ordered = jnp.einsum(
            "jp,phms->hjms",
            wanted_hot,
            slab.reshape(n_rows, HALVES, half, width),
            preferred_element_type=F32,
        ).astype(BF16)
        shares = jnp.dot(
            ordered.reshape(n_rows * merged, width), fc_weight, preferred_element_type=F32
        ).astype(BF16)
        return shares.reshape(HALVES, parts, SUBS, half, hid)

    def sum_parts(shares):
        summed = shares[0].astype(F32)
        for e in range(1, parts):
            summed = summed + over_part(shares[e], e).astype(F32)
        return summed.astype(BF16)

    def sum_subs(summed):
        pre = summed[0].astype(F32)
        for d in range(1, SUBS):
            pre = pre + over_sub(summed[d], d).astype(F32)
        return pre

    def finish(pre):
        return (jax.nn.gelu(pre + fc_bias, approximate=False) * own_mask).astype(BF16)

    heads, rows, slab, shares, summed, pre, outs = {}, {}, {}, {}, {}, {}, {}
    state = total, heads, rows, slab, shares, summed, pre, outs
    units = [(j, h) for j in range(CHUNKS) for h in range(HALVES)]
    for tick in range(3 + CHUNKS + len(units) + 1):
        total, heads, rows, slab, shares, summed, pre, outs = state
        new = total, {}, {}, {}, dict(shares), {}, {}, dict(outs)
        if tick < CHUNKS:
            new[1][tick] = heads_of(tick, total)
        for j in heads:
            new[2][j] = gather_rows(heads[j])
        for j in rows:
            new[3][j] = to_slab(j, rows[j])
        for j in slab:
            given = to_shares(slab[j])
            new[4].update({(j, h): given[h] for h in range(HALVES)})
        if shares:
            unit = min(shares)
            new[5][unit] = sum_parts(new[4].pop(unit))
        for unit in summed:
            new[6][unit] = sum_subs(summed[unit])
        for unit in pre:
            new[7][unit] = finish(pre[unit])
        state = fence(new)
    outs = state[-1]
    return jnp.concatenate([outs[unit] for unit in units], axis=0)[None]


def solution(mesh):
    return jax.shard_map(
        per_device,
        mesh=mesh,
        in_specs=(
            P("rows", "seq", None),
            P(),
            P(None, "seq"),
            P(None, "seq"),
            P("seq", None),
            P(),
            P("rows", "seq"),
            P("rows", "seq"),
            P(),
            P(),
            P("rows", None),
            P(),
            P(),
        ),
        out_specs=P("rows", "seq", None),
        check_vma=False,
    )
```

time: 776 us -> 584 us (0.75)
  waiting for transfers between devices: 384 us -> 235 us
  matrix products: 151 us -> 54.1 us
  blocking collectives: 96.4 us -> 0 us
  starting transfers between devices: 3.4 us -> 72 us
  Pallas kernels: 0 us -> 68.1 us
  between operations: 13.7 us -> 36 us
  other arithmetic: 52.2 us -> 35.2 us
    reduce_scatter x2 -> x0, waiting for transfers between devices: 296 us -> none  [the longest x1 193 us: per_device(): lax.psum_scatter(jnp.dot(piece, fc_weight, preferred_element_type=jnp.flo...]
    ppermute x0 -> x55, waiting for transfers between devices: none -> 235 us  [the longest x27 108 us: over_sub(): lax.ppermute(value, 'rows', [(i, i ^ d * parts) for i in range(n_rows)])]
    all_gather x1, waiting for transfers between devices: 81.1 us -> 0.01 us  [per_device(): out_blocks[d] = lax.all_gather(strips[d], 'rows', axis=0, tiled=True)]
    all_to_all x1 -> x0, blocking collectives: 79.8 us -> none  [per_device(): lax.all_to_all(merged_norm, 'rows', split_axis=1, concat_axis=0, tiled=True)]
    ppermute x0 -> x55, starting transfers between devices: none -> 72 us  [the longest x27 46.4 us: over_sub(): lax.ppermute(value, 'rows', [(i, i ^ d * parts) for i in range(n_rows)])]
    pallas_call x0 -> x6, Pallas kernels: none -> 68.1 us  [the longest x3 44.7 us: project(): pl.pallas_call(functools.partial(qkv_kernel, count), grid=(width // block...]
    dot_general x9 -> x6, matrix products: 106 us -> 54.1 us  [the longest x2 33.6 us: to_shares(): jnp.dot(ordered.reshape(n_rows * merged, width), fc_weight, preferred_ele...]
    sub x4 -> x0, matrix products: 44.8 us -> none  [one_block(): exp_terms = jnp.exp(scores - peak_val)]
  transfers between devices with their start and end apart: 4 -> 56, of which waited for: 4 -> 23; matrix products, arithmetic and copies ran while one was open for 0% -> 17% of each run, Pallas kernels for 0% -> 12%
where the time goes in v1:
time: 584 us; the launch traced here: 574 us
  waiting for transfers between devices  235 us (40%)
  local copies, waits for them, and re-layouts  73.8 us (13%)
  starting transfers between devices  72 us (12%)
  Pallas kernels  68.1 us (12%)
  matrix products  54.1 us (9%)
  between operations  36 us (6%)
  other arithmetic  35.2 us (6%)
    ppermute x27, waiting for transfers between devices, over_sub(): lax.ppermute(value, 'rows', [(i, i ^ d * parts) for i in range(n_rows)])  108 us
    ppermute x6, waiting for transfers between devices, over_part(): return lax.ppermute(value, 'rows', [(i, i ^ d) for i in range(n_rows)])  47 us
    ppermute x27, starting transfers between devices, over_sub(): lax.ppermute(value, 'rows', [(i, i ^ d * parts) for i in range(n_rows)])  46.4 us
    pallas_call x3, Pallas kernels, project(): pl.pallas_call(functools.partial(qkv_kernel, count), grid=(width // block...  44.7 us
    ppermute x17, waiting for transfers between devices, over_seq(): return lax.ppermute(value, 'seq', [(i, i ^ d) for i in range(n_seq)])  43.4 us
    ppermute x5, waiting for transfers between devices, spread(): value = jnp.concatenate([value, lax.ppermute(value, axis, steps)])  36.4 us
    dot_general x2, matrix products, to_shares(): jnp.dot(ordered.reshape(n_rows * merged, width), fc_weight, preferred_ele...  33.6 us
    pallas_call x2, Pallas kernels, attend(): pl.pallas_call(functools.partial(attend_kernel, plan, rows, first, chunk,...  22.1 us
  transfers between devices with their start and end apart: 56, of which 23 were waited for; matrix products, arithmetic and copies ran while one was open for 17% of the time, Pallas kernels for 12%

profile of v1, /device:TPU:0, one launch (start us, length us, event | category | flops | bytes accessed | tf_op | source)
XLA Modules:
  0.0 574.4 jit_solution(15723641387933589777)
XLA Ops:
  6.5 1.9 copy-done.1
  11.2 2.1 slice.420
  13.2 2.3 collective-permute-start
  15.5 1.8 constant_dynamic-slice_fusion
  19.0 2.1 collective-permute-start.2
  21.1 2.6 collective-permute-start.3
  25.3 20.6 %qkv.3 = (f32[512,1536]{1,0:T(8,128)}, f32[512,1536]{1,0:T(8,128)}, f32[2,512]{1,0:T(2,128)}, f32[2,512]{1,0:T(2,128)}) custom-call(bf16[512,3200]{1,0:T(8,128)(2,1)} %copy-done, bf16[512,3200]{1,0:T(8,128)(2,1)} %collective-permute-done.4.refs_1_, f32[1,3200]{1,0:T(1,128)} %reshape.298.refs_2_, bf16[3200,1536]{1,0:T(8,128)(2,1)} %refs_3_.5), custom_call_target="tpu_custom_call" | custom-call | flops 10066329600 | bytes 22675456 | tf_op jit(solution)/shard_map/qkv/pallas_call | solution.py:95
  45.9 32.8 %collective-permute-done.1 = bf16[64,3200]{1,0:T(8,128)(2,1)} collective-permute-done((bf16[64,3200]{1,0:T(8,128)(2,1)}, bf16[64,3200]{1,0:T(8,128)(2,1)}, u32[]{:S(2)}, u32[]{:S(2)}) %collective-permute-start.1) | collective-permute-done | bytes 409632 | tf_op jit(solution)/shard_map/ppermute | solution.py:261
  81.0 1.7 collective-permute-start.5
  82.7 3.6 collective-permute-start.6
  89.3 1.9 constant_dynamic-update-slice_fusion.9
  92.7 2.2 collective-permute-done.10
  94.9 2.7 pad_add_fusion
  98.1 3.8 collective-permute-done.9
  101.9 1.8 collective-permute-start.11
  105.7 4.8 collective-permute-done.11
  113.1 25.7 %collective-permute-done.12 = s32[4]{0:T(128)S(1)} collective-permute-done((s32[4]{0:T(128)S(1)}, s32[4]{0:T(128)S(1)}, u32[]{:S(2)}, u32[]{:S(2)}) %collective-permute-start.12) | collective-permute-done | bytes 48 | tf_op jit(solution)/shard_map/ppermute | solution.py:273
  138.8 1.9 pad_add_fusion.4
  140.7 16.2 %qkv.4 = (f32[384,1536]{1,0:T(8,128)}, f32[384,1536]{1,0:T(8,128)}, f32[2,384]{1,0:T(2,128)}, f32[2,384]{1,0:T(2,128)}) custom-call(bf16[384,3200]{1,0:T(8,128)(2,1)} %collective-permute-done.refs_0_, bf16[384,3200]{1,0:T(8,128)(2,1)} %collective-permute-done.7.refs_1_, f32[1,3200]{1,0:T(1,128)} %reshape.298.refs_2_, bf16[3200,1536]{1,0:T(8,128)(2,1)} %refs_3_.5), custom_call_target="tpu_custom_call" | custom-call | flops 7549747200 | bytes 19464192 | tf_op jit(solution)/shard_map/qkv/pallas_call | solution.py:95
  157.8 2.1 slice_bitcast_fusion.12
  159.8 2.1 slice_bitcast_fusion.13
  161.9 2.1 slice_bitcast_fusion.14
  164.9 7.9 %qkv.5 = (f32[128,1536]{1,0:T(8,128)}, f32[128,1536]{1,0:T(8,128)}, f32[2,128]{1,0:T(2,128)}, f32[2,128]{1,0:T(2,128)}) custom-call(bf16[128,3200]{1,0:T(8,128)(2,1)} %collective-permute-done.5.refs_0_, bf16[128,3200]{1,0:T(8,128)(2,1)} %copy-done.11, f32[1,3200]{1,0:T(1,128)} %reshape.298.refs_2_, bf16[3200,1536]{1,0:T(8,128)(2,1)} %refs_3_.5), custom_call_target="tpu_custom_call" | custom-call | flops 2516582400 | bytes 13041664 | tf_op jit(solution)/shard_map/qkv/pallas_call | solution.py:95
  174.8 2.1 slice_bitcast_fusion.15
  178.3 2.3 collective-permute-done.15
  181.4 11.0 %attend.2 = bf16[4,256,512]{2,1,0:T(8,128)(2,1)} custom-call(s32[2]{0:T(128)} %slice.328.refs_0_, f32[2,2048]{1,0:T(2,128)} %bitcast.209, f32[2,512]{1,0:T(2,128)} %refs_2_.3, f32[512,1536]{1,0:T(8,128)} %get-tuple-element.100.refs_3_, f32[512,1536]{1,0:T(8,128)} %get-tuple-element.101.refs_4_, f32[384,1536]{1,0:T(8,128)} %get-tuple-element.102.refs_5_, ...), custom_call_target="tpu_custom_call" | custom-call | flops 8589934592 | bytes 12582912 | tf_op jit(solution)/shard_map/attend/pallas_call | solution.py:206
  195.8 3.8 constant_dynamic-update-slice_fusion.8
  199.6 2.3 collective-permute-done.19
  201.9 6.0 %collective-permute-done.18 = bf16[256,512]{1,0:T(8,128)(2,1)S(1)} collective-permute-done((bf16[256,512]{1,0:T(8,128)(2,1)S(1)}, bf16[256,512]{1,0:T(8,128)(2,1)S(1)}, u32[]{:S(2)}, u32[]{:S(2)}) %collective-permute-start.18) | collective-permute-done | bytes 262176 | tf_op jit(solution)/shard_map/ppermute | solution.py:261
  208.1 6.9 %collective-permute-start.22 = (bf16[64,2048]{1,0:T(8,128)(2,1)S(1)}, bf16[64,2048]{1,0:T(8,128)(2,1)S(1)}, u32[]{:S(2)}, u32[]{:S(2)}) collective-permute-start(bf16[64,2048]{1,0:T(8,128)(2,1)S(1)} %get-tuple-element.180), channel_id=1, source_target_pairs={{0,24},{4,28},{8,16},{12,20},{16,8},{20,12},{24,0},{28,4},{1,25},{... | collective-permute-start | bytes 786440 | tf_op jit(solution)/shard_map/ppermute | solution.py:264
  215.7 11.1 %attend.3 = bf16[4,256,512]{2,1,0:T(8,128)(2,1)} custom-call(s32[2]{0:T(128)} %slice.328.refs_0_, f32[2,2048]{1,0:T(2,128)} %bitcast.210, f32[2,512]{1,0:T(2,128)} %refs_2_.3, f32[512,1536]{1,0:T(8,128)} %get-tuple-element.100.refs_3_, f32[512,1536]{1,0:T(8,128)} %get-tuple-element.101.refs_4_, f32[384,1536]{1,0:T(8,128)} %get-tuple-element.102.refs_5_, ...), custom_call_target="tpu_custom_call" | custom-call | flops 8589934592 | bytes 12582912 | tf_op jit(solution)/shard_map/attend/pallas_call | solution.py:206
  226.8 8.2 %collective-permute-done.21 = bf16[64,2048]{1,0:T(8,128)(2,1)S(1)} collective-permute-done((bf16[64,2048]{1,0:T(8,128)(2,1)S(1)}, bf16[64,2048]{1,0:T(8,128)(2,1)S(1)}, u32[]{:S(2)}, u32[]{:S(2)}) %collective-permute-start.21) | collective-permute-done | bytes 262176 | tf_op jit(solution)/shard_map/ppermute | solution.py:264
  235.2 2.0 constant_dynamic-update-slice_fusion.7
  237.3 4.0 constant_dynamic-update-slice_fusion.6
  241.3 7.8 %fusion.110 = (f32[256]{0:T(256)S(1)}, f32[256,3200]{1,0:T(8,128)S(1)}) fusion(bf16[256,2048]{1,0:T(8,128)(2,1)S(1)} %pad_maximum_fusion.3, bf16[2048,3200]{1,0:T(8,128)(2,1)} %constant_dynamic-update-slice_fusion.6, f32[3200]{0:T(1024)S(1)} %copy-done.25, bf16[64,3200]{1,0:T(8,128)(2,1)S(1)} %copy-done.12, bf16[64,3200]{1,0:T(8,128)(2,1)S(1)} %copy-done.13, ...), kind=kOutput, calls=%fused_computation.271 | convolution fusion | flops 3364454144 | bytes 19084800 | tf_op jit(solution)/shard_map/dot_general | solution.py:365
  252.8 2.1 fusion.94
  257.2 2.8 collective-permute-start.31
  275.3 6.3 %collective-permute-start.34 = (bf16[256,1600]{0,1:T(8,128)(2,1)S(1)}, bf16[256,1600]{0,1:T(8,128)(2,1)}, u32[]{:S(2)}, u32[]{:S(2)}) collective-permute-start(bf16[256,1600]{0,1:T(8,128)(2,1)S(1)} %bitcast.202), channel_id=1, source_target_pairs={{0,4},{4,0},{8,12},{12,8},{16,20},{20,16},{24,28},{28,24},{1,5},{5... | collective-permute-start | bytes 2457608 | tf_op jit(solution)/shard_map/ppermute | solution.py:267
  283.7 3.7 collective-permute-start.26
  309.7 2.0 pad_maximum_fusion.5
  314.9 8.9 %fusion.111 = (f32[256]{0:T(256)S(1)}, f32[256,3200]{1,0:T(8,128)S(1)}) fusion(bf16[256,2048]{1,0:T(8,128)(2,1)S(1)} %copy-done.10, bf16[2048,3200]{1,0:T(8,128)(2,1)} %constant_dynamic-update-slice_fusion.6, f32[3200]{0:T(1024)S(1)} %copy-done.26, bf16[64,3200]{1,0:T(8,128)(2,1)} %get-tuple-element.193, bf16[64,3200]{1,0:T(8,128)(2,1)} %get-tuple-element.191, ...), kind=kOutput, calls=%fused_computation.272 | convolution fusion | flops 3364454144 | bytes 19084800 | tf_op jit(solution)/shard_map/dot_general | solution.py:365
  325.9 2.9 collective-permute-start.35
  328.8 2.6 fusion.6
  331.6 17.6 %convolution_convert_fusion.1 = bf16[512,6144]{1,0:T(8,128)(2,1)} fusion(bf16[512,1600]{1,0:T(8,128)(2,1)S(1)} %bitcast.198, bf16[1600,6144]{1,0:T(8,128)(2,1)} %param.24), kind=kOutput, calls=%fused_computation.1 | convolution fusion | flops 10069475328 | bytes 27590656 | tf_op jit(solution)/shard_map/dot_general | solution.py:396
  353.8 5.2 fusion.93
  359.0 12.3 %collective-permute-done.38 = bf16[256,1600]{0,1:T(8,128)(2,1)} collective-permute-done((bf16[256,1600]{0,1:T(8,128)(2,1)}, bf16[256,1600]{0,1:T(8,128)(2,1)}, u32[]{:S(2)}, u32[]{:S(2)}) %collective-permute-start.38) | collective-permute-done | bytes 819232 | tf_op jit(solution)/shard_map/ppermute | solution.py:267
  371.4 2.2 copy.36
  376.4 16.0 %convolution_convert_fusion = bf16[512,6144]{1,0:T(8,128)(2,1)S(1)} fusion(bf16[512,1600]{1,0:T(8,128)(2,1)S(1)} %bitcast.199, bf16[1600,6144]{1,0:T(8,128)(2,1)} %param.24), kind=kOutput, calls=%fused_computation | convolution fusion | flops 10069475328 | bytes 27590656 | tf_op jit(solution)/shard_map/dot_general | solution.py:396
  392.9 2.1 fusion.92
  395.0 30.1 %collective-permute-done.39 = bf16[4,32,6144]{2,1,0:T(8,128)(2,1)S(1)} collective-permute-done((bf16[4,32,6144]{2,1,0:T(8,128)(2,1)S(1)}, bf16[4,32,6144]{2,1,0:T(8,128)(2,1)S(1)}, u32[]{:S(2)}, u32[]{:S(2)}) %collective-permute-start.39) | collective-permute-done | bytes 1572896 | tf_op jit(solution)/shard_map/ppermute | solution.py:267
  428.7 2.4 collective-permute-start.41
  434.8 5.9 %collective-permute-done.43 = bf16[32,6144]{1,0:T(8,128)(2,1)S(1)} collective-permute-done((bf16[32,6144]{1,0:T(8,128)(2,1)}, bf16[32,6144]{1,0:T(8,128)(2,1)S(1)}, u32[]{:S(2)}, u32[]{:S(2)}) %collective-permute-start.43) | collective-permute-done | bytes 393248 | tf_op jit(solution)/shard_map/ppermute | solution.py:264
  440.7 18.0 %collective-permute-done.42 = bf16[32,6144]{1,0:T(8,128)(2,1)} collective-permute-done((bf16[32,6144]{1,0:T(8,128)(2,1)}, bf16[32,6144]{1,0:T(8,128)(2,1)}, u32[]{:S(2)}, u32[]{:S(2)}) %collective-permute-start.42) | collective-permute-done | bytes 393248 | tf_op jit(solution)/shard_map/ppermute | solution.py:264
  460.2 3.1 collective-permute-done.40
  463.3 2.2 fusion.4
  469.2 1.9 collective-permute-start.45
  472.9 7.7 %collective-permute-done.47 = bf16[32,6144]{1,0:T(8,128)(2,1)S(1)} collective-permute-done((bf16[32,6144]{1,0:T(8,128)(2,1)S(1)}, bf16[32,6144]{1,0:T(8,128)(2,1)S(1)}, u32[]{:S(2)}, u32[]{:S(2)}) %collective-permute-start.47) | collective-permute-done | bytes 393248 | tf_op jit(solution)/shard_map/ppermute | solution.py:264
  480.6 15.9 %collective-permute-done.46 = bf16[32,6144]{1,0:T(8,128)(2,1)S(1)} collective-permute-done((bf16[32,6144]{1,0:T(8,128)(2,1)S(1)}, bf16[32,6144]{1,0:T(8,128)(2,1)S(1)}, u32[]{:S(2)}, u32[]{:S(2)}) %collective-permute-start.46) | collective-permute-done | bytes 393248 | tf_op jit(solution)/shard_map/ppermute | solution.py:264
  501.5 2.9 collective-permute-start.49
  506.1 7.7 %collective-permute-done.51 = bf16[32,6144]{1,0:T(8,128)(2,1)S(1)} collective-permute-done((bf16[32,6144]{1,0:T(8,128)(2,1)S(1)}, bf16[32,6144]{1,0:T(8,128)(2,1)S(1)}, u32[]{:S(2)}, u32[]{:S(2)}) %collective-permute-start.51) | collective-permute-done | bytes 393248 | tf_op jit(solution)/shard_map/ppermute | solution.py:264
  513.8 17.5 %collective-permute-done.50 = bf16[32,6144]{1,0:T(8,128)(2,1)S(1)} collective-permute-done((bf16[32,6144]{1,0:T(8,128)(2,1)S(1)}, bf16[32,6144]{1,0:T(8,128)(2,1)S(1)}, u32[]{:S(2)}, u32[]{:S(2)}) %collective-permute-start.50) | collective-permute-done | bytes 393248 | tf_op jit(solution)/shard_map/ppermute | solution.py:264
  533.4 3.1 collective-permute-start.52
  538.2 7.7 %collective-permute-done.54 = bf16[32,6144]{1,0:T(8,128)(2,1)S(1)} collective-permute-done((bf16[32,6144]{1,0:T(8,128)(2,1)S(1)}, bf16[32,6144]{1,0:T(8,128)(2,1)S(1)}, u32[]{:S(2)}, u32[]{:S(2)}) %collective-permute-start.54) | collective-permute-done | bytes 393248 | tf_op jit(solution)/shard_map/ppermute | solution.py:264
  545.9 18.0 %collective-permute-done.53 = bf16[32,6144]{1,0:T(8,128)(2,1)S(1)} collective-permute-done((bf16[32,6144]{1,0:T(8,128)(2,1)S(1)}, bf16[32,6144]{1,0:T(8,128)(2,1)S(1)}, u32[]{:S(2)}, u32[]{:S(2)}) %collective-permute-start.53) | collective-permute-done | bytes 393248 | tf_op jit(solution)/shard_map/ppermute | solution.py:264
  (240 shorter events, 93.0 us)
Async XLA Ops:
  6.5 174.8 %all-gather.2.cloned.1.call-start = ((), (), s32[]{:S(2)}) async-start(), calls=%async_computation | async-start | bytes 3686400 | tf_op jit(solution)/shard_map/all_gather | solution.py:307
  10.6 14.7 %collective-permute-start.4 = (bf16[512,3200]{1,0:T(8,128)(2,1)S(1)}, bf16[512,3200]{1,0:T(8,128)(2,1)}, u32[]{:S(2)}, u32[]{:S(2)}) collective-permute-start(bf16[512,3200]{1,0:T(8,128)(2,1)S(1)} %reorder.1.refs_0_), channel_id=1, source_target_pairs={{0,1},{1,0},{2,3},{3,2},{4,5},{5,4},{6,7},{7,6},{8,9},{9,8},{10,11... | collective-permute-start | bytes 9830408 | tf_op jit(solution)/shard_map/ppermute | solution.py:261
  13.2 65.4 %collective-permute-start = (bf16[384,3200]{1,0:T(8,128)(2,1)}, bf16[384,3200]{1,0:T(8,128)(2,1)}, u32[]{:S(2)}, u32[]{:S(2)}) collective-permute-start(bf16[384,3200]{1,0:T(8,128)(2,1)} %slice.420), channel_id=1, source_target_pairs={{0,2},{1,3},{2,0},{3,1},{4,6},{5,7},{6,4},{7,5},{8,10},{9,11},{10,... | collective-permute-start | bytes 7372808 | tf_op jit(solution)/shard_map/ppermute | solution.py:261
  17.3 61.3 %collective-permute-start.1 = (bf16[64,3200]{1,0:T(8,128)(2,1)}, bf16[64,3200]{1,0:T(8,128)(2,1)}, u32[]{:S(2)}, u32[]{:S(2)}) collective-permute-start(bf16[64,3200]{1,0:T(8,128)(2,1)} %constant_dynamic-slice_fusion), channel_id=1, source_target_pairs={{0,2},{1,3},{2,0},{3,1},{4,6},{5,7},{6,4},{7,5},{8,10},{9,11},{10,... | collective-permute-start | bytes 1228808 | tf_op jit(solution)/shard_map/ppermute | solution.py:261
  19.0 59.6 %collective-permute-start.2 = (bf16[2,64,3200]{2,1,0:T(8,128)(2,1)}, bf16[2,64,3200]{2,1,0:T(8,128)(2,1)}, u32[]{:S(2)}, u32[]{:S(2)}) collective-permute-start(bf16[2,64,3200]{2,1,0:T(8,128)(2,1)} %get-tuple-element.149), channel_id=1, source_target_pairs={{0,8},{4,12},{8,0},{12,4},{16,24},{20,28},{24,16},{28,20},{1,9},{5... | collective-permute-start | bytes 2457608 | tf_op jit(solution)/shard_map/ppermute | solution.py:264
  21.1 57.5 %collective-permute-start.3 = (bf16[2,64,3200]{2,1,0:T(8,128)(2,1)}, bf16[2,64,3200]{2,1,0:T(8,128)(2,1)}, u32[]{:S(2)}, u32[]{:S(2)}) collective-permute-start(bf16[2,64,3200]{2,1,0:T(8,128)(2,1)} %get-tuple-element.148), channel_id=1, source_target_pairs={{0,16},{4,20},{8,24},{12,28},{16,0},{20,4},{24,8},{28,12},{1,17},{... | collective-permute-start | bytes 2457608 | tf_op jit(solution)/shard_map/ppermute | solution.py:264
  25.3 63.4 %copy-start.8 = (bf16[512,3200]{1,0:T(8,128)(2,1)S(1)}, bf16[512,3200]{1,0:T(8,128)(2,1)}, u32[]{:S(2)}) copy-start(bf16[512,3200]{1,0:T(8,128)(2,1)} %param.18) | copy-start | bytes 9830404
  78.6 62.0 %collective-permute-start.7 = (bf16[384,3200]{1,0:T(8,128)(2,1)}, bf16[384,3200]{1,0:T(8,128)(2,1)}, u32[]{:S(2)}, u32[]{:S(2)}) collective-permute-start(bf16[384,3200]{1,0:T(8,128)(2,1)} %collective-permute-done.refs_0_), channel_id=1, source_target_pairs={{0,1},{1,0},{2,3},{3,2},{4,5},{5,4},{6,7},{7,6},{8,9},{9,8},{10,11... | collective-permute-start | bytes 7372808 | tf_op jit(solution)/shard_map/ppermute | solution.py:261
  81.0 76.0 %collective-permute-start.5 = (bf16[128,3200]{1,0:T(8,128)(2,1)}, bf16[128,3200]{1,0:T(8,128)(2,1)}, u32[]{:S(2)}, u32[]{:S(2)}) collective-permute-start(bf16[128,3200]{1,0:T(8,128)(2,1)} %slice.421), channel_id=1, source_target_pairs={{0,2},{1,3},{2,0},{3,1},{4,6},{5,7},{6,4},{7,5},{8,10},{9,11},{10,... | collective-permute-start | bytes 2457608 | tf_op jit(solution)/shard_map/ppermute | solution.py:261
  82.7 74.2 %collective-permute-start.6 = (bf16[2,64,3200]{2,1,0:T(8,128)(2,1)}, bf16[2,64,3200]{2,1,0:T(8,128)(2,1)}, u32[]{:S(2)}, u32[]{:S(2)}) collective-permute-start(bf16[2,64,3200]{2,1,0:T(8,128)(2,1)} %get-tuple-element.80), channel_id=1, source_target_pairs={{0,24},{4,28},{8,16},{12,20},{16,8},{20,12},{24,0},{28,4},{1,25},{... | collective-permute-start | bytes 2457608 | tf_op jit(solution)/shard_map/ppermute | solution.py:264
  87.5 3.7 collective-permute-start.8
  88.7 107.0 %collective-permute-start.29 = (bf16[512,3200]{1,0:T(8,128)(2,1)S(1)}, bf16[512,3200]{1,0:T(8,128)(2,1)}, u32[]{:S(2)}, u32[]{:S(2)}) collective-permute-start(bf16[512,3200]{1,0:T(8,128)(2,1)S(1)} %copy-done.8), channel_id=1, source_target_pairs={{0,1},{1,0},{2,3},{3,2},{4,5},{5,4},{6,7},{7,6},{8,9},{9,8},{10,11... | collective-permute-start | bytes 9830408 | tf_op jit(solution)/shard_map/ppermute | solution.py:261
  91.2 3.7 collective-permute-start.10
  97.6 4.3 collective-permute-start.9
  101.9 8.6 %collective-permute-start.11 = (s32[2]{0:T(128)S(1)}, s32[2]{0:T(128)S(1)}, u32[]{:S(2)}, u32[]{:S(2)}) collective-permute-start(s32[2]{0:T(128)S(1)} %get-tuple-element.255), channel_id=1, source_target_pairs={{0,8},{4,12},{8,0},{12,4},{16,24},{20,28},{24,16},{28,20},{1,9},{5... | collective-permute-start | bytes 32 | tf_op jit(solution)/shard_map/ppermute | solution.py:273
  111.9 26.9 %collective-permute-start.12 = (s32[4]{0:T(128)S(1)}, s32[4]{0:T(128)S(1)}, u32[]{:S(2)}, u32[]{:S(2)}) collective-permute-start(s32[4]{0:T(128)S(1)} %pad_add_fusion.3), channel_id=1, source_target_pairs={{0,16},{4,20},{8,24},{12,28},{16,0},{20,4},{24,8},{28,12},{1,17},{... | collective-permute-start | bytes 56 | tf_op jit(solution)/shard_map/ppermute | solution.py:273
  140.7 16.4 %copy-start.21 = (f32[2,512]{1,0:T(2,128)S(1)}, f32[2,512]{1,0:T(2,128)}, u32[]{:S(2)}) copy-start(f32[2,512]{1,0:T(2,128)} %get-tuple-element.93) | copy-start | bytes 12292
  156.9 7.1 %collective-permute-start.13 = (bf16[128,3200]{1,0:T(8,128)(2,1)}, bf16[128,3200]{1,0:T(8,128)(2,1)S(1)}, u32[]{:S(2)}, u32[]{:S(2)}) collective-permute-start(bf16[128,3200]{1,0:T(8,128)(2,1)} %collective-permute-done.5.refs_0_), channel_id=1, source_target_pairs={{0,1},{1,0},{2,3},{3,2},{4,5},{5,4},{6,7},{7,6},{8,9},{9,8},{10,11... | collective-permute-start | bytes 2457608 | tf_op jit(solution)/shard_map/ppermute | solution.py:261
  174.2 4.0 collective-permute-start.14
  176.9 3.7 collective-permute-start.15
  176.9 3.7 collective-permute-start.16
  181.3 56.0 %collective-permute-start.30 = (bf16[512,3200]{1,0:T(8,128)(2,1)}, bf16[512,3200]{1,0:T(8,128)(2,1)}, u32[]{:S(2)}, u32[]{:S(2)}) collective-permute-start(bf16[512,3200]{1,0:T(8,128)(2,1)} %all-gather.2.cloned.1.call-done), channel_id=1, source_target_pairs={{0,1},{1,0},{2,3},{3,2},{4,5},{5,4},{6,7},{7,6},{8,9},{9,8},{10,11... | collective-permute-start | bytes 9830408 | tf_op jit(solution)/shard_map/ppermute | solution.py:261
  193.6 8.3 %collective-permute-start.19 = (bf16[256,512]{1,0:T(8,128)(2,1)S(1)}, bf16[256,512]{1,0:T(8,128)(2,1)S(1)}, u32[]{:S(2)}, u32[]{:S(2)}) collective-permute-start(bf16[256,512]{1,0:T(8,128)(2,1)S(1)} %get-tuple-element.184), channel_id=1, source_target_pairs={{0,3},{1,2},{2,1},{3,0},{4,7},{5,6},{6,5},{7,4},{8,11},{9,10},{10,... | collective-permute-start | bytes 786440 | tf_op jit(solution)/shard_map/ppermute | solution.py:261
  195.3 12.7 %collective-permute-start.18 = (bf16[256,512]{1,0:T(8,128)(2,1)S(1)}, bf16[256,512]{1,0:T(8,128)(2,1)S(1)}, u32[]{:S(2)}, u32[]{:S(2)}) collective-permute-start(bf16[256,512]{1,0:T(8,128)(2,1)S(1)} %get-tuple-element.185), channel_id=1, source_target_pairs={{0,2},{1,3},{2,0},{3,1},{4,6},{5,7},{6,4},{7,5},{8,10},{9,11},{10,... | collective-permute-start | bytes 786440 | tf_op jit(solution)/shard_map/ppermute | solution.py:261
  195.8 12.2 %collective-permute-start.17 = (bf16[256,512]{1,0:T(8,128)(2,1)S(1)}, bf16[256,512]{1,0:T(8,128)(2,1)S(1)}, u32[]{:S(2)}, u32[]{:S(2)}) collective-permute-start(bf16[256,512]{1,0:T(8,128)(2,1)S(1)} %get-tuple-element.186), channel_id=1, source_target_pairs={{0,1},{1,0},{2,3},{3,2},{4,5},{5,4},{6,7},{7,6},{8,9},{9,8},{10,11... | collective-permute-start | bytes 786440 | tf_op jit(solution)/shard_map/ppermute | solution.py:261
  208.1 18.7 %collective-permute-start.22 = (bf16[64,2048]{1,0:T(8,128)(2,1)S(1)}, bf16[64,2048]{1,0:T(8,128)(2,1)S(1)}, u32[]{:S(2)}, u32[]{:S(2)}) collective-permute-start(bf16[64,2048]{1,0:T(8,128)(2,1)S(1)} %get-tuple-element.180), channel_id=1, source_target_pairs={{0,24},{4,28},{8,16},{12,20},{16,8},{20,12},{24,0},{28,4},{1,25},{... | collective-permute-start | bytes 786440 | tf_op jit(solution)/shard_map/ppermute | solution.py:264
  215.1 20.0 %collective-permute-start.21 = (bf16[64,2048]{1,0:T(8,128)(2,1)S(1)}, bf16[64,2048]{1,0:T(8,128)(2,1)S(1)}, u32[]{:S(2)}, u32[]{:S(2)}) collective-permute-start(bf16[64,2048]{1,0:T(8,128)(2,1)S(1)} %get-tuple-element.181), channel_id=1, source_target_pairs={{0,16},{4,20},{8,24},{12,28},{16,0},{20,4},{24,8},{28,12},{1,17},{... | collective-permute-start | bytes 786440 | tf_op jit(solution)/shard_map/ppermute | solution.py:264
  215.1 20.0 %collective-permute-start.20 = (bf16[64,2048]{1,0:T(8,128)(2,1)S(1)}, bf16[64,2048]{1,0:T(8,128)(2,1)S(1)}, u32[]{:S(2)}, u32[]{:S(2)}) collective-permute-start(bf16[64,2048]{1,0:T(8,128)(2,1)S(1)} %get-tuple-element.182), channel_id=1, source_target_pairs={{0,8},{4,12},{8,0},{12,4},{16,24},{20,28},{24,16},{28,20},{1,9},{5... | collective-permute-start | bytes 786440 | tf_op jit(solution)/shard_map/ppermute | solution.py:264
  215.7 19.5 %copy-start.9 = (bf16[512,3200]{1,0:T(8,128)(2,1)S(1)}, bf16[512,3200]{1,0:T(8,128)(2,1)}, u32[]{:S(2)}) copy-start(bf16[512,3200]{1,0:T(8,128)(2,1)} %all-gather.2.cloned.1.call-done) | copy-start | bytes 9830404
  251.6 5.6 collective-permute-start.33
  254.9 26.7 %collective-permute-start.25 = (bf16[256,512]{1,0:T(8,128)(2,1)}, bf16[256,512]{1,0:T(8,128)(2,1)}, u32[]{:S(2)}, u32[]{:S(2)}) collective-permute-start(bf16[256,512]{1,0:T(8,128)(2,1)} %get-tuple-element.176), channel_id=1, source_target_pairs={{0,3},{1,2},{2,1},{3,0},{4,7},{5,6},{6,5},{7,4},{8,11},{9,10},{10,... | collective-permute-start | bytes 786440 | tf_op jit(solution)/shard_map/ppermute | solution.py:261
  255.0 26.7 %collective-permute-start.24 = (bf16[256,512]{1,0:T(8,128)(2,1)}, bf16[256,512]{1,0:T(8,128)(2,1)}, u32[]{:S(2)}, u32[]{:S(2)}) collective-permute-start(bf16[256,512]{1,0:T(8,128)(2,1)} %get-tuple-element.177), channel_id=1, source_target_pairs={{0,2},{1,3},{2,0},{3,1},{4,6},{5,7},{6,4},{7,5},{8,10},{9,11},{10,... | collective-permute-start | bytes 786440 | tf_op jit(solution)/shard_map/ppermute | solution.py:261
  256.5 25.2 %collective-permute-start.23 = (bf16[256,512]{1,0:T(8,128)(2,1)}, bf16[256,512]{1,0:T(8,128)(2,1)}, u32[]{:S(2)}, u32[]{:S(2)}) collective-permute-start(bf16[256,512]{1,0:T(8,128)(2,1)} %get-tuple-element.178), channel_id=1, source_target_pairs={{0,1},{1,0},{2,3},{3,2},{4,5},{5,4},{6,7},{7,6},{8,9},{9,8},{10,11... | collective-permute-start | bytes 786440 | tf_op jit(solution)/shard_map/ppermute | solution.py:261
  256.8 4.7 collective-permute-start.32
  257.2 7.6 %collective-permute-start.31 = (f32[2,4,64]{2,1,0:T(4,128)}, f32[2,4,64]{2,1,0:T(4,128)}, u32[]{:S(2)}, u32[]{:S(2)}) collective-permute-start(f32[2,4,64]{2,1,0:T(4,128)} %constant_dynamic-update-slice_fusion.10), channel_id=1, source_target_pairs={{0,8},{4,12},{8,0},{12,4},{16,24},{20,28},{24,16},{28,20},{1,9},{5... | collective-permute-start | bytes 6152 | tf_op jit(solution)/shard_map/ppermute | solution.py:264
  275.3 36.4 %collective-permute-start.34 = (bf16[256,1600]{0,1:T(8,128)(2,1)S(1)}, bf16[256,1600]{0,1:T(8,128)(2,1)}, u32[]{:S(2)}, u32[]{:S(2)}) collective-permute-start(bf16[256,1600]{0,1:T(8,128)(2,1)S(1)} %bitcast.202), channel_id=1, source_target_pairs={{0,4},{4,0},{8,12},{12,8},{16,20},{20,16},{24,28},{28,24},{1,5},{5... | collective-permute-start | bytes 2457608 | tf_op jit(solution)/shard_map/ppermute | solution.py:267
  283.0 26.7 %collective-permute-start.28 = (bf16[64,2048]{1,0:T(8,128)(2,1)S(1)}, bf16[64,2048]{1,0:T(8,128)(2,1)S(1)}, u32[]{:S(2)}, u32[]{:S(2)}) collective-permute-start(bf16[64,2048]{1,0:T(8,128)(2,1)S(1)} %get-tuple-element.172), channel_id=1, source_target_pairs={{0,24},{4,28},{8,16},{12,20},{16,8},{20,12},{24,0},{28,4},{1,25},{... | collective-permute-start | bytes 786440 | tf_op jit(solution)/shard_map/ppermute | solution.py:264
  283.7 26.0 %collective-permute-start.27 = (bf16[64,2048]{1,0:T(8,128)(2,1)S(1)}, bf16[64,2048]{1,0:T(8,128)(2,1)S(1)}, u32[]{:S(2)}, u32[]{:S(2)}) collective-permute-start(bf16[64,2048]{1,0:T(8,128)(2,1)S(1)} %get-tuple-element.173), channel_id=1, source_target_pairs={{0,16},{4,20},{8,24},{12,28},{16,0},{20,4},{24,8},{28,12},{1,17},{... | collective-permute-start | bytes 786440 | tf_op jit(solution)/shard_map/ppermute | solution.py:264
  283.7 26.0 %collective-permute-start.26 = (bf16[64,2048]{1,0:T(8,128)(2,1)S(1)}, bf16[64,2048]{1,0:T(8,128)(2,1)}, u32[]{:S(2)}, u32[]{:S(2)}) collective-permute-start(bf16[64,2048]{1,0:T(8,128)(2,1)S(1)} %get-tuple-element.174), channel_id=1, source_target_pairs={{0,8},{4,12},{8,0},{12,4},{16,24},{20,28},{24,16},{28,20},{1,9},{5... | collective-permute-start | bytes 786440 | tf_op jit(solution)/shard_map/ppermute | solution.py:264
  324.4 24.8 %collective-permute-start.37 = (f32[2,4,64]{2,1,0:T(4,128)S(1)}, f32[2,4,64]{2,1,0:T(4,128)S(1)}, u32[]{:S(2)}, u32[]{:S(2)}) collective-permute-start(f32[2,4,64]{2,1,0:T(4,128)S(1)} %constant_dynamic-update-slice_fusion.12), channel_id=1, source_target_pairs={{0,24},{4,28},{8,16},{12,20},{16,8},{20,12},{24,0},{28,4},{1,25},{... | collective-permute-start | bytes 6152 | tf_op jit(solution)/shard_map/ppermute | solution.py:264
  325.1 24.2 %collective-permute-start.36 = (f32[2,4,64]{2,1,0:T(4,128)S(1)}, f32[2,4,64]{2,1,0:T(4,128)S(1)}, u32[]{:S(2)}, u32[]{:S(2)}) collective-permute-start(f32[2,4,64]{2,1,0:T(4,128)S(1)} %constant_dynamic-update-slice_fusion.12), channel_id=1, source_target_pairs={{0,16},{4,20},{8,24},{12,28},{16,0},{20,4},{24,8},{28,12},{1,17},{... | collective-permute-start | bytes 6152 | tf_op jit(solution)/shard_map/ppermute | solution.py:264
  325.9 23.6 %collective-permute-start.35 = (f32[2,4,64]{2,1,0:T(4,128)S(1)}, f32[2,4,64]{2,1,0:T(4,128)S(1)}, u32[]{:S(2)}, u32[]{:S(2)}) collective-permute-start(f32[2,4,64]{2,1,0:T(4,128)S(1)} %constant_dynamic-update-slice_fusion.12), channel_id=1, source_target_pairs={{0,8},{4,12},{8,0},{12,4},{16,24},{20,28},{24,16},{28,20},{1,9},{5... | collective-permute-start | bytes 6152 | tf_op jit(solution)/shard_map/ppermute | solution.py:264
  331.6 18.3 %copy-start.17 = (f32[3200]{0:T(1024)S(1)}, f32[3200]{0:T(1024)}, u32[]{:S(2)}) copy-start(f32[3200]{0:T(1024)} %dynamic_slice.104) | copy-start | bytes 38404
  353.8 17.5 %collective-permute-start.38 = (bf16[256,1600]{0,1:T(8,128)(2,1)}, bf16[256,1600]{0,1:T(8,128)(2,1)}, u32[]{:S(2)}, u32[]{:S(2)}) collective-permute-start(bf16[256,1600]{0,1:T(8,128)(2,1)} %bitcast.47), channel_id=1, source_target_pairs={{0,4},{4,0},{8,12},{12,8},{16,20},{20,16},{24,28},{28,24},{1,5},{5... | collective-permute-start | bytes 2457608 | tf_op jit(solution)/shard_map/ppermute | solution.py:267
  359.0 33.4 %copy-start.5 = (bf16[256,6144]{1,0:T(8,128)(2,1)}, bf16[256,6144]{1,0:T(8,128)(2,1)S(1)}, u32[]{:S(2)}) copy-start(bf16[256,6144]{1,0:T(8,128)(2,1)S(1)} %get-tuple-element.146) | copy-start | bytes 9437188
  392.6 32.5 %copy-start.6 = (bf16[256,6144]{1,0:T(8,128)(2,1)S(1)}, bf16[256,6144]{1,0:T(8,128)(2,1)}, u32[]{:S(2)}) copy-start(bf16[256,6144]{1,0:T(8,128)(2,1)} %copy-done.5) | copy-start | bytes 9437188
  392.6 32.5 %collective-permute-start.39 = (bf16[4,32,6144]{2,1,0:T(8,128)(2,1)S(1)}, bf16[4,32,6144]{2,1,0:T(8,128)(2,1)S(1)}, u32[]{:S(2)}, u32[]{:S(2)}) collective-permute-start(bf16[4,32,6144]{2,1,0:T(8,128)(2,1)S(1)} %slice_bitcast_fusion.3), channel_id=1, source_target_pairs={{0,4},{4,0},{8,12},{12,8},{16,20},{20,16},{24,28},{28,24},{1,5},{5... | collective-permute-start | bytes 4718600 | tf_op jit(solution)/shard_map/ppermute | solution.py:267
  395.0 36.0 %copy-start.4 = (bf16[256,6144]{1,0:T(8,128)(2,1)S(1)}, bf16[256,6144]{1,0:T(8,128)(2,1)}, u32[]{:S(2)}) copy-start(bf16[256,6144]{1,0:T(8,128)(2,1)} %get-tuple-element.145) | copy-start | bytes 9437188
  426.6 14.1 %collective-permute-start.43 = (bf16[32,6144]{1,0:T(8,128)(2,1)}, bf16[32,6144]{1,0:T(8,128)(2,1)S(1)}, u32[]{:S(2)}, u32[]{:S(2)}) collective-permute-start(bf16[32,6144]{1,0:T(8,128)(2,1)} %get-tuple-element.169), channel_id=1, source_target_pairs={{0,24},{4,28},{8,16},{12,20},{16,8},{20,12},{24,0},{28,4},{1,25},{... | collective-permute-start | bytes 1179656 | tf_op jit(solution)/shard_map/ppermute | solution.py:264
  427.7 31.0 %collective-permute-start.42 = (bf16[32,6144]{1,0:T(8,128)(2,1)}, bf16[32,6144]{1,0:T(8,128)(2,1)}, u32[]{:S(2)}, u32[]{:S(2)}) collective-permute-start(bf16[32,6144]{1,0:T(8,128)(2,1)} %get-tuple-element.170), channel_id=1, source_target_pairs={{0,16},{4,20},{8,24},{12,28},{16,0},{20,4},{24,8},{28,12},{1,17},{... | collective-permute-start | bytes 1179656 | tf_op jit(solution)/shard_map/ppermute | solution.py:264
  428.7 30.1 %collective-permute-start.41 = (bf16[32,6144]{1,0:T(8,128)(2,1)}, bf16[32,6144]{1,0:T(8,128)(2,1)}, u32[]{:S(2)}, u32[]{:S(2)}) collective-permute-start(bf16[32,6144]{1,0:T(8,128)(2,1)} %get-tuple-element.168), channel_id=1, source_target_pairs={{0,8},{4,12},{8,0},{12,4},{16,24},{20,28},{24,16},{28,20},{1,9},{5... | collective-permute-start | bytes 1179656 | tf_op jit(solution)/shard_map/ppermute | solution.py:264
  432.3 31.0 %collective-permute-start.40 = (bf16[4,32,6144]{2,1,0:T(8,128)(2,1)}, bf16[4,32,6144]{2,1,0:T(8,128)(2,1)}, u32[]{:S(2)}, u32[]{:S(2)}) collective-permute-start(bf16[4,32,6144]{2,1,0:T(8,128)(2,1)} %slice_bitcast_fusion.2), channel_id=1, source_target_pairs={{0,4},{4,0},{8,12},{12,8},{16,20},{20,16},{24,28},{28,24},{1,5},{5... | collective-permute-start | bytes 4718600 | tf_op jit(solution)/shard_map/ppermute | solution.py:267
  434.8 30.8 %copy-start.3 = (bf16[256,6144]{1,0:T(8,128)(2,1)S(1)}, bf16[256,6144]{1,0:T(8,128)(2,1)}, u32[]{:S(2)}) copy-start(bf16[256,6144]{1,0:T(8,128)(2,1)} %get-tuple-element.144) | copy-start | bytes 9437188
  465.7 32.5 %collective-permute-start.44 = (bf16[4,32,6144]{2,1,0:T(8,128)(2,1)S(1)}, bf16[4,32,6144]{2,1,0:T(8,128)(2,1)S(1)}, u32[]{:S(2)}, u32[]{:S(2)}) collective-permute-start(bf16[4,32,6144]{2,1,0:T(8,128)(2,1)S(1)} %slice_bitcast_fusion.1), channel_id=1, source_target_pairs={{0,4},{4,0},{8,12},{12,8},{16,20},{20,16},{24,28},{28,24},{1,5},{5... | collective-permute-start | bytes 4718600 | tf_op jit(solution)/shard_map/ppermute | solution.py:267
  466.7 13.9 %collective-permute-start.47 = (bf16[32,6144]{1,0:T(8,128)(2,1)S(1)}, bf16[32,6144]{1,0:T(8,128)(2,1)S(1)}, u32[]{:S(2)}, u32[]{:S(2)}) collective-permute-start(bf16[32,6144]{1,0:T(8,128)(2,1)S(1)} %get-tuple-element.166), channel_id=1, source_target_pairs={{0,24},{4,28},{8,16},{12,20},{16,8},{20,12},{24,0},{28,4},{1,25},{... | collective-permute-start | bytes 1179656 | tf_op jit(solution)/shard_map/ppermute | solution.py:264
  468.1 28.4 %collective-permute-start.46 = (bf16[32,6144]{1,0:T(8,128)(2,1)S(1)}, bf16[32,6144]{1,0:T(8,128)(2,1)S(1)}, u32[]{:S(2)}, u32[]{:S(2)}) collective-permute-start(bf16[32,6144]{1,0:T(8,128)(2,1)S(1)} %get-tuple-element.167), channel_id=1, source_target_pairs={{0,16},{4,20},{8,24},{12,28},{16,0},{20,4},{24,8},{28,12},{1,17},{... | collective-permute-start | bytes 1179656 | tf_op jit(solution)/shard_map/ppermute | solution.py:264
  469.2 27.3 %collective-permute-start.45 = (bf16[32,6144]{1,0:T(8,128)(2,1)S(1)}, bf16[32,6144]{1,0:T(8,128)(2,1)S(1)}, u32[]{:S(2)}, u32[]{:S(2)}) collective-permute-start(bf16[32,6144]{1,0:T(8,128)(2,1)S(1)} %get-tuple-element.165), channel_id=1, source_target_pairs={{0,8},{4,12},{8,0},{12,4},{16,24},{20,28},{24,16},{28,20},{1,9},{5... | collective-permute-start | bytes 1179656 | tf_op jit(solution)/shard_map/ppermute | solution.py:264
  498.7 32.8 %collective-permute-start.48 = (bf16[4,32,6144]{2,1,0:T(8,128)(2,1)S(1)}, bf16[4,32,6144]{2,1,0:T(8,128)(2,1)S(1)}, u32[]{:S(2)}, u32[]{:S(2)}) collective-permute-start(bf16[4,32,6144]{2,1,0:T(8,128)(2,1)S(1)} %slice_bitcast_fusion), channel_id=1, source_target_pairs={{0,4},{4,0},{8,12},{12,8},{16,20},{20,16},{24,28},{28,24},{1,5},{5... | collective-permute-start | bytes 4718600 | tf_op jit(solution)/shard_map/ppermute | solution.py:267
  499.9 13.9 %collective-permute-start.51 = (bf16[32,6144]{1,0:T(8,128)(2,1)S(1)}, bf16[32,6144]{1,0:T(8,128)(2,1)S(1)}, u32[]{:S(2)}, u32[]{:S(2)}) collective-permute-start(bf16[32,6144]{1,0:T(8,128)(2,1)S(1)} %get-tuple-element.163), channel_id=1, source_target_pairs={{0,24},{4,28},{8,16},{12,20},{16,8},{20,12},{24,0},{28,4},{1,25},{... | collective-permute-start | bytes 1179656 | tf_op jit(solution)/shard_map/ppermute | solution.py:264
  501.5 29.9 %collective-permute-start.50 = (bf16[32,6144]{1,0:T(8,128)(2,1)S(1)}, bf16[32,6144]{1,0:T(8,128)(2,1)S(1)}, u32[]{:S(2)}, u32[]{:S(2)}) collective-permute-start(bf16[32,6144]{1,0:T(8,128)(2,1)S(1)} %get-tuple-element.164), channel_id=1, source_target_pairs={{0,16},{4,20},{8,24},{12,28},{16,0},{20,4},{24,8},{28,12},{1,17},{... | collective-permute-start | bytes 1179656 | tf_op jit(solution)/shard_map/ppermute | solution.py:264
  501.5 29.9 %collective-permute-start.49 = (bf16[32,6144]{1,0:T(8,128)(2,1)S(1)}, bf16[32,6144]{1,0:T(8,128)(2,1)S(1)}, u32[]{:S(2)}, u32[]{:S(2)}) collective-permute-start(bf16[32,6144]{1,0:T(8,128)(2,1)S(1)} %get-tuple-element.162), channel_id=1, source_target_pairs={{0,8},{4,12},{8,0},{12,4},{16,24},{20,28},{24,16},{28,20},{1,9},{5... | collective-permute-start | bytes 1179656 | tf_op jit(solution)/shard_map/ppermute | solution.py:264
  532.0 13.9 %collective-permute-start.54 = (bf16[32,6144]{1,0:T(8,128)(2,1)S(1)}, bf16[32,6144]{1,0:T(8,128)(2,1)S(1)}, u32[]{:S(2)}, u32[]{:S(2)}) collective-permute-start(bf16[32,6144]{1,0:T(8,128)(2,1)S(1)} %get-tuple-element.160), channel_id=1, source_target_pairs={{0,24},{4,28},{8,16},{12,20},{16,8},{20,12},{24,0},{28,4},{1,25},{... | collective-permute-start | bytes 1179656 | tf_op jit(solution)/shard_map/ppermute | solution.py:264
  533.4 30.6 %collective-permute-start.53 = (bf16[32,6144]{1,0:T(8,128)(2,1)S(1)}, bf16[32,6144]{1,0:T(8,128)(2,1)S(1)}, u32[]{:S(2)}, u32[]{:S(2)}) collective-permute-start(bf16[32,6144]{1,0:T(8,128)(2,1)S(1)} %get-tuple-element.161), channel_id=1, source_target_pairs={{0,16},{4,20},{8,24},{12,28},{16,0},{20,4},{24,8},{28,12},{1,17},{... | collective-permute-start | bytes 1179656 | tf_op jit(solution)/shard_map/ppermute | solution.py:264
  533.4 30.6 %collective-permute-start.52 = (bf16[32,6144]{1,0:T(8,128)(2,1)S(1)}, bf16[32,6144]{1,0:T(8,128)(2,1)S(1)}, u32[]{:S(2)}, u32[]{:S(2)}) collective-permute-start(bf16[32,6144]{1,0:T(8,128)(2,1)S(1)} %get-tuple-element.159), channel_id=1, source_target_pairs={{0,8},{4,12},{8,0},{12,4},{16,24},{20,28},{24,16},{28,20},{1,9},{5... | collective-permute-start | bytes 1179656 | tf_op jit(solution)/shard_map/ppermute | solution.py:264
  (19 other events, 98.6 us)
Sparse Core Ops, SparseCore 0:
  89.4 73.6 all-gather.1

commit v2 on v1

--- a/solution.py
+++ b/solution.py
@@ -20,6 +20,7 @@
 MIB = 1024 * 1024
 BF16 = jnp.bfloat16
 F32 = jnp.float32
+TINY = pl.CostEstimate(flops=1, bytes_accessed=1, transcendentals=0)
 
 
 def reorder_kernel(pick_ref, x_ref, out_ref):
@@ -109,11 +110,7 @@
             pltpu.VMEM((count, rows, HEAD_DIM), F32),
             pltpu.VMEM((count, rows, HEAD_DIM), F32),
         ],
-        cost_estimate=pl.CostEstimate(
-            flops=2 * count * rows * D * width,
-            bytes_accessed=2 * D * width + count * rows * (2 * D + 4 * width),
-            transcendentals=0,
-        ),
+        cost_estimate=TINY,
         compiler_params=pltpu.CompilerParams(vmem_limit_bytes=56 * MIB),
         name="qkv",
     )(*pieces, norm_gain.reshape(1, D), qkv_weight)
@@ -125,7 +122,8 @@
     blocks = plan[-1][0] + 1
     seg_ref, sq_ref, gain_ref = refs[:3]
     p_refs = refs[3 : 3 + count]
-    out_ref, q_scale, k_scale, q_all, k_all, v_all = refs[3 + count :]
+    out_refs = refs[3 + count : 3 + count + blocks]
+    q_scale, k_scale, q_all, k_all, v_all = refs[3 + count + blocks :]
     head = pl.program_id(0)
     factor = HEAD_DIM ** (-0.5) * math.log2(math.e)
 
@@ -171,7 +169,7 @@
         peak = jnp.max(scores, axis=-1, keepdims=True)
         terms = jnp.exp2(scores - peak).astype(BF16)
         both = jnp.dot(terms, v_all[low:high, :], preferred_element_type=F32)
-        out_ref[d, begin : begin + step, :] = (
+        out_refs[d][begin : begin + step, :] = (
             both[:, :HEAD_DIM] / both[:, HEAD_DIM:]
         ).astype(BF16)
 
@@ -212,8 +210,8 @@
             pl.BlockSpec((2, HEAD_DIM), lambda h: (0, h)),
         ]
         + [pl.BlockSpec((size, 3 * HEAD_DIM), lambda h: (0, h)) for _, _, size in plan],
-        out_specs=pl.BlockSpec((blocks, chunk, HEAD_DIM), lambda h: (0, 0, h)),
-        out_shape=jax.ShapeDtypeStruct((blocks, chunk, heads * HEAD_DIM), BF16),
+        out_specs=[pl.BlockSpec((chunk, HEAD_DIM), lambda h: (0, h))] * blocks,
+        out_shape=[jax.ShapeDtypeStruct((chunk, heads * HEAD_DIM), BF16)] * blocks,
         scratch_shapes=[
             pltpu.VMEM((blocks * chunk, HEAD_DIM), F32),
             pltpu.VMEM((total, HEAD_DIM), F32),
@@ -221,14 +219,230 @@
             pltpu.VMEM((total, HEAD_DIM), BF16),
             pltpu.VMEM((total, 2 * HEAD_DIM), BF16),
         ],
-        cost_estimate=pl.CostEstimate(
-            flops=8 * heads * blocks * chunk * total * HEAD_DIM,
-            bytes_accessed=4 * total * width,
-            transcendentals=heads * blocks * chunk * total,
-        ),
+        cost_estimate=TINY,
         compiler_params=pltpu.CompilerParams(vmem_limit_bytes=56 * MIB),
         name="attend",
     )(segments, squares, qk_gain, *pieces)
+
+
+def pack_kernel(sub_ref, *refs):
+    outs = refs[-SUBS:]
+    rows, width = outs[0].shape[0], refs[0].shape[1]
+    for d in range(SUBS):
+        part = pl.ds(pl.multiple_of((sub_ref[0] ^ d) * rows, rows), rows)
+        for i, ref in enumerate(refs[:-SUBS]):
+            outs[d][:, i * width : (i + 1) * width] = ref[part, :]
+
+
+def pack(groups, sub):
+    chunk, width = groups[0].shape
+    shape = (chunk // SUBS, width * len(groups))
+    vmem = pl.BlockSpec(memory_space=pltpu.VMEM)
+    return pl.pallas_call(
+        pack_kernel,
+        in_specs=[pl.BlockSpec(memory_space=pltpu.SMEM)] + [vmem] * len(groups),
+        out_specs=[vmem] * SUBS,
+        out_shape=[jax.ShapeDtypeStruct(shape, BF16)] * SUBS,
+        compiler_params=pltpu.CompilerParams(vmem_limit_bytes=32 * MIB),
+        name="pack",
+    )(sub.reshape(1), *groups)
+
+
+def hidden_kernel(count, mask_ref, *refs):
+    mine_refs, stream_refs = refs[:SUBS], refs[SUBS : 2 * SUBS]
+    w_refs = refs[2 * SUBS : 2 * SUBS + count]
+    scale_ref, hidden_ref, stats_ref, mine, mean_wide, spread_wide = refs[2 * SUBS + count :]
+    rows = mine_refs[0].shape[0]
+    depth, block = w_refs[0].shape
+    n = pl.program_id(0)
+
+    @pl.when(n == 0)
+    def _():
+        for d in range(SUBS):
+            mine[d * rows : (d + 1) * rows, :] = mine_refs[d][...]
+
+    attn = jnp.dot(mine[:, :depth], w_refs[0][...], preferred_element_type=F32)
+    for i in range(1, count):
+        attn += jnp.dot(
+            mine[:, i * depth : (i + 1) * depth], w_refs[i][...], preferred_element_type=F32
+        )
+    columns = pl.ds(pl.multiple_of(n * block, block), block)
+    for d in range(SUBS):
+        part = slice(d * rows, (d + 1) * rows)
+        stream = stream_refs[d][0].astype(F32)
+        hidden_ref[part, columns] = stream + scale_ref[...] * attn[part, :]
+
+    @pl.when(n == pl.num_programs(0) - 1)
+    def _():
+        for d in range(SUBS):
+            part = slice(d * rows, (d + 1) * rows)
+            hidden = hidden_ref[part, :]
+            mean = jnp.sum(hidden, axis=-1, keepdims=True) / D
+            centre = hidden - mean
+            spread = jnp.sum(centre * centre, axis=-1, keepdims=True)
+            mean_wide[part, :] = jnp.broadcast_to(mean, (rows, 128))
+            spread_wide[part, :] = jnp.broadcast_to(spread, (rows, 128))
+        stats_ref[0:1, :] = mean_wide[...].T[0:1, :]
+        stats_ref[1:2, :] = spread_wide[...].T[0:1, :]
+        stats_ref[2:3, :] = jnp.full((1, SUBS * rows), mask_ref[0].astype(F32))
+
+
+def hidden_of(places, mine, residual, weights, layer_scale, mask):
+    rows = mine[0].shape[0]
+    count, depth, block = len(weights), weights[0].shape[0], 640
+    total = SUBS * rows
+    return pl.pallas_call(
+        functools.partial(hidden_kernel, count),
+        grid=(D // block,),
+        in_specs=[pl.BlockSpec(memory_space=pltpu.SMEM)]
+        + [pl.BlockSpec(mine[0].shape, lambda n: (0, 0))] * SUBS
+        + [pl.BlockSpec((1, rows, block), lambda n, j=j: (j, 0, n)) for j in places]
+        + [pl.BlockSpec((depth, block), lambda n: (0, n))] * count
+        + [pl.BlockSpec((1, block), lambda n: (0, n))],
+        out_specs=[
+            pl.BlockSpec((total, D), lambda n: (0, 0)),
+            pl.BlockSpec((3, total), lambda n: (0, 0)),
+        ],
+        out_shape=[
+            jax.ShapeDtypeStruct((total, D), F32),
+            jax.ShapeDtypeStruct((3, total), F32),
+        ],
+        scratch_shapes=[
+            pltpu.VMEM((total, count * depth), BF16),
+            pltpu.VMEM((total, 128), F32),
+            pltpu.VMEM((total, 128), F32),
+        ],
+        cost_estimate=pl.CostEstimate(
+            flops=2 * total * count * depth * D,
+            bytes_accessed=2 * count * depth * D + 6 * total * D,
+            transcendentals=0,
+        ),
+        compiler_params=pltpu.CompilerParams(vmem_limit_bytes=48 * MIB),
+        name="hidden",
+    )(mask, *mine, *residual, *weights, layer_scale.reshape(1, D))
+
+
+def norm_kernel(parts, part_ref, hidden_ref, *refs):
+    stats_refs, (w_ref, b_ref), outs = refs[:SUBS], refs[SUBS : SUBS + 2], refs[SUBS + 2 :]
+    total = hidden_ref.shape[0]
+    rows, width = total // SUBS, D // parts
+    means = [jnp.broadcast_to(ref[0:1, :], (128, total)).T for ref in stats_refs]
+    spreads = [jnp.broadcast_to(ref[1:2, :], (128, total)).T for ref in stats_refs]
+    for out in outs:
+        if out.shape[1] > width:
+            out[:, out.shape[1] - 128 :] = jnp.zeros((total, 128), BF16)
+    for d in range(SUBS):
+        where = [slice((d ^ e) * rows, ((d ^ e) + 1) * rows) for e in range(SUBS)]
+        mean = sum(means[e][where[e], :] for e in range(SUBS)) / SUBS
+        var = 0.0
+        for e in range(SUBS):
+            off = means[e][where[e], :] - mean
+            var = var + spreads[e][where[e], :] + D * off * off
+        inv = lax.rsqrt(var / (SUBS * D) + 1e-05)
+        part = slice(d * rows, (d + 1) * rows)
+        normed = (hidden_ref[part, :] - mean[:, 0:1]) * inv[:, 0:1] * w_ref[...] + b_ref[...]
+        for i in range(parts):
+            cut = normed[:, i * width : (i + 1) * width].astype(BF16)
+            for e in range(parts):
+
+                @pl.when((part_ref[0] ^ e) == i)
+                def _():
+                    outs[e][part, :width] = cut
+
+
+def norm(hidden, stats, weight, bias, part, parts):
+    total = hidden.shape[0]
+    padded = pl.cdiv(D // parts, 128) * 128
+    vmem = pl.BlockSpec(memory_space=pltpu.VMEM)
+    return pl.pallas_call(
+        functools.partial(norm_kernel, parts),
+        in_specs=[pl.BlockSpec(memory_space=pltpu.SMEM)] + [vmem] * (SUBS + 3),
+        out_specs=[vmem] * parts,
+        out_shape=[jax.ShapeDtypeStruct((total, padded), BF16)] * parts,
+        cost_estimate=pl.CostEstimate(
+            flops=8 * total * D, bytes_accessed=6 * total * D, transcendentals=0
+        ),
+        compiler_params=pltpu.CompilerParams(vmem_limit_bytes=48 * MIB),
+        name="norm",
+    )(part.reshape(1), hidden, *stats, weight.reshape(1, D), bias.reshape(1, D))
+
+
+def shares_kernel(parts, place_ref, owner_ref, *refs):
+    slab_refs, w_ref, outs, ordered = refs[:parts], refs[parts], refs[parts + 1 : -1], refs[-1]
+    merged, width = slab_refs[0].shape[0] // SUBS, w_ref.shape[0]
+    half = merged // HALVES
+    size = SUBS * half
+
+    @pl.when(pl.program_id(0) == 0)
+    def _():
+        sub, part = place_ref[0], place_ref[1]
+        for e in range(parts):
+            for d in range(SUBS):
+                target = owner_ref[(sub ^ d) * parts + (part ^ e)]
+                f, g = lax.rem(target, parts) ^ part, lax.div(target, parts) ^ sub
+                for h in range(HALVES):
+                    start = pl.multiple_of((h * parts + f) * size + g * half, half)
+                    low = d * merged + h * half
+                    ordered[pl.ds(start, half), :] = slab_refs[e][low : low + half, :width]
+
+    product = jnp.dot(ordered[...], w_ref[...], preferred_element_type=F32)
+    for i, out in enumerate(outs):
+        out[...] = product[i * size : (i + 1) * size, :].astype(BF16)
+
+
+def shares_of(slab, place, owner, fc_weight):
+    parts = len(slab)
+    total = slab[0].shape[0]
+    width, hid = fc_weight.shape
+    block = 768
+    size = total // HALVES
+    outs = pl.pallas_call(
+        functools.partial(shares_kernel, parts),
+        grid=(hid // block,),
+        in_specs=[pl.BlockSpec(memory_space=pltpu.SMEM)] * 2
+        + [pl.BlockSpec(slab[0].shape, lambda n: (0, 0))] * parts
+        + [pl.BlockSpec((width, block), lambda n: (0, n))],
+        out_specs=[pl.BlockSpec((size, block), lambda n: (0, n))] * (HALVES * parts),
+        out_shape=[jax.ShapeDtypeStruct((size, hid), BF16)] * (HALVES * parts),
+        scratch_shapes=[pltpu.VMEM((parts * total, width), BF16)],
+        cost_estimate=pl.CostEstimate(
+            flops=2 * parts * total * width * hid,
+            bytes_accessed=2 * width * hid + 2 * parts * total * (width + hid),
+            transcendentals=0,
+        ),
+        compiler_params=pltpu.CompilerParams(vmem_limit_bytes=48 * MIB),
+        name="shares",
+    )(place, owner, *slab, fc_weight)
+    return [outs[h * parts : (h + 1) * parts] for h in range(HALVES)]
+
+
+def add_kernel(count, *refs):
+    rows = refs[count].shape[0]
+    for d in range(SUBS):
+        part = slice(d * rows, (d + 1) * rows)
+        total = refs[0][part, :].astype(F32)
+        for ref in refs[1:count]:
+            total += ref[part, :].astype(F32)
+        refs[count + d][...] = total.astype(BF16)
+
+
+def add(terms):
+    rows, hid = terms[0].shape
+    block = 1536
+    return pl.pallas_call(
+        functools.partial(add_kernel, len(terms)),
+        grid=(hid // block,),
+        in_specs=[pl.BlockSpec((rows, block), lambda n: (0, n))] * len(terms),
+        out_specs=[pl.BlockSpec((rows // SUBS, block), lambda n: (0, n))] * SUBS,
+        out_shape=[jax.ShapeDtypeStruct((rows // SUBS, hid), BF16)] * SUBS,
+        cost_estimate=pl.CostEstimate(
+            flops=len(terms) * rows * hid,
+            bytes_accessed=2 * (len(terms) + 1) * rows * hid,
+            transcendentals=0,
+        ),
+        compiler_params=pltpu.CompilerParams(vmem_limit_bytes=32 * MIB),
+        name="add",
+    )(*terms)
 
 
 def per_device(
@@ -251,7 +465,7 @@
     n_seq, n_rows = lax.axis_size("seq"), lax.axis_size("rows")
     row = lax.axis_index("rows")
     parts = n_rows // SUBS
-    sub, part = row // parts, row % parts
+    sub, part = lax.div(row, parts), lax.rem(row, parts)
     width = D // parts
     chunk = rows_here // CHUNKS
     merged = chunk // SUBS
@@ -266,21 +480,13 @@
     def over_part(value, d):
         return lax.ppermute(value, "rows", [(i, i ^ d) for i in range(n_rows)])
 
-    def spread(value, axis):
-        count = 1
-        while count < lax.axis_size(axis):
-            steps = [(i, i ^ count) for i in range(lax.axis_size(axis))]
-            value = jnp.concatenate([value, lax.ppermute(value, axis, steps)])
-            count *= 2
-        return value
-
     def pick(value, index, axis=0):
         return lax.dynamic_index_in_dim(value, index, axis, keepdims=False)
 
     fence = lax.optimization_barrier
 
     tokens = reorder(x, chunk)
-    cuts = [0, rows_here * 3 // 4, rows_here]
+    cuts = [0, rows_here // 4, rows_here * 3 // 4, rows_here]
     cut = [tokens[low:high] for low, high in zip(cuts, cuts[1:])]
     by_sub = tokens.reshape(CHUNKS, SUBS, merged, D)
     residual = {0: pick(by_sub, sub, 1)}
@@ -290,36 +496,41 @@
     group = max(1, min(n_seq, TILE // rows_here))
     projected, squares = {}, {}
 
+    own_id = segment_ids[0, :1]
+    leads = [own_id] + [over_seq(own_id, d) for d in range(group, n_seq, group)]
+    strips = {d: over_seq(strip, d) for d in range(2, n_seq, 2)}
     far = {d: over_seq(cut[0], d) for d in range(2, n_seq, 2)}
     near = over_seq(tokens, 1)
-    strips = {d: over_seq(strip, d) for d in range(2, n_seq, 2)}
-    for d in (1, 2):
-        residual[d] = over_sub(to_send[d], d)
+    residual[1] = over_sub(to_send[1], 1)
     given, given_s = project([tokens, near], norm_gain, qkv_weight)
     for d in range(2):
         projected[d, 0], squares[d, 0] = given[d], given_s[d]
-    state = far, cut[1], strips, residual, to_send, squares, segment_ids, pad_mask, out_weight
-    far, later, strips, residual, to_send, squares, segment_ids, pad_mask, out_weight = fence(state)
-
-    coming = {d: over_seq(later, d) for d in range(2, n_seq, 2)}
-    out_blocks = {0: out_weight, 1: over_seq(out_weight, 1)}
+    state = leads, strips, far, residual, to_send, cut, squares, out_weight
+    leads, strips, far, residual, to_send, cut, squares, out_weight = fence(state)
+    leads = jnp.concatenate(leads)
+
+    out_blocks = {0: out_weight}
     for d in range(2, n_seq, 2):
         out_blocks[d] = lax.all_gather(strips[d], "rows", axis=0, tiled=True)
-        far[d + 1] = over_seq(far[d], 1)
-    for d in range(3, SUBS):
-        residual[d] = over_sub(to_send[d], d)
-    leads = spread(segment_ids[0, :1], "seq")[::group]
-    masks = spread(pad_mask[0, :1], "rows")
-    given, given_s = project([far[d] for d in range(2, n_seq)], norm_gain, qkv_weight)
-    for d in range(2, n_seq):
-        projected[d, 0], squares[d, 0] = given[d - 2], given_s[d - 2]
-    far, residual, squares, leads, masks = fence((coming, residual, squares, leads, masks))
-
-    for d in range(2, n_seq, 2):
-        far[d + 1] = over_seq(far[d], 1)
-    given, given_s = project([far[d] for d in range(2, n_seq)], norm_gain, qkv_weight)
-    for d in range(2, n_seq):
-        projected[d, 1], squares[d, 1] = given[d - 2], given_s[d - 2]
+    for i in range(len(cut)):
+        coming = {}
+        if i + 1 < len(cut):
+            coming = {d: over_seq(cut[i + 1], d) for d in range(2, n_seq, 2)}
+        if i == 0:
+            residual[2] = over_sub(to_send[2], 2)
+        if i == 1:
+            residual[3] = over_sub(to_send[3][:1], 3)
+            out_blocks[1] = over_seq(out_weight, 1)
+        for d in range(2, n_seq, 2):
+            far[d + 1] = over_seq(far[d], 1)
+        given, given_s = project([far[d] for d in range(2, n_seq)], norm_gain, qkv_weight)
+        for d in range(2, n_seq):
+            projected[d, i], squares[d, i] = given[d - 2], given_s[d - 2]
+        if i + 1 < len(cut):
+            held = {d: residual[d] for d in range(3)}
+            state = coming, held, to_send, cut, squares, out_weight
+            far, held, to_send, cut, squares, out_weight = fence(state)
+            residual.update(held)
     plan, pieces = [], []
     for d, i in sorted(projected):
         plan.append((d, cuts[i], projected[d, i].shape[0]))
@@ -333,111 +544,88 @@
         total = total + jnp.stack([there[d ^ e] for d in range(n_seq)])
     total = jnp.transpose(total, (1, 0, 2)).reshape(2, n_seq * rows_here)
 
+    sub_ln = lax.dynamic_slice_in_dim(ln_weight, sub * D, D, 0)
+    sub_bias = lax.dynamic_slice_in_dim(ln_bias, sub * D, D, 0)
+    place = jnp.stack([sub, part])
+    relative = np.array([d * parts + e for e in range(parts) for d in range(SUBS)], np.int32)
+
+    def heads_of(j, sums):
+        return attend(pieces, plan, rows_here, sums, leads, qk_gain, j * chunk, chunk)
+
+    def gather_heads(heads):
+        return [heads[0]] + [over_seq(heads[d], d) for d in range(1, n_seq)]
+
+    def gather_rows(groups):
+        packed = pack(groups, sub)
+        return [packed[0]] + [over_sub(packed[d], d) for d in range(1, SUBS)]
+
+    def to_hidden(j, mine):
+        own = pad_mask[0, :1]
+        return hidden_of(places[j], mine, residual, out_weights, layer_scale, own)
+
+    def to_normed(hidden, stats):
+        known = [stats] + [over_sub(stats, e) for e in range(1, SUBS)]
+        return norm(hidden, known, sub_ln, sub_bias, part, parts), known
+
+    def over_parts(values):
+        return [values[0]] + [over_part(values[e], e) for e in range(1, parts)]
+
+    def finish(terms, own_mask):
+        pre = sum(term.astype(F32) for term in terms)
+        return (jax.nn.gelu(pre + fc_bias, approximate=False) * own_mask).astype(BF16)
+
+    heads_0 = heads_of(0, total)
+    heads_0, total, out_blocks, residual = fence((heads_0, total, out_blocks, residual))
+    places = [(0, 0, 0, 0), (1, 1, 1, 0)]
+    residual = [residual[d] for d in range(SUBS)]
+
     for d in range(2, n_seq, 2):
         out_blocks[d + 1] = over_seq(out_blocks[d], 1)
-    out_full = jnp.concatenate([out_blocks[d] for d in range(n_seq)], axis=0)
-
-    sub_ln = lax.dynamic_slice_in_dim(ln_weight, sub * D, D, 0)
-    sub_bias = lax.dynamic_slice_in_dim(ln_bias, sub * D, D, 0)
-    source = jnp.argmax(owner[None, :] == jnp.arange(n_rows, dtype=jnp.int32)[:, None], axis=1)
-    own_mask = pick(masks, pick(source, row) ^ row).astype(F32)
-    wanted = []
-    for f in range(parts):
-        for g in range(SUBS):
-            p = pick(source, (sub ^ g) * parts + (part ^ f))
-            wanted.append((p % parts ^ part) * SUBS + (p // parts ^ sub))
-    wanted_hot = (
-        jnp.stack(wanted)[:, None] == jnp.arange(n_rows, dtype=jnp.int32)[None, :]
-    ).astype(BF16)
-
-    def heads_of(j, sums):
-        return attend(pieces, plan, rows_here, sums, leads, qk_gain, j * chunk, chunk)
-
-    def gather_rows(heads):
-        groups = [heads[0]] + [over_seq(heads[d], d) for d in range(1, n_seq)]
-        heads = jnp.concatenate(groups, axis=-1).reshape(SUBS, merged, HEADS * HEAD_DIM)
-        mine = [pick(heads, sub)]
-        for d in range(1, SUBS):
-            mine.append(over_sub(pick(heads, sub ^ d), d))
-        return jnp.concatenate(mine, axis=0)
-
-    def to_slab(j, mine):
-        attn = jnp.dot(mine, out_full, preferred_element_type=F32)
-        stream = jnp.concatenate([residual[d][j] for d in range(SUBS)], axis=0).astype(F32)
-        hidden = stream + layer_scale * attn
-        mean_here = jnp.mean(hidden, axis=-1)
-        centre = hidden - mean_here[:, None]
-        spread_here = jnp.sum(centre * centre, axis=-1)
-        stats = jnp.stack([mean_here, spread_here]).reshape(2, SUBS, merged)
-        known = [stats]
-        for e in range(1, SUBS):
-            there = over_sub(stats, e)
-            known.append(jnp.stack([there[:, d ^ e] for d in range(SUBS)], axis=1))
-        mean = sum(k[0] for k in known) / SUBS
-        var = sum(k[1] + D * (k[0] - mean) * (k[0] - mean) for k in known) / (SUBS * D)
-        mean, var = mean.reshape(-1, 1), var.reshape(-1, 1)
-        normed = (
-            (hidden - mean) * lax.rsqrt(var + 1e-05) * sub_ln + sub_bias
-        ).astype(BF16)
-        by_part = jnp.stack([normed[:, i * width : (i + 1) * width] for i in range(parts)])
-        slab = [pick(by_part, part)]
-        for e in range(1, parts):
-            slab.append(over_part(pick(by_part, part ^ e), e))
-        return jnp.concatenate(slab, axis=0)
-
-    def to_shares(slab):
-        half = merged // HALVES
-        ordered = jnp.einsum(
-            "jp,phms->hjms",
-            wanted_hot,
-            slab.reshape(n_rows, HALVES, half, width),
-            preferred_element_type=F32,
-        ).astype(BF16)
-        shares = jnp.dot(
-            ordered.reshape(n_rows * merged, width), fc_weight, preferred_element_type=F32
-        ).astype(BF16)
-        return shares.reshape(HALVES, parts, SUBS, half, hid)
-
-    def sum_parts(shares):
-        summed = shares[0].astype(F32)
-        for e in range(1, parts):
-            summed = summed + over_part(shares[e], e).astype(F32)
-        return summed.astype(BF16)
-
-    def sum_subs(summed):
-        pre = summed[0].astype(F32)
-        for d in range(1, SUBS):
-            pre = pre + over_sub(summed[d], d).astype(F32)
-        return pre
-
-    def finish(pre):
-        return (jax.nn.gelu(pre + fc_bias, approximate=False) * own_mask).astype(BF16)
-
-    heads, rows, slab, shares, summed, pre, outs = {}, {}, {}, {}, {}, {}, {}
-    state = total, heads, rows, slab, shares, summed, pre, outs
-    units = [(j, h) for j in range(CHUNKS) for h in range(HALVES)]
-    for tick in range(3 + CHUNKS + len(units) + 1):
-        total, heads, rows, slab, shares, summed, pre, outs = state
-        new = total, {}, {}, {}, dict(shares), {}, {}, dict(outs)
-        if tick < CHUNKS:
-            new[1][tick] = heads_of(tick, total)
-        for j in heads:
-            new[2][j] = gather_rows(heads[j])
-        for j in rows:
-            new[3][j] = to_slab(j, rows[j])
-        for j in slab:
-            given = to_shares(slab[j])
-            new[4].update({(j, h): given[h] for h in range(HALVES)})
-        if shares:
-            unit = min(shares)
-            new[5][unit] = sum_parts(new[4].pop(unit))
-        for unit in summed:
-            new[6][unit] = sum_subs(summed[unit])
-        for unit in pre:
-            new[7][unit] = finish(pre[unit])
-        state = fence(new)
-    outs = state[-1]
-    return jnp.concatenate([outs[unit] for unit in units], axis=0)[None]
+    last = over_sub(to_send[3][1:], 3)
+    heads_1 = heads_of(1, total)
+    rows_0 = gather_rows(gather_heads(heads_0))
+    heads_1, rows_0, out_blocks, last = fence((heads_1, rows_0, out_blocks, last))
+    out_weights = [out_blocks[d] for d in range(n_seq)]
+
+    hidden_0 = to_hidden(0, rows_0)
+    groups_1 = gather_heads(heads_1)
+    hidden_0, groups_1 = fence((hidden_0, groups_1))
+
+    rows_1 = gather_rows(groups_1)
+    normed_0, known = to_normed(*hidden_0)
+    slab_0 = over_parts(normed_0)
+    slab_0, known, rows_1 = fence((slab_0, known, rows_1))
+
+    residual = [*residual[:3], last]
+    normed_1, _ = to_normed(*to_hidden(1, rows_1))
+    slab_0, known, normed_1 = fence((slab_0, known, normed_1))
+
+    slab_1 = over_parts(normed_1)
+    waiting = shares_of(slab_0, place, owner, fc_weight)
+    slab_1, waiting, known = fence((slab_1, waiting, known))
+
+    units = CHUNKS * HALVES
+    by_part, by_sub, outs, own_mask = [], [], [], None
+    for tick in range(units + 2):
+        new_by_part, new_by_sub = [], []
+        if waiting:
+            new_by_part = [over_parts(waiting[0])]
+            waiting = waiting[1:]
+        if tick == 0:
+            waiting = waiting + shares_of(slab_1, place, owner, fc_weight)
+            line = jnp.stack([stats[2, 0] for stats in known])
+            masks = jnp.concatenate(over_parts([line] * parts))
+            given = (row ^ relative)[:, None] == jnp.arange(n_rows, dtype=jnp.int32)[None, :]
+            given = given & (owner[None, :] == row)
+            own_mask = jnp.sum(jnp.where(given, masks[:, None], 0.0))
+        if by_part:
+            summed = add(by_part[0])
+            new_by_sub = [[summed[0]] + [over_sub(summed[d], d) for d in range(1, SUBS)]]
+        if by_sub:
+            outs = outs + [finish(by_sub[0], own_mask)]
+        state = waiting, new_by_part, new_by_sub, outs, own_mask
+        waiting, by_part, by_sub, outs, own_mask = fence(state)
+    return jnp.concatenate(outs, axis=0)[None]
 
 
 def solution(mesh):

time: 584 us -> 495 us (0.85)
  the two profiles are of different devices: /device:TPU:0 before, /device:TPU:16 now
where the time goes in v2:
time: 495 us; the launch traced here: 486 us
  waiting for transfers between devices  216 us (44%)
  Pallas kernels  147 us (30%)
  starting transfers between devices  59.5 us (12%)
  local copies, waits for them, and re-layouts  31.4 us (6%)
  other arithmetic  17.1 us (3%)
  between operations  14.1 us (3%)
    ppermute x28, waiting for transfers between devices, over_sub(): lax.ppermute(value, 'rows', [(i, i ^ d * parts) for i in range(n_rows)])  184 us
    pallas_call x4, Pallas kernels, project(): pl.pallas_call(functools.partial(qkv_kernel, count), grid=(width // block...  48.5 us
    ppermute x28, starting transfers between devices, over_sub(): lax.ppermute(value, 'rows', [(i, i ^ d * parts) for i in range(n_rows)])  39.4 us
    pallas_call x2, Pallas kernels, shares_of(): pl.pallas_call(functools.partial(shares_kernel, parts), grid=(hid // bloc...  33.1 us
    pallas_call x2, Pallas kernels, attend(): pl.pallas_call(functools.partial(attend_kernel, plan, rows, first, chunk,...  32.3 us
    ppermute x20, waiting for transfers between devices, over_seq(): return lax.ppermute(value, 'seq', [(i, i ^ d) for i in range(n_seq)])  24.1 us
    pallas_call x2, Pallas kernels, hidden_of(): pl.pallas_call(functools.partial(hidden_kernel, count), grid=(D // block,...  22.8 us
    unnamed x74, local copies, waits for them, and re-layouts  15.3 us
  transfers between devices with their start and end apart: 56, of which 29 were waited for; matrix products, arithmetic and copies ran while one was open for 6% of the time, Pallas kernels for 27%

profile of v2, /device:TPU:16, one launch (start us, length us, event | category | flops | bytes accessed | tf_op | source)
XLA Modules:
  0.0 485.7 jit_solution(4440612862902257626)
XLA Ops:
  6.5 1.9 copy-done.2
  12.1 1.5 collective-permute-start.2
  13.6 1.8 dynamic-slice_bitcast_fusion
  15.5 1.6 collective-permute-start.3
  19.9 1.5 collective-permute-start
  23.3 20.6 %qkv.4 = (f32[512,1536]{1,0:T(8,128)}, f32[512,1536]{1,0:T(8,128)}, f32[2,512]{1,0:T(2,128)}, f32[2,512]{1,0:T(2,128)}) custom-call(bf16[512,3200]{1,0:T(8,128)(2,1)} %copy-done, bf16[512,3200]{1,0:T(8,128)(2,1)} %collective-permute-done.4.refs_1_, f32[1,3200]{1,0:T(1,128)} %reshape.42.refs_2_, bf16[3200,1536]{1,0:T(8,128)(2,1)} %refs_3_.7), custom_call_target="tpu_custom_call" | custom-call | flops 1 | bytes 1 | tf_op jit(solution)/shard_map/qkv/pallas_call | solution.py:96
  45.0 2.2 collective-permute-done.7.refs_1_
  48.1 7.8 %qkv.5 = (f32[128,1536]{1,0:T(8,128)}, f32[128,1536]{1,0:T(8,128)}, f32[2,128]{1,0:T(2,128)}, f32[2,128]{1,0:T(2,128)}) custom-call(bf16[128,3200]{1,0:T(8,128)(2,1)} %collective-permute-done.2.refs_0_, bf16[128,3200]{1,0:T(8,128)(2,1)} %copy-done.22, f32[1,3200]{1,0:T(1,128)} %reshape.42.refs_2_, bf16[3200,1536]{1,0:T(8,128)(2,1)} %refs_3_.7), custom_call_target="tpu_custom_call" | custom-call | flops 1 | bytes 1 | tf_op jit(solution)/shard_map/qkv/pallas_call | solution.py:96
  55.9 39.8 %collective-permute-done.6.refs_6_ = bf16[2,64,3200]{2,1,0:T(8,128)(2,1)S(1)} collective-permute-done((bf16[2,64,3200]{2,1,0:T(8,128)(2,1)S(1)}, bf16[2,64,3200]{2,1,0:T(8,128)(2,1)S(1)}, u32[]{:S(2)}, u32[]{:S(2)}) %collective-permute-start.6) | collective-permute-done | bytes 819232 | tf_op jit(solution)/shard_map/ppermute | solution.py:478
  97.6 3.2 collective-permute-done.9.refs_1_
  101.9 12.1 %qkv.6 = (f32[256,1536]{1,0:T(8,128)}, f32[256,1536]{1,0:T(8,128)}, f32[2,256]{1,0:T(2,128)}, f32[2,256]{1,0:T(2,128)}) custom-call(bf16[256,3200]{1,0:T(8,128)(2,1)} %copy-done.17, bf16[256,3200]{1,0:T(8,128)(2,1)} %copy-done.18, f32[1,3200]{1,0:T(1,128)} %reshape.42.refs_2_, bf16[3200,1536]{1,0:T(8,128)(2,1)} %refs_3_.7), custom_call_target="tpu_custom_call" | custom-call | flops 1 | bytes 1 | tf_op jit(solution)/shard_map/qkv/pallas_call | solution.py:96
  114.0 2.6 collective-permute-done.8.refs_0_
  117.4 1.6 collective-permute-done.10.refs_1_
  119.9 8.0 %qkv.7 = (f32[128,1536]{1,0:T(8,128)}, f32[128,1536]{1,0:T(8,128)}, f32[2,128]{1,0:T(2,128)}, f32[2,128]{1,0:T(2,128)}) custom-call(bf16[128,3200]{1,0:T(8,128)(2,1)} %copy-done.20, bf16[128,3200]{1,0:T(8,128)(2,1)} %copy-done.21, f32[1,3200]{1,0:T(1,128)} %reshape.42.refs_2_, bf16[3200,1536]{1,0:T(8,128)(2,1)} %refs_3_.7), custom_call_target="tpu_custom_call" | custom-call | flops 1 | bytes 1 | tf_op jit(solution)/shard_map/qkv/pallas_call | solution.py:96
  130.7 1.9 pad_add_fusion.refs_0_
  132.6 6.3 %collective-permute-start.15 = (bf16[1,64,3200]{2,1,0:T(8,128)(2,1)S(1)}, bf16[1,64,3200]{2,1,0:T(8,128)(2,1)S(1)}, u32[]{:S(2)}, u32[]{:S(2)}) collective-permute-start(bf16[1,64,3200]{2,1,0:T(8,128)(2,1)S(1)} %slice.83), channel_id=1, source_target_pairs={{0,24},{4,28},{8,16},{12,20},{16,8},{20,12},{24,0},{28,4},{1,25},{... | collective-permute-start | bytes 1228808 | tf_op jit(solution)/shard_map/ppermute | solution.py:478
  140.1 2.0 collective-permute-done.13
  142.8 16.0 %attend.2 = (bf16[256,512]{1,0:T(8,128)(2,1)}, bf16[256,512]{1,0:T(8,128)(2,1)}, bf16[256,512]{1,0:T(8,128)(2,1)}, bf16[256,512]{1,0:T(8,128)(2,1)}) custom-call(s32[2]{0:T(128)} %pad_add_fusion.refs_0_, f32[2,2048]{1,0:T(2,128)} %bitcast.36, f32[2,512]{1,0:T(2,128)} %refs_2_.5, f32[512,1536]{1,0:T(8,128)} %get-tuple-element.252.refs_3_, ...), custom_call_target="tpu_custom_call" | custom-call | flops 1 | bytes 1 | tf_op jit(solution)/shard_map/attend/pallas_call | solution.py:204
  160.9 4.0 collective-permute-done.16.refs_1_
  164.9 3.8 collective-permute-done.17.refs_2_
  168.7 3.9 collective-permute-done.18.refs_3_
  173.6 3.2 collective-permute-start.19
  176.9 2.7 collective-permute-start.20
  181.2 16.4 %attend.3 = (bf16[256,512]{1,0:T(8,128)(2,1)}, bf16[256,512]{1,0:T(8,128)(2,1)}, bf16[256,512]{1,0:T(8,128)(2,1)}, bf16[256,512]{1,0:T(8,128)(2,1)}) custom-call(s32[2]{0:T(128)} %pad_add_fusion.refs_0_, f32[2,2048]{1,0:T(2,128)} %bitcast.37, f32[2,512]{1,0:T(2,128)} %refs_2_.5, f32[512,1536]{1,0:T(8,128)} %get-tuple-element.252.refs_3_, ...), custom_call_target="tpu_custom_call" | custom-call | flops 1 | bytes 1 | tf_op jit(solution)/shard_map/attend/pallas_call | solution.py:204
  197.7 6.6 %collective-permute-done.21.refs_3_ = bf16[64,2048]{1,0:T(8,128)(2,1)S(1)} collective-permute-done((bf16[64,2048]{1,0:T(8,128)(2,1)S(1)}, bf16[64,2048]{1,0:T(8,128)(2,1)S(1)}, u32[]{:S(2)}, u32[]{:S(2)}) %collective-permute-start.21) | collective-permute-done | bytes 262176 | tf_op jit(solution)/shard_map/ppermute | solution.py:478
  206.1 11.4 %hidden.2 = (f32[256,3200]{1,0:T(8,128)}, f32[3,256]{1,0:T(4,128)S(1)}) custom-call(s32[1]{0:T(128)} %bitcast.1.mask_ref, bf16[64,2048]{1,0:T(8,128)(2,1)S(1)} %get-tuple-element.285.refs_0_, bf16[64,2048]{1,0:T(8,128)(2,1)S(1)} %collective-permute-done.19.refs_1_, bf16[64,2048]{1,0:T(8,128)(2,1)S(1)} %collective-permute-done.20.refs_2_, ...), custom_call_target="tpu_custom_call" | custom-call | flops 3355443200 | bytes 18022400 | tf_op jit(solution)/shard_map/hidden/pallas_call | solution.py:294
  219.4 2.5 collective-permute-start.27
  223.9 1.9 copy-done.3
  225.8 1.9 norm.2
  232.0 5.8 %collective-permute-done.31.refs_1_ = bf16[64,2048]{1,0:T(8,128)(2,1)S(1)} collective-permute-done((bf16[64,2048]{1,0:T(8,128)(2,1)S(1)}, bf16[64,2048]{1,0:T(8,128)(2,1)S(1)}, u32[]{:S(2)}, u32[]{:S(2)}) %collective-permute-start.31) | collective-permute-done | bytes 262176 | tf_op jit(solution)/shard_map/ppermute | solution.py:478
  237.8 10.8 %collective-permute-done.32.refs_2_ = bf16[64,2048]{1,0:T(8,128)(2,1)S(1)} collective-permute-done((bf16[64,2048]{1,0:T(8,128)(2,1)S(1)}, bf16[64,2048]{1,0:T(8,128)(2,1)S(1)}, u32[]{:S(2)}, u32[]{:S(2)}) %collective-permute-start.32) | collective-permute-done | bytes 262176 | tf_op jit(solution)/shard_map/ppermute | solution.py:478
  248.6 4.7 collective-permute-done.33.refs_3_
  253.3 11.4 %hidden.3 = (f32[256,3200]{1,0:T(8,128)}, f32[3,256]{1,0:T(4,128)S(1)}) custom-call(s32[1]{0:T(128)} %bitcast.1.mask_ref, bf16[64,2048]{1,0:T(8,128)(2,1)S(1)} %get-tuple-element.321.refs_0_, bf16[64,2048]{1,0:T(8,128)(2,1)S(1)} %collective-permute-done.31.refs_1_, bf16[64,2048]{1,0:T(8,128)(2,1)S(1)} %collective-permute-done.32.refs_2_, ...), custom_call_target="tpu_custom_call" | custom-call | flops 3355443200 | bytes 18022400 | tf_op jit(solution)/shard_map/hidden/pallas_call | solution.py:294
  266.0 2.2 collective-permute-start.34
  268.3 2.1 collective-permute-done.35.refs_2_
  270.5 1.9 copy-done.4
  272.4 2.0 norm.3
  275.9 16.7 %shares.2 = (bf16[128,6144]{1,0:T(8,128)(2,1)S(1)}, bf16[128,6144]{1,0:T(8,128)(2,1)}, bf16[128,6144]{1,0:T(8,128)(2,1)}, bf16[128,6144]{1,0:T(8,128)(2,1)}) custom-call(s32[2]{0:T(128)S(1)} %pad_add_fusion.1.place_ref, s32[8]{0:T(128)S(1)} %copy-done.14, bf16[256,1664]{1,0:T(8,128)(2,1)S(1)} %get-tuple-element.332.refs_0_, ...), custom_call_target="tpu_custom_call" | custom-call | flops 10066329600 | bytes 27590656 | tf_op jit(solution)/shard_map/shares/pallas_call | solution.py:399
  295.7 2.7 pad_maximum_fusion
  299.8 16.4 %shares.3 = (bf16[128,6144]{1,0:T(8,128)(2,1)S(1)}, bf16[128,6144]{1,0:T(8,128)(2,1)S(1)}, bf16[128,6144]{1,0:T(8,128)(2,1)}, bf16[128,6144]{1,0:T(8,128)(2,1)}) custom-call(s32[2]{0:T(128)S(1)} %pad_add_fusion.1.place_ref, s32[8]{0:T(128)S(1)} %copy-done.14, bf16[256,1664]{1,0:T(8,128)(2,1)S(1)} %get-tuple-element.344.refs_0_, ...), custom_call_target="tpu_custom_call" | custom-call | flops 10066329600 | bytes 27590656 | tf_op jit(solution)/shard_map/shares/pallas_call | solution.py:399
  317.3 8.4 %collective-permute-done.39 = f32[4]{0:T(128)S(1)} collective-permute-done((f32[4]{0:T(128)S(1)}, f32[4]{0:T(128)S(1)}, u32[]{:S(2)}, u32[]{:S(2)}) %collective-permute-start.39) | collective-permute-done | bytes 48 | tf_op jit(solution)/shard_map/ppermute | solution.py:481
  325.7 2.7 concatenate.15
  331.6 2.6 add.192
  334.2 1.8 collective-permute-start.41
  337.8 10.4 %collective-permute-done.41 = bf16[32,6144]{1,0:T(8,128)(2,1)S(1)} collective-permute-done((bf16[32,6144]{1,0:T(8,128)(2,1)S(1)}, bf16[32,6144]{1,0:T(8,128)(2,1)S(1)}, u32[]{:S(2)}, u32[]{:S(2)}) %collective-permute-start.41) | collective-permute-done | bytes 393248 | tf_op jit(solution)/shard_map/ppermute | solution.py:478
  348.2 13.3 %collective-permute-done.42 = bf16[32,6144]{1,0:T(8,128)(2,1)S(1)} collective-permute-done((bf16[32,6144]{1,0:T(8,128)(2,1)S(1)}, bf16[32,6144]{1,0:T(8,128)(2,1)S(1)}, u32[]{:S(2)}, u32[]{:S(2)}) %collective-permute-start.42) | collective-permute-done | bytes 393248 | tf_op jit(solution)/shard_map/ppermute | solution.py:478
  361.5 5.9 %collective-permute-done.43 = bf16[32,6144]{1,0:T(8,128)(2,1)S(1)} collective-permute-done((bf16[32,6144]{1,0:T(8,128)(2,1)S(1)}, bf16[32,6144]{1,0:T(8,128)(2,1)S(1)}, u32[]{:S(2)}, u32[]{:S(2)}) %collective-permute-start.43) | collective-permute-done | bytes 393248 | tf_op jit(solution)/shard_map/ppermute | solution.py:478
  368.9 2.2 collective-permute-start.46
  372.4 2.6 fusion.3
  375.0 6.2 %collective-permute-done.45 = bf16[32,6144]{1,0:T(8,128)(2,1)S(1)} collective-permute-done((bf16[32,6144]{1,0:T(8,128)(2,1)S(1)}, bf16[32,6144]{1,0:T(8,128)(2,1)S(1)}, u32[]{:S(2)}, u32[]{:S(2)}) %collective-permute-start.45) | collective-permute-done | bytes 393248 | tf_op jit(solution)/shard_map/ppermute | solution.py:478
  381.2 15.0 %collective-permute-done.46 = bf16[32,6144]{1,0:T(8,128)(2,1)S(1)} collective-permute-done((bf16[32,6144]{1,0:T(8,128)(2,1)S(1)}, bf16[32,6144]{1,0:T(8,128)(2,1)S(1)}, u32[]{:S(2)}, u32[]{:S(2)}) %collective-permute-start.46) | collective-permute-done | bytes 393248 | tf_op jit(solution)/shard_map/ppermute | solution.py:478
  396.2 6.2 %collective-permute-done.47 = bf16[32,6144]{1,0:T(8,128)(2,1)S(1)} collective-permute-done((bf16[32,6144]{1,0:T(8,128)(2,1)S(1)}, bf16[32,6144]{1,0:T(8,128)(2,1)S(1)}, u32[]{:S(2)}, u32[]{:S(2)}) %collective-permute-start.47) | collective-permute-done | bytes 393248 | tf_op jit(solution)/shard_map/ppermute | solution.py:478
  402.4 1.5 collective-permute-start.48
  406.2 2.1 collective-permute-start.51
  408.2 2.6 fusion.7
  410.8 7.0 %collective-permute-done.49 = bf16[32,6144]{1,0:T(8,128)(2,1)S(1)} collective-permute-done((bf16[32,6144]{1,0:T(8,128)(2,1)S(1)}, bf16[32,6144]{1,0:T(8,128)(2,1)S(1)}, u32[]{:S(2)}, u32[]{:S(2)}) %collective-permute-start.49) | collective-permute-done | bytes 393248 | tf_op jit(solution)/shard_map/ppermute | solution.py:478
  417.8 14.1 %collective-permute-done.50 = bf16[32,6144]{1,0:T(8,128)(2,1)S(1)} collective-permute-done((bf16[32,6144]{1,0:T(8,128)(2,1)S(1)}, bf16[32,6144]{1,0:T(8,128)(2,1)S(1)}, u32[]{:S(2)}, u32[]{:S(2)}) %collective-permute-start.50) | collective-permute-done | bytes 393248 | tf_op jit(solution)/shard_map/ppermute | solution.py:478
  431.9 7.1 %collective-permute-done.51 = bf16[32,6144]{1,0:T(8,128)(2,1)S(1)} collective-permute-done((bf16[32,6144]{1,0:T(8,128)(2,1)S(1)}, bf16[32,6144]{1,0:T(8,128)(2,1)S(1)}, u32[]{:S(2)}, u32[]{:S(2)}) %collective-permute-start.51) | collective-permute-done | bytes 393248 | tf_op jit(solution)/shard_map/ppermute | solution.py:478
  441.2 2.5 collective-permute-start.54
  443.6 2.6 fusion.11
  446.2 6.4 %collective-permute-done.52 = bf16[32,6144]{1,0:T(8,128)(2,1)S(1)} collective-permute-done((bf16[32,6144]{1,0:T(8,128)(2,1)S(1)}, bf16[32,6144]{1,0:T(8,128)(2,1)S(1)}, u32[]{:S(2)}, u32[]{:S(2)}) %collective-permute-start.52) | collective-permute-done | bytes 393248 | tf_op jit(solution)/shard_map/ppermute | solution.py:478
  452.6 14.9 %collective-permute-done.53 = bf16[32,6144]{1,0:T(8,128)(2,1)S(1)} collective-permute-done((bf16[32,6144]{1,0:T(8,128)(2,1)S(1)}, bf16[32,6144]{1,0:T(8,128)(2,1)S(1)}, u32[]{:S(2)}, u32[]{:S(2)}) %collective-permute-start.53) | collective-permute-done | bytes 393248 | tf_op jit(solution)/shard_map/ppermute | solution.py:478
  467.6 7.2 %collective-permute-done.54 = bf16[32,6144]{1,0:T(8,128)(2,1)S(1)} collective-permute-done((bf16[32,6144]{1,0:T(8,128)(2,1)S(1)}, bf16[32,6144]{1,0:T(8,128)(2,1)S(1)}, u32[]{:S(2)}, u32[]{:S(2)}) %collective-permute-start.54) | collective-permute-done | bytes 393248 | tf_op jit(solution)/shard_map/ppermute | solution.py:478
  474.7 2.6 fusion.15
  (178 shorter events, 56.4 us)
Async XLA Ops:
  6.5 152.2 %all-gather.2.cloned.1.call-start = ((), (), s32[]{:S(2)}) async-start(), calls=%async_computation | async-start | bytes 3686400 | tf_op jit(solution)/shard_map/all_gather | solution.py:514
  10.6 12.7 %collective-permute-start.4 = (bf16[512,3200]{1,0:T(8,128)(2,1)S(1)}, bf16[512,3200]{1,0:T(8,128)(2,1)}, u32[]{:S(2)}, u32[]{:S(2)}) collective-permute-start(bf16[512,3200]{1,0:T(8,128)(2,1)S(1)} %reorder.1.refs_0_), channel_id=1, source_target_pairs={{0,1},{1,0},{2,3},{3,2},{4,5},{5,4},{6,7},{7,6},{8,9},{9,8},{10,11... | collective-permute-start | bytes 9830408 | tf_op jit(solution)/shard_map/ppermute | solution.py:475
  12.1 31.9 %collective-permute-start.2 = (bf16[128,3200]{1,0:T(8,128)(2,1)}, bf16[128,3200]{1,0:T(8,128)(2,1)}, u32[]{:S(2)}, u32[]{:S(2)}) collective-permute-start(bf16[128,3200]{1,0:T(8,128)(2,1)} %get-tuple-element.424), channel_id=1, source_target_pairs={{0,2},{1,3},{2,0},{3,1},{4,6},{5,7},{6,4},{7,5},{8,10},{9,11},{10,... | collective-permute-start | bytes 2457608 | tf_op jit(solution)/shard_map/ppermute | solution.py:475
  15.5 28.6 %collective-permute-start.3 = (bf16[2,64,3200]{2,1,0:T(8,128)(2,1)}, bf16[2,64,3200]{2,1,0:T(8,128)(2,1)}, u32[]{:S(2)}, u32[]{:S(2)}) collective-permute-start(bf16[2,64,3200]{2,1,0:T(8,128)(2,1)} %get-tuple-element.427), channel_id=1, source_target_pairs={{0,8},{4,12},{8,0},{12,4},{16,24},{20,28},{24,16},{28,20},{1,9},{5... | collective-permute-start | bytes 2457608 | tf_op jit(solution)/shard_map/ppermute | solution.py:478
  18.1 25.9 %collective-permute-start.1 = (bf16[64,3200]{1,0:T(8,128)(2,1)S(1)}, bf16[64,3200]{1,0:T(8,128)(2,1)}, u32[]{:S(2)}, u32[]{:S(2)}) collective-permute-start(bf16[64,3200]{1,0:T(8,128)(2,1)S(1)} %constant_dynamic-slice_fusion), channel_id=1, source_target_pairs={{0,2},{1,3},{2,0},{3,1},{4,6},{5,7},{6,4},{7,5},{8,10},{9,11},{10,... | collective-permute-start | bytes 1228808 | tf_op jit(solution)/shard_map/ppermute | solution.py:475
  19.9 24.1 %collective-permute-start = (s32[1]{0:T(128)}, s32[1]{0:T(128)}, u32[]{:S(2)}, u32[]{:S(2)}) collective-permute-start(s32[1]{0:T(128)} %bitcast.2), channel_id=1, source_target_pairs={{0,2},{1,3},{2,0},{3,1},{4,6},{5,7},{6,4},{7,5},{8,10},{9,11},{10,... | collective-permute-start | bytes 20 | tf_op jit(solution)/shard_map/ppermute | solution.py:475
  44.1 51.6 %collective-permute-start.5 = (bf16[256,3200]{1,0:T(8,128)(2,1)S(1)}, bf16[256,3200]{1,0:T(8,128)(2,1)S(1)}, u32[]{:S(2)}, u32[]{:S(2)}) collective-permute-start(bf16[256,3200]{1,0:T(8,128)(2,1)S(1)} %copy-done.16), channel_id=1, source_target_pairs={{0,2},{1,3},{2,0},{3,1},{4,6},{5,7},{6,4},{7,5},{8,10},{9,11},{10,... | collective-permute-start | bytes 4915208 | tf_op jit(solution)/shard_map/ppermute | solution.py:475
  44.7 2.5 collective-permute-start.7
  44.7 51.0 %collective-permute-start.6 = (bf16[2,64,3200]{2,1,0:T(8,128)(2,1)S(1)}, bf16[2,64,3200]{2,1,0:T(8,128)(2,1)S(1)}, u32[]{:S(2)}, u32[]{:S(2)}) collective-permute-start(bf16[2,64,3200]{2,1,0:T(8,128)(2,1)S(1)} %copy-done.19), channel_id=1, source_target_pairs={{0,16},{4,20},{8,24},{12,28},{16,0},{20,4},{24,8},{28,12},{1,17},{... | collective-permute-start | bytes 2457608 | tf_op jit(solution)/shard_map/ppermute | solution.py:478
  95.6 5.1 %collective-permute-start.9 = (bf16[256,3200]{1,0:T(8,128)(2,1)S(1)}, bf16[256,3200]{1,0:T(8,128)(2,1)S(1)}, u32[]{:S(2)}, u32[]{:S(2)}) collective-permute-start(bf16[256,3200]{1,0:T(8,128)(2,1)S(1)} %collective-permute-done.5.refs_0_), channel_id=1, source_target_pairs={{0,1},{1,0},{2,3},{3,2},{4,5},{5,4},{6,7},{7,6},{8,9},{9,8},{10,11... | collective-permute-start | bytes 4915208 | tf_op jit(solution)/shard_map/ppermute | solution.py:475
  95.7 63.0 %collective-permute-start.14 = (bf16[512,3200]{1,0:T(8,128)(2,1)}, bf16[512,3200]{1,0:T(8,128)(2,1)}, u32[]{:S(2)}, u32[]{:S(2)}) collective-permute-start(bf16[512,3200]{1,0:T(8,128)(2,1)} %refs_8_.1), channel_id=1, source_target_pairs={{0,1},{1,0},{2,3},{3,2},{4,5},{5,4},{6,7},{7,6},{8,9},{9,8},{10,11... | collective-permute-start | bytes 9830408 | tf_op jit(solution)/shard_map/ppermute | solution.py:475
  96.2 20.4 %collective-permute-start.8 = (bf16[128,3200]{1,0:T(8,128)(2,1)}, bf16[128,3200]{1,0:T(8,128)(2,1)S(1)}, u32[]{:S(2)}, u32[]{:S(2)}) collective-permute-start(bf16[128,3200]{1,0:T(8,128)(2,1)} %get-tuple-element.230), channel_id=1, source_target_pairs={{0,2},{1,3},{2,0},{3,1},{4,6},{5,7},{6,4},{7,5},{8,10},{9,11},{10,... | collective-permute-start | bytes 2457608 | tf_op jit(solution)/shard_map/ppermute | solution.py:475
  116.7 2.3 collective-permute-start.10
  129.3 10.8 %collective-permute-start.12 = (f32[4,2,512]{2,0,1:T(4,128)S(1)}, f32[4,2,512]{2,0,1:T(4,128)S(1)}, u32[]{:S(2)}, u32[]{:S(2)}) collective-permute-start(f32[4,2,512]{2,0,1:T(4,128)S(1)} %bitcast.38), channel_id=1, source_target_pairs={{0,2},{1,3},{2,0},{3,1},{4,6},{5,7},{6,4},{7,5},{8,10},{9,11},{10,... | collective-permute-start | bytes 49160 | tf_op jit(solution)/shard_map/ppermute | solution.py:475
  132.6 26.2 %collective-permute-start.15 = (bf16[1,64,3200]{2,1,0:T(8,128)(2,1)S(1)}, bf16[1,64,3200]{2,1,0:T(8,128)(2,1)S(1)}, u32[]{:S(2)}, u32[]{:S(2)}) collective-permute-start(bf16[1,64,3200]{2,1,0:T(8,128)(2,1)S(1)} %slice.83), channel_id=1, source_target_pairs={{0,24},{4,28},{8,16},{12,20},{16,8},{20,12},{24,0},{28,4},{1,25},{... | collective-permute-start | bytes 1228808 | tf_op jit(solution)/shard_map/ppermute | solution.py:478
  138.9 3.2 collective-permute-start.13
  139.1 2.9 collective-permute-start.11
  142.8 38.4 %copy-start.25 = (f32[3200]{0:T(1024)S(1)}, f32[3200]{0:T(1024)}, u32[]{:S(2)}) copy-start(f32[3200]{0:T(1024)} %param.20) | copy-start | bytes 38404
  158.8 45.5 %collective-permute-start.22 = (bf16[512,3200]{1,0:T(8,128)(2,1)}, bf16[512,3200]{1,0:T(8,128)(2,1)}, u32[]{:S(2)}, u32[]{:S(2)}) collective-permute-start(bf16[512,3200]{1,0:T(8,128)(2,1)} %all-gather.2.cloned.1.call-done.refs_10_), channel_id=1, source_target_pairs={{0,1},{1,0},{2,3},{3,2},{4,5},{5,4},{6,7},{7,6},{8,9},{9,8},{10,11... | collective-permute-start | bytes 9830408 | tf_op jit(solution)/shard_map/ppermute | solution.py:475
  158.9 6.1 %collective-permute-start.16 = (bf16[256,512]{1,0:T(8,128)(2,1)}, bf16[256,512]{1,0:T(8,128)(2,1)S(1)}, u32[]{:S(2)}, u32[]{:S(2)}) collective-permute-start(bf16[256,512]{1,0:T(8,128)(2,1)} %get-tuple-element.274), channel_id=1, source_target_pairs={{0,1},{1,0},{2,3},{3,2},{4,5},{5,4},{6,7},{7,6},{8,9},{9,8},{10,11... | collective-permute-start | bytes 786440 | tf_op jit(solution)/shard_map/ppermute | solution.py:475
  159.4 9.4 %collective-permute-start.17 = (bf16[256,512]{1,0:T(8,128)(2,1)}, bf16[256,512]{1,0:T(8,128)(2,1)S(1)}, u32[]{:S(2)}, u32[]{:S(2)}) collective-permute-start(bf16[256,512]{1,0:T(8,128)(2,1)} %get-tuple-element.275), channel_id=1, source_target_pairs={{0,2},{1,3},{2,0},{3,1},{4,6},{5,7},{6,4},{7,5},{8,10},{9,11},{10,... | collective-permute-start | bytes 786440 | tf_op jit(solution)/shard_map/ppermute | solution.py:475
  160.4 12.2 %collective-permute-start.18 = (bf16[256,512]{1,0:T(8,128)(2,1)}, bf16[256,512]{1,0:T(8,128)(2,1)S(1)}, u32[]{:S(2)}, u32[]{:S(2)}) collective-permute-start(bf16[256,512]{1,0:T(8,128)(2,1)} %get-tuple-element.276), channel_id=1, source_target_pairs={{0,3},{1,2},{2,1},{3,0},{4,7},{5,6},{6,5},{7,4},{8,11},{9,10},{10,... | collective-permute-start | bytes 786440 | tf_op jit(solution)/shard_map/ppermute | solution.py:475
  160.8 36.8 %collective-permute-start.23 = (bf16[1,64,3200]{2,1,0:T(8,128)(2,1)S(1)}, bf16[1,64,3200]{2,1,0:T(8,128)(2,1)S(1)}, u32[]{:S(2)}, u32[]{:S(2)}) collective-permute-start(bf16[1,64,3200]{2,1,0:T(8,128)(2,1)S(1)} %slice.84), channel_id=1, source_target_pairs={{0,24},{4,28},{8,16},{12,20},{16,8},{20,12},{24,0},{28,4},{1,25},{... | collective-permute-start | bytes 1228808 | tf_op jit(solution)/shard_map/ppermute | solution.py:478
  173.6 24.0 %collective-permute-start.19 = (bf16[64,2048]{1,0:T(8,128)(2,1)S(1)}, bf16[64,2048]{1,0:T(8,128)(2,1)S(1)}, u32[]{:S(2)}, u32[]{:S(2)}) collective-permute-start(bf16[64,2048]{1,0:T(8,128)(2,1)S(1)} %get-tuple-element.278), channel_id=1, source_target_pairs={{0,8},{4,12},{8,0},{12,4},{16,24},{20,28},{24,16},{28,20},{1,9},{5... | collective-permute-start | bytes 786440 | tf_op jit(solution)/shard_map/ppermute | solution.py:478
  176.9 20.8 %collective-permute-start.20 = (bf16[64,2048]{1,0:T(8,128)(2,1)S(1)}, bf16[64,2048]{1,0:T(8,128)(2,1)S(1)}, u32[]{:S(2)}, u32[]{:S(2)}) collective-permute-start(bf16[64,2048]{1,0:T(8,128)(2,1)S(1)} %get-tuple-element.279), channel_id=1, source_target_pairs={{0,16},{4,20},{8,24},{12,28},{16,0},{20,4},{24,8},{28,12},{1,17},{... | collective-permute-start | bytes 786440 | tf_op jit(solution)/shard_map/ppermute | solution.py:478
  179.5 24.7 %collective-permute-start.21 = (bf16[64,2048]{1,0:T(8,128)(2,1)S(1)}, bf16[64,2048]{1,0:T(8,128)(2,1)S(1)}, u32[]{:S(2)}, u32[]{:S(2)}) collective-permute-start(bf16[64,2048]{1,0:T(8,128)(2,1)S(1)} %get-tuple-element.280), channel_id=1, source_target_pairs={{0,24},{4,28},{8,16},{12,20},{16,8},{20,12},{24,0},{28,4},{1,25},{... | collective-permute-start | bytes 786440 | tf_op jit(solution)/shard_map/ppermute | solution.py:478
  181.2 24.9 %copy-start.1 = (bf16[2,64,3200]{2,1,0:T(8,128)(2,1)S(1)}, bf16[2,64,3200]{2,1,0:T(8,128)(2,1)}, u32[]{:S(2)}) copy-start(bf16[2,64,3200]{2,1,0:T(8,128)(2,1)} %get-tuple-element.289.refs_4_) | copy-start | bytes 2457604
  204.3 13.3 %collective-permute-start.24 = (bf16[256,512]{1,0:T(8,128)(2,1)}, bf16[256,512]{1,0:T(8,128)(2,1)S(1)}, u32[]{:S(2)}, u32[]{:S(2)}) collective-permute-start(bf16[256,512]{1,0:T(8,128)(2,1)} %get-tuple-element.300), channel_id=1, source_target_pairs={{0,1},{1,0},{2,3},{3,2},{4,5},{5,4},{6,7},{7,6},{8,9},{9,8},{10,11... | collective-permute-start | bytes 786440 | tf_op jit(solution)/shard_map/ppermute | solution.py:475
  204.3 13.3 %collective-permute-start.25 = (bf16[256,512]{1,0:T(8,128)(2,1)}, bf16[256,512]{1,0:T(8,128)(2,1)S(1)}, u32[]{:S(2)}, u32[]{:S(2)}) collective-permute-start(bf16[256,512]{1,0:T(8,128)(2,1)} %get-tuple-element.301), channel_id=1, source_target_pairs={{0,2},{1,3},{2,0},{3,1},{4,6},{5,7},{6,4},{7,5},{8,10},{9,11},{10,... | collective-permute-start | bytes 786440 | tf_op jit(solution)/shard_map/ppermute | solution.py:475
  205.3 13.1 %collective-permute-start.26 = (bf16[256,512]{1,0:T(8,128)(2,1)}, bf16[256,512]{1,0:T(8,128)(2,1)S(1)}, u32[]{:S(2)}, u32[]{:S(2)}) collective-permute-start(bf16[256,512]{1,0:T(8,128)(2,1)} %get-tuple-element.302), channel_id=1, source_target_pairs={{0,3},{1,2},{2,1},{3,0},{4,7},{5,6},{6,5},{7,4},{8,11},{9,10},{10,... | collective-permute-start | bytes 786440 | tf_op jit(solution)/shard_map/ppermute | solution.py:475
  218.4 5.1 %collective-permute-start.29 = (f32[3,256]{1,0:T(4,128)S(1)}, f32[3,256]{1,0:T(4,128)S(1)}, u32[]{:S(2)}, u32[]{:S(2)}) collective-permute-start(f32[3,256]{1,0:T(4,128)S(1)} %get-tuple-element.352.refs_0_), channel_id=1, source_target_pairs={{0,24},{4,28},{8,16},{12,20},{16,8},{20,12},{24,0},{28,4},{1,25},{... | collective-permute-start | bytes 9224 | tf_op jit(solution)/shard_map/ppermute | solution.py:478
  219.4 4.5 collective-permute-start.28
  219.4 4.5 collective-permute-start.27
  227.7 25.6 %collective-permute-start.30 = (bf16[256,1664]{1,0:T(8,128)(2,1)S(1)}, bf16[256,1664]{1,0:T(8,128)(2,1)S(1)}, u32[]{:S(2)}, u32[]{:S(2)}) collective-permute-start(bf16[256,1664]{1,0:T(8,128)(2,1)S(1)} %get-tuple-element.306), channel_id=1, source_target_pairs={{0,4},{4,0},{8,12},{12,8},{16,20},{20,16},{24,28},{28,24},{1,5},{5... | collective-permute-start | bytes 2555912 | tf_op jit(solution)/shard_map/ppermute | solution.py:481
  228.4 9.4 %collective-permute-start.31 = (bf16[64,2048]{1,0:T(8,128)(2,1)S(1)}, bf16[64,2048]{1,0:T(8,128)(2,1)S(1)}, u32[]{:S(2)}, u32[]{:S(2)}) collective-permute-start(bf16[64,2048]{1,0:T(8,128)(2,1)S(1)} %get-tuple-element.312), channel_id=1, source_target_pairs={{0,8},{4,12},{8,0},{12,4},{16,24},{20,28},{24,16},{28,20},{1,9},{5... | collective-permute-start | bytes 786440 | tf_op jit(solution)/shard_map/ppermute | solution.py:478
  229.6 19.0 %collective-permute-start.32 = (bf16[64,2048]{1,0:T(8,128)(2,1)S(1)}, bf16[64,2048]{1,0:T(8,128)(2,1)S(1)}, u32[]{:S(2)}, u32[]{:S(2)}) collective-permute-start(bf16[64,2048]{1,0:T(8,128)(2,1)S(1)} %get-tuple-element.313), channel_id=1, source_target_pairs={{0,16},{4,20},{8,24},{12,28},{16,0},{20,4},{24,8},{28,12},{1,17},{... | collective-permute-start | bytes 786440 | tf_op jit(solution)/shard_map/ppermute | solution.py:478
  230.6 22.7 %collective-permute-start.33 = (bf16[64,2048]{1,0:T(8,128)(2,1)S(1)}, bf16[64,2048]{1,0:T(8,128)(2,1)S(1)}, u32[]{:S(2)}, u32[]{:S(2)}) collective-permute-start(bf16[64,2048]{1,0:T(8,128)(2,1)S(1)} %get-tuple-element.314), channel_id=1, source_target_pairs={{0,24},{4,28},{8,16},{12,20},{16,8},{20,12},{24,0},{28,4},{1,25},{... | collective-permute-start | bytes 786440 | tf_op jit(solution)/shard_map/ppermute | solution.py:478
  264.7 3.6 collective-permute-start.36
  266.0 4.5 collective-permute-start.35
  266.0 4.5 collective-permute-start.34
  274.5 18.2 %collective-permute-start.37 = (bf16[256,1664]{1,0:T(8,128)(2,1)S(1)}, bf16[256,1664]{1,0:T(8,128)(2,1)S(1)}, u32[]{:S(2)}, u32[]{:S(2)}) collective-permute-start(bf16[256,1664]{1,0:T(8,128)(2,1)S(1)} %get-tuple-element.331), channel_id=1, source_target_pairs={{0,4},{4,0},{8,12},{12,8},{16,20},{20,16},{24,28},{28,24},{1,5},{5... | collective-permute-start | bytes 2555912 | tf_op jit(solution)/shard_map/ppermute | solution.py:481
  292.6 23.6 %copy-start.7 = (bf16[128,6144]{1,0:T(8,128)(2,1)}, bf16[128,6144]{1,0:T(8,128)(2,1)S(1)}, u32[]{:S(2)}) copy-start(bf16[128,6144]{1,0:T(8,128)(2,1)S(1)} %get-tuple-element.362.refs_0_) | copy-start | bytes 4718596
  292.6 36.6 %collective-permute-start.38 = (bf16[128,6144]{1,0:T(8,128)(2,1)}, bf16[128,6144]{1,0:T(8,128)(2,1)}, u32[]{:S(2)}, u32[]{:S(2)}) collective-permute-start(bf16[128,6144]{1,0:T(8,128)(2,1)} %get-tuple-element.351), channel_id=1, source_target_pairs={{0,4},{4,0},{8,12},{12,8},{16,20},{20,16},{24,28},{28,24},{1,5},{5... | collective-permute-start | bytes 4718600 | tf_op jit(solution)/shard_map/ppermute | solution.py:481
  298.4 27.3 %collective-permute-start.39 = (f32[4]{0:T(128)S(1)}, f32[4]{0:T(128)S(1)}, u32[]{:S(2)}, u32[]{:S(2)}) collective-permute-start(f32[4]{0:T(128)S(1)} %pad_maximum_fusion), channel_id=1, source_target_pairs={{0,4},{4,0},{8,12},{12,8},{16,20},{20,16},{24,28},{28,24},{1,5},{5... | collective-permute-start | bytes 56 | tf_op jit(solution)/shard_map/ppermute | solution.py:481
  317.3 50.7 %copy-start.6 = (bf16[128,6144]{1,0:T(8,128)(2,1)S(1)}, bf16[128,6144]{1,0:T(8,128)(2,1)}, u32[]{:S(2)}) copy-start(bf16[128,6144]{1,0:T(8,128)(2,1)} %get-tuple-element.373.refs_0_) | copy-start | bytes 4718596
  329.2 38.1 %collective-permute-start.40 = (bf16[128,6144]{1,0:T(8,128)(2,1)}, bf16[128,6144]{1,0:T(8,128)(2,1)S(1)}, u32[]{:S(2)}, u32[]{:S(2)}) collective-permute-start(bf16[128,6144]{1,0:T(8,128)(2,1)} %get-tuple-element.361), channel_id=1, source_target_pairs={{0,4},{4,0},{8,12},{12,8},{16,20},{20,16},{24,28},{28,24},{1,5},{5... | collective-permute-start | bytes 4718600 | tf_op jit(solution)/shard_map/ppermute | solution.py:481
  331.6 35.7 %copy-start.13 = (bf16[128,6144]{1,0:T(8,128)(2,1)S(1)}, bf16[128,6144]{1,0:T(8,128)(2,1)}, u32[]{:S(2)}) copy-start(bf16[128,6144]{1,0:T(8,128)(2,1)} %copy-done.12) | copy-start | bytes 4718596
  331.6 40.8 %copy-start.23 = (f32[6144]{0:T(1024)S(1)}, f32[6144]{0:T(1024)}, u32[]{:S(2)}) copy-start(f32[6144]{0:T(1024)} %param.26) | copy-start | bytes 73732
  334.2 68.2 %copy-start.31 = (bf16[128,6144]{1,0:T(8,128)(2,1)S(1)}, bf16[128,6144]{1,0:T(8,128)(2,1)}, u32[]{:S(2)}) copy-start(bf16[128,6144]{1,0:T(8,128)(2,1)} %get-tuple-element.385) | copy-start | bytes 4718596
  334.2 13.9 %collective-permute-start.41 = (bf16[32,6144]{1,0:T(8,128)(2,1)S(1)}, bf16[32,6144]{1,0:T(8,128)(2,1)S(1)}, u32[]{:S(2)}, u32[]{:S(2)}) collective-permute-start(bf16[32,6144]{1,0:T(8,128)(2,1)S(1)} %get-tuple-element.365), channel_id=1, source_target_pairs={{0,8},{4,12},{8,0},{12,4},{16,24},{20,28},{24,16},{28,20},{1,9},{5... | collective-permute-start | bytes 1179656 | tf_op jit(solution)/shard_map/ppermute | solution.py:478
  336.0 25.4 %collective-permute-start.42 = (bf16[32,6144]{1,0:T(8,128)(2,1)S(1)}, bf16[32,6144]{1,0:T(8,128)(2,1)S(1)}, u32[]{:S(2)}, u32[]{:S(2)}) collective-permute-start(bf16[32,6144]{1,0:T(8,128)(2,1)S(1)} %get-tuple-element.366), channel_id=1, source_target_pairs={{0,16},{4,20},{8,24},{12,28},{16,0},{20,4},{24,8},{28,12},{1,17},{... | collective-permute-start | bytes 1179656 | tf_op jit(solution)/shard_map/ppermute | solution.py:478
  336.9 30.4 %collective-permute-start.43 = (bf16[32,6144]{1,0:T(8,128)(2,1)S(1)}, bf16[32,6144]{1,0:T(8,128)(2,1)S(1)}, u32[]{:S(2)}, u32[]{:S(2)}) collective-permute-start(bf16[32,6144]{1,0:T(8,128)(2,1)S(1)} %get-tuple-element.367), channel_id=1, source_target_pairs={{0,24},{4,28},{8,16},{12,20},{16,8},{20,12},{24,0},{28,4},{1,25},{... | collective-permute-start | bytes 1179656 | tf_op jit(solution)/shard_map/ppermute | solution.py:478
  367.3 35.1 %collective-permute-start.44 = (bf16[128,6144]{1,0:T(8,128)(2,1)S(1)}, bf16[128,6144]{1,0:T(8,128)(2,1)S(1)}, u32[]{:S(2)}, u32[]{:S(2)}) collective-permute-start(bf16[128,6144]{1,0:T(8,128)(2,1)S(1)} %copy-done.13), channel_id=1, source_target_pairs={{0,4},{4,0},{8,12},{12,8},{16,20},{20,16},{24,28},{28,24},{1,5},{5... | collective-permute-start | bytes 4718600 | tf_op jit(solution)/shard_map/ppermute | solution.py:481
  368.8 12.3 %collective-permute-start.45 = (bf16[32,6144]{1,0:T(8,128)(2,1)S(1)}, bf16[32,6144]{1,0:T(8,128)(2,1)S(1)}, u32[]{:S(2)}, u32[]{:S(2)}) collective-permute-start(bf16[32,6144]{1,0:T(8,128)(2,1)S(1)} %get-tuple-element.376), channel_id=1, source_target_pairs={{0,8},{4,12},{8,0},{12,4},{16,24},{20,28},{24,16},{28,20},{1,9},{5... | collective-permute-start | bytes 1179656 | tf_op jit(solution)/shard_map/ppermute | solution.py:478
  368.9 27.3 %collective-permute-start.46 = (bf16[32,6144]{1,0:T(8,128)(2,1)S(1)}, bf16[32,6144]{1,0:T(8,128)(2,1)S(1)}, u32[]{:S(2)}, u32[]{:S(2)}) collective-permute-start(bf16[32,6144]{1,0:T(8,128)(2,1)S(1)} %get-tuple-element.377), channel_id=1, source_target_pairs={{0,16},{4,20},{8,24},{12,28},{16,0},{20,4},{24,8},{28,12},{1,17},{... | collective-permute-start | bytes 1179656 | tf_op jit(solution)/shard_map/ppermute | solution.py:478
  371.1 68.0 %copy-start.5 = (bf16[128,6144]{1,0:T(8,128)(2,1)S(1)}, bf16[128,6144]{1,0:T(8,128)(2,1)}, u32[]{:S(2)}) copy-start(bf16[128,6144]{1,0:T(8,128)(2,1)} %get-tuple-element.398.refs_0_) | copy-start | bytes 4718596
  371.1 31.3 %collective-permute-start.47 = (bf16[32,6144]{1,0:T(8,128)(2,1)S(1)}, bf16[32,6144]{1,0:T(8,128)(2,1)S(1)}, u32[]{:S(2)}, u32[]{:S(2)}) collective-permute-start(bf16[32,6144]{1,0:T(8,128)(2,1)S(1)} %get-tuple-element.378), channel_id=1, source_target_pairs={{0,24},{4,28},{8,16},{12,20},{16,8},{20,12},{24,0},{28,4},{1,25},{... | collective-permute-start | bytes 1179656 | tf_op jit(solution)/shard_map/ppermute | solution.py:478
  402.4 36.7 %collective-permute-start.48 = (bf16[128,6144]{1,0:T(8,128)(2,1)S(1)}, bf16[128,6144]{1,0:T(8,128)(2,1)S(1)}, u32[]{:S(2)}, u32[]{:S(2)}) collective-permute-start(bf16[128,6144]{1,0:T(8,128)(2,1)S(1)} %copy-done.31), channel_id=1, source_target_pairs={{0,4},{4,0},{8,12},{12,8},{16,20},{20,16},{24,28},{28,24},{1,5},{5... | collective-permute-start | bytes 4718600 | tf_op jit(solution)/shard_map/ppermute | solution.py:481
  404.7 13.2 %collective-permute-start.49 = (bf16[32,6144]{1,0:T(8,128)(2,1)S(1)}, bf16[32,6144]{1,0:T(8,128)(2,1)S(1)}, u32[]{:S(2)}, u32[]{:S(2)}) collective-permute-start(bf16[32,6144]{1,0:T(8,128)(2,1)S(1)} %get-tuple-element.389), channel_id=1, source_target_pairs={{0,8},{4,12},{8,0},{12,4},{16,24},{20,28},{24,16},{28,20},{1,9},{5... | collective-permute-start | bytes 1179656 | tf_op jit(solution)/shard_map/ppermute | solution.py:478
  404.8 27.2 %collective-permute-start.50 = (bf16[32,6144]{1,0:T(8,128)(2,1)S(1)}, bf16[32,6144]{1,0:T(8,128)(2,1)S(1)}, u32[]{:S(2)}, u32[]{:S(2)}) collective-permute-start(bf16[32,6144]{1,0:T(8,128)(2,1)S(1)} %get-tuple-element.390), channel_id=1, source_target_pairs={{0,16},{4,20},{8,24},{12,28},{16,0},{20,4},{24,8},{28,12},{1,17},{... | collective-permute-start | bytes 1179656 | tf_op jit(solution)/shard_map/ppermute | solution.py:478
  406.2 32.9 %collective-permute-start.51 = (bf16[32,6144]{1,0:T(8,128)(2,1)S(1)}, bf16[32,6144]{1,0:T(8,128)(2,1)S(1)}, u32[]{:S(2)}, u32[]{:S(2)}) collective-permute-start(bf16[32,6144]{1,0:T(8,128)(2,1)S(1)} %get-tuple-element.391), channel_id=1, source_target_pairs={{0,24},{4,28},{8,16},{12,20},{16,8},{20,12},{24,0},{28,4},{1,25},{... | collective-permute-start | bytes 1179656 | tf_op jit(solution)/shard_map/ppermute | solution.py:478
  440.1 12.6 %collective-permute-start.52 = (bf16[32,6144]{1,0:T(8,128)(2,1)S(1)}, bf16[32,6144]{1,0:T(8,128)(2,1)S(1)}, u32[]{:S(2)}, u32[]{:S(2)}) collective-permute-start(bf16[32,6144]{1,0:T(8,128)(2,1)S(1)} %get-tuple-element.401), channel_id=1, source_target_pairs={{0,8},{4,12},{8,0},{12,4},{16,24},{20,28},{24,16},{28,20},{1,9},{5... | collective-permute-start | bytes 1179656 | tf_op jit(solution)/shard_map/ppermute | solution.py:478
  440.2 27.4 %collective-permute-start.53 = (bf16[32,6144]{1,0:T(8,128)(2,1)S(1)}, bf16[32,6144]{1,0:T(8,128)(2,1)S(1)}, u32[]{:S(2)}, u32[]{:S(2)}) collective-permute-start(bf16[32,6144]{1,0:T(8,128)(2,1)S(1)} %get-tuple-element.402), channel_id=1, source_target_pairs={{0,16},{4,20},{8,24},{12,28},{16,0},{20,4},{24,8},{28,12},{1,17},{... | collective-permute-start | bytes 1179656 | tf_op jit(solution)/shard_map/ppermute | solution.py:478
  441.2 33.6 %collective-permute-start.54 = (bf16[32,6144]{1,0:T(8,128)(2,1)S(1)}, bf16[32,6144]{1,0:T(8,128)(2,1)S(1)}, u32[]{:S(2)}, u32[]{:S(2)}) collective-permute-start(bf16[32,6144]{1,0:T(8,128)(2,1)S(1)} %get-tuple-element.403), channel_id=1, source_target_pairs={{0,24},{4,28},{8,16},{12,20},{16,8},{20,12},{24,0},{28,4},{1,25},{... | collective-permute-start | bytes 1179656 | tf_op jit(solution)/shard_map/ppermute | solution.py:478
  (25 other events, 233.6 us)
Sparse Core Ops, SparseCore 0:
  44.2 80.1 all-gather.1

commit v3 on v2

--- a/solution.py
+++ b/solution.py
@@ -120,10 +120,12 @@
 def attend_kernel(plan, rows, first, chunk, group, *refs):
     count = len(plan)
     blocks = plan[-1][0] + 1
-    seg_ref, sq_ref, gain_ref = refs[:3]
-    p_refs = refs[3 : 3 + count]
-    out_refs = refs[3 + count : 3 + count + blocks]
-    q_scale, k_scale, q_all, k_all, v_all = refs[3 + count + blocks :]
+    groups = blocks // group
+    seg_refs, refs = refs[:groups], refs[groups:]
+    sq_ref, gain_ref = refs[:2]
+    p_refs = refs[2 : 2 + count]
+    out_refs = refs[2 + count : 2 + count + blocks]
+    q_scale, k_scale, q_all, k_all, v_all = refs[2 + count + blocks :]
     head = pl.program_id(0)
     factor = HEAD_DIM ** (-0.5) * math.log2(math.e)
 
@@ -148,7 +150,6 @@
             q = p_ref[low - start : high - start, :HEAD_DIM]
             q_all[part, :] = (q * q_scale[part, :] * gain_ref[0:1, :]).astype(BF16)
 
-    groups = blocks // group
     keys = group * rows
     step = min(chunk, 128)
 
@@ -163,7 +164,7 @@
             for g in range(groups):
                 part = scores[:, g * keys : (g + 1) * keys]
                 if g != own:
-                    part = jnp.where(seg_ref[g] == seg_ref[own], part, -1e30)
+                    part = jnp.where(seg_refs[g][0] == seg_refs[own][0], part, -1e30)
                 masked.append(part)
             scores = jnp.concatenate(masked, axis=1)
         peak = jnp.max(scores, axis=-1, keepdims=True)
@@ -181,7 +182,7 @@
         for d in range(blocks):
             attend_all(d, 0, blocks * rows)
     else:
-        joint = seg_ref[0] == seg_ref[1]
+        joint = seg_refs[0][0] == seg_refs[1][0]
 
         @pl.when(joint)
         def _():
@@ -204,8 +205,8 @@
     return pl.pallas_call(
         functools.partial(attend_kernel, plan, rows, first, chunk, group),
         grid=(heads,),
-        in_specs=[
-            pl.BlockSpec(memory_space=pltpu.SMEM),
+        in_specs=[pl.BlockSpec(memory_space=pltpu.SMEM)] * len(segments)
+        + [
             pl.BlockSpec((2, total), lambda h: (0, 0)),
             pl.BlockSpec((2, HEAD_DIM), lambda h: (0, h)),
         ]
@@ -222,7 +223,7 @@
         cost_estimate=TINY,
         compiler_params=pltpu.CompilerParams(vmem_limit_bytes=56 * MIB),
         name="attend",
-    )(segments, squares, qk_gain, *pieces)
+    )(*segments, squares, qk_gain, *pieces)
 
 
 def pack_kernel(sub_ref, *refs):
@@ -248,7 +249,8 @@
     )(sub.reshape(1), *groups)
 
 
-def hidden_kernel(count, mask_ref, *refs):
+def hidden_kernel(sizes, strip_ref, mask_ref, *refs):
+    count = sum(sizes)
     mine_refs, stream_refs = refs[:SUBS], refs[SUBS : 2 * SUBS]
     w_refs = refs[2 * SUBS : 2 * SUBS + count]
     scale_ref, hidden_ref, stats_ref, mine, mean_wide, spread_wide = refs[2 * SUBS + count :]
@@ -258,14 +260,25 @@
 
     @pl.when(n == 0)
     def _():
-        for d in range(SUBS):
-            mine[d * rows : (d + 1) * rows, :] = mine_refs[d][...]
-
-    attn = jnp.dot(mine[:, :depth], w_refs[0][...], preferred_element_type=F32)
-    for i in range(1, count):
-        attn += jnp.dot(
-            mine[:, i * depth : (i + 1) * depth], w_refs[i][...], preferred_element_type=F32
+        for i, size in enumerate(sizes):
+            width = depth // size
+            for k in range(size):
+                start = i * depth + (strip_ref[0] ^ k) * width if size > 1 else i * depth
+                columns = pl.ds(pl.multiple_of(start, width), width)
+                low = i * depth + k * width
+                for d in range(SUBS):
+                    part = slice(d * rows, (d + 1) * rows)
+                    mine[part, low : low + width] = mine_refs[d][:, columns]
+
+    attn = None
+    for i, size in enumerate(sizes):
+        first = sum(sizes[:i])
+        weight = [ref[...] for ref in w_refs[first : first + size]]
+        weight = jnp.concatenate(weight, axis=0) if size > 1 else weight[0]
+        product = jnp.dot(
+            mine[:, i * depth : (i + 1) * depth], weight, preferred_element_type=F32
         )
+        attn = product if attn is None else attn + product
     columns = pl.ds(pl.multiple_of(n * block, block), block)
     for d in range(SUBS):
         part = slice(d * rows, (d + 1) * rows)
@@ -287,17 +300,19 @@
         stats_ref[2:3, :] = jnp.full((1, SUBS * rows), mask_ref[0].astype(F32))
 
 
-def hidden_of(places, mine, residual, weights, layer_scale, mask):
+def hidden_of(places, mine, residual, weights, strip, layer_scale, mask):
     rows = mine[0].shape[0]
-    count, depth, block = len(weights), weights[0].shape[0], 640
+    count, depth, block = len(weights), weights[0][0].shape[0], 640
+    sizes = [len(strips) for strips in weights]
+    weights = [part for strips in weights for part in strips]
     total = SUBS * rows
     return pl.pallas_call(
-        functools.partial(hidden_kernel, count),
+        functools.partial(hidden_kernel, sizes),
         grid=(D // block,),
-        in_specs=[pl.BlockSpec(memory_space=pltpu.SMEM)]
+        in_specs=[pl.BlockSpec(memory_space=pltpu.SMEM)] * 2
         + [pl.BlockSpec(mine[0].shape, lambda n: (0, 0))] * SUBS
         + [pl.BlockSpec((1, rows, block), lambda n, j=j: (j, 0, n)) for j in places]
-        + [pl.BlockSpec((depth, block), lambda n: (0, n))] * count
+        + [pl.BlockSpec((part.shape[0], block), lambda n: (0, n)) for part in weights]
         + [pl.BlockSpec((1, block), lambda n: (0, n))],
         out_specs=[
             pl.BlockSpec((total, D), lambda n: (0, 0)),
@@ -319,7 +334,7 @@
         ),
         compiler_params=pltpu.CompilerParams(vmem_limit_bytes=48 * MIB),
         name="hidden",
-    )(mask, *mine, *residual, *weights, layer_scale.reshape(1, D))
+    )(strip, mask, *mine, *residual, *weights, layer_scale.reshape(1, D))
 
 
 def norm_kernel(parts, part_ref, hidden_ref, *refs):
@@ -394,7 +409,7 @@
     parts = len(slab)
     total = slab[0].shape[0]
     width, hid = fc_weight.shape
-    block = 768
+    block = 1536
     size = total // HALVES
     outs = pl.pallas_call(
         functools.partial(shares_kernel, parts),
@@ -491,46 +506,53 @@
     by_sub = tokens.reshape(CHUNKS, SUBS, merged, D)
     residual = {0: pick(by_sub, sub, 1)}
     to_send = {d: pick(by_sub, sub ^ d, 1) for d in range(1, SUBS)}
-    share = out_weight.shape[0] // n_rows
-    strip = lax.dynamic_slice_in_dim(out_weight, row * share, share, 0)
+    depth = out_weight.shape[0]
+    across = max(1, min(2, depth // 256, parts))
+    strip = lax.bitwise_and(part, across - 1) * 2 + lax.bitwise_and(sub, 1)
+    size = depth // (2 * across)
+    own_strip = lax.dynamic_slice_in_dim(out_weight, strip * size, size, 0)
     group = max(1, min(n_seq, TILE // rows_here))
     projected, squares = {}, {}
 
     own_id = segment_ids[0, :1]
     leads = [own_id] + [over_seq(own_id, d) for d in range(group, n_seq, group)]
-    strips = {d: over_seq(strip, d) for d in range(2, n_seq, 2)}
+    strips = {(d, 0): over_seq(own_strip, d) for d in range(2, n_seq, 2)}
     far = {d: over_seq(cut[0], d) for d in range(2, n_seq, 2)}
     near = over_seq(tokens, 1)
     residual[1] = over_sub(to_send[1], 1)
+    residual[2] = over_sub(to_send[2][:1], 2)
     given, given_s = project([tokens, near], norm_gain, qkv_weight)
     for d in range(2):
         projected[d, 0], squares[d, 0] = given[d], given_s[d]
     state = leads, strips, far, residual, to_send, cut, squares, out_weight
     leads, strips, far, residual, to_send, cut, squares, out_weight = fence(state)
-    leads = jnp.concatenate(leads)
-
-    out_blocks = {0: out_weight}
-    for d in range(2, n_seq, 2):
-        out_blocks[d] = lax.all_gather(strips[d], "rows", axis=0, tiled=True)
+
     for i in range(len(cut)):
         coming = {}
         if i + 1 < len(cut):
             coming = {d: over_seq(cut[i + 1], d) for d in range(2, n_seq, 2)}
+        arrived = dict(strips)
+        for d, k in [key for key in arrived if key[0] % 2 == 0]:
+            if k == 0 and i == 0:
+                strips[d, 1] = over_sub(arrived[d, 0], 1)
+            if k == i and across == 2:
+                strips[d, 2 + k] = over_part(arrived[d, k], 1)
+            if (d + 1, k) not in strips:
+                strips[d + 1, k] = over_seq(arrived[d, k], 1)
         if i == 0:
-            residual[2] = over_sub(to_send[2], 2)
+            residual[3] = over_sub(to_send[3][:1], 3)
         if i == 1:
-            residual[3] = over_sub(to_send[3][:1], 3)
-            out_blocks[1] = over_seq(out_weight, 1)
+            last = {2: over_sub(to_send[2][1:], 2)}
+            out_near = over_seq(out_weight, 1)
         for d in range(2, n_seq, 2):
             far[d + 1] = over_seq(far[d], 1)
         given, given_s = project([far[d] for d in range(2, n_seq)], norm_gain, qkv_weight)
         for d in range(2, n_seq):
             projected[d, i], squares[d, i] = given[d - 2], given_s[d - 2]
         if i + 1 < len(cut):
-            held = {d: residual[d] for d in range(3)}
-            state = coming, held, to_send, cut, squares, out_weight
-            far, held, to_send, cut, squares, out_weight = fence(state)
-            residual.update(held)
+            held = last if i == 1 else {}
+            state = coming, residual, to_send, cut, squares, out_weight, strips, held
+            far, residual, to_send, cut, squares, out_weight, strips, last = fence(state)
     plan, pieces = [], []
     for d, i in sorted(projected):
         plan.append((d, cuts[i], projected[d, i].shape[0]))
@@ -549,19 +571,22 @@
     place = jnp.stack([sub, part])
     relative = np.array([d * parts + e for e in range(parts) for d in range(SUBS)], np.int32)
 
+    places = [(0, 0, 0, 0), (1, 1, 0, 0)]
+
     def heads_of(j, sums):
         return attend(pieces, plan, rows_here, sums, leads, qk_gain, j * chunk, chunk)
 
     def gather_heads(heads):
         return [heads[0]] + [over_seq(heads[d], d) for d in range(1, n_seq)]
 
-    def gather_rows(groups):
-        packed = pack(groups, sub)
+    def gather_rows(packed):
         return [packed[0]] + [over_sub(packed[d], d) for d in range(1, SUBS)]
 
     def to_hidden(j, mine):
         own = pad_mask[0, :1]
-        return hidden_of(places[j], mine, residual, out_weights, layer_scale, own)
+        return hidden_of(
+            places[j], mine, residual, out_weights, strip.reshape(1), layer_scale, own
+        )
 
     def to_normed(hidden, stats):
         known = [stats] + [over_sub(stats, e) for e in range(1, SUBS)]
@@ -574,29 +599,33 @@
         pre = sum(term.astype(F32) for term in terms)
         return (jax.nn.gelu(pre + fc_bias, approximate=False) * own_mask).astype(BF16)
 
+    total, to_send, last, strips = fence((total, to_send, last, strips))
+
+    last[3] = over_sub(to_send[3][1:], 3)
     heads_0 = heads_of(0, total)
-    heads_0, total, out_blocks, residual = fence((heads_0, total, out_blocks, residual))
-    places = [(0, 0, 0, 0), (1, 1, 1, 0)]
+    heads_0, total, last = fence((heads_0, total, last))
+
+    heads_1 = heads_of(1, total)
+    groups_0 = gather_heads(heads_0)
+    heads_1, groups_0 = fence((heads_1, groups_0))
+
+    rows_0 = gather_rows(pack(groups_0, sub))
+    packed_1 = pack(gather_heads(heads_1), sub)
+    rows_0, packed_1 = fence((rows_0, packed_1))
+
+    out_weights = [[out_weight], [out_near]]
+    for d in range(2, n_seq):
+        out_weights.append([strips[d, k] for k in range(2 * across)])
     residual = [residual[d] for d in range(SUBS)]
-
-    for d in range(2, n_seq, 2):
-        out_blocks[d + 1] = over_seq(out_blocks[d], 1)
-    last = over_sub(to_send[3][1:], 3)
-    heads_1 = heads_of(1, total)
-    rows_0 = gather_rows(gather_heads(heads_0))
-    heads_1, rows_0, out_blocks, last = fence((heads_1, rows_0, out_blocks, last))
-    out_weights = [out_blocks[d] for d in range(n_seq)]
-
+    rows_1 = gather_rows(packed_1)
     hidden_0 = to_hidden(0, rows_0)
-    groups_1 = gather_heads(heads_1)
-    hidden_0, groups_1 = fence((hidden_0, groups_1))
-
-    rows_1 = gather_rows(groups_1)
+    hidden_0, rows_1 = fence((hidden_0, rows_1))
+
     normed_0, known = to_normed(*hidden_0)
+    normed_0, known, rows_1 = fence((normed_0, known, rows_1))
+
     slab_0 = over_parts(normed_0)
-    slab_0, known, rows_1 = fence((slab_0, known, rows_1))
-
-    residual = [*residual[:3], last]
+    residual = [*residual[:2], last[2], last[3]]
     normed_1, _ = to_normed(*to_hidden(1, rows_1))
     slab_0, known, normed_1 = fence((slab_0, known, normed_1))
 
@@ -613,8 +642,11 @@
             waiting = waiting[1:]
         if tick == 0:
             waiting = waiting + shares_of(slab_1, place, owner, fc_weight)
+        if tick == 1:
             line = jnp.stack([stats[2, 0] for stats in known])
-            masks = jnp.concatenate(over_parts([line] * parts))
+            own_mask = over_parts([line] * parts)
+        if tick == 2:
+            masks = jnp.concatenate(own_mask)
             given = (row ^ relative)[:, None] == jnp.arange(n_rows, dtype=jnp.int32)[None, :]
             given = given & (owner[None, :] == row)
             own_mask = jnp.sum(jnp.where(given, masks[:, None], 0.0))
@@ -623,8 +655,8 @@
             new_by_sub = [[summed[0]] + [over_sub(summed[d], d) for d in range(1, SUBS)]]
         if by_sub:
             outs = outs + [finish(by_sub[0], own_mask)]
-        state = waiting, new_by_part, new_by_sub, outs, own_mask
-        waiting, by_part, by_sub, outs, own_mask = fence(state)
+        state = waiting, new_by_part, new_by_sub, outs, own_mask, known
+        waiting, by_part, by_sub, outs, own_mask, known = fence(state)
     return jnp.concatenate(outs, axis=0)[None]
 
 

time: 495 us -> 462 us (0.933)
  the two profiles are of different devices: /device:TPU:16 before, /device:TPU:8 now
where the time goes in v3:
time: 462 us; the launch traced here: 453 us
  waiting for transfers between devices  200 us (43%)
  Pallas kernels  136 us (29%)
  starting transfers between devices  71.7 us (16%)
  local copies, waits for them, and re-layouts  30.4 us (7%)
  other arithmetic  14.4 us (3%)
    ppermute x30, waiting for transfers between devices, over_sub(): lax.ppermute(value, 'rows', [(i, i ^ d * parts) for i in range(n_rows)])  131 us
    pallas_call x4, Pallas kernels, project(): pl.pallas_call(functools.partial(qkv_kernel, count), grid=(width // block...  47.9 us
    ppermute x30, starting transfers between devices, over_sub(): lax.ppermute(value, 'rows', [(i, i ^ d * parts) for i in range(n_rows)])  46.2 us
    ppermute x9, waiting for transfers between devices, over_part(): return lax.ppermute(value, 'rows', [(i, i ^ d) for i in range(n_rows)])  42.5 us
    pallas_call x2, Pallas kernels, shares_of(): pl.pallas_call(functools.partial(shares_kernel, parts), grid=(hid // bloc...  31.5 us
    ppermute x23, waiting for transfers between devices, over_seq(): return lax.ppermute(value, 'seq', [(i, i ^ d) for i in range(n_seq)])  26.8 us
    pallas_call x2, Pallas kernels, attend(): pl.pallas_call(functools.partial(attend_kernel, plan, rows, first, chunk,...  24.6 us
    pallas_call x2, Pallas kernels, hidden_of(): pl.pallas_call(functools.partial(hidden_kernel, sizes), grid=(D // block,...  22.3 us
  transfers between devices with their start and end apart: 62, of which 35 were waited for; matrix products, arithmetic and copies ran while one was open for 6% of the time, Pallas kernels for 29%

profile of v3, /device:TPU:8, one launch (start us, length us, event | category | flops | bytes accessed | tf_op | source)
XLA Modules:
  0.0 453.2 jit_solution(575905737025856100)
XLA Ops:
  0.0 1.9 copy-done.2
  4.2 2.0 dynamic-slice_bitcast_fusion
  7.4 1.9 collective-permute-start.1
  10.6 3.0 collective-permute-start.4
  18.3 20.4 %qkv.4 = (f32[512,1536]{1,0:T(8,128)}, f32[512,1536]{1,0:T(8,128)}, f32[2,512]{1,0:T(2,128)}, f32[2,512]{1,0:T(2,128)}) custom-call(bf16[512,3200]{1,0:T(8,128)(2,1)} %copy-done, bf16[512,3200]{1,0:T(8,128)(2,1)} %collective-permute-done.5.refs_1_, f32[1,3200]{1,0:T(1,128)} %reshape.49.refs_2_, bf16[3200,1536]{1,0:T(8,128)(2,1)} %refs_3_.9), custom_call_target="tpu_custom_call" | custom-call | flops 1 | bytes 1 | tf_op jit(solution)/shard_map/qkv/pallas_call | solution.py:96
  38.6 7.2 %collective-permute-done.refs_1_ = s32[1]{0:T(128)} collective-permute-done((s32[1]{0:T(128)}, s32[1]{0:T(128)}, u32[]{:S(2)}, u32[]{:S(2)}) %collective-permute-start) | collective-permute-done | bytes 36 | tf_op jit(solution)/shard_map/ppermute | solution.py:490
  45.9 1.7 collective-permute-start.6
  51.0 1.6 collective-permute-start.7
  52.7 7.7 %qkv.5 = (f32[128,1536]{1,0:T(8,128)}, f32[128,1536]{1,0:T(8,128)}, f32[2,128]{1,0:T(2,128)}, f32[2,128]{1,0:T(2,128)}) custom-call(bf16[128,3200]{1,0:T(8,128)(2,1)} %copy-done.34, bf16[128,3200]{1,0:T(8,128)(2,1)} %copy-done.35, f32[1,3200]{1,0:T(1,128)} %reshape.49.refs_2_, bf16[3200,1536]{1,0:T(8,128)(2,1)} %refs_3_.9), custom_call_target="tpu_custom_call" | custom-call | flops 1 | bytes 1 | tf_op jit(solution)/shard_map/qkv/pallas_call | solution.py:96
  60.4 2.1 collective-permute-done.7.refs_7_
  62.5 5.8 %collective-permute-done.10.refs_12_ = bf16[128,3200]{1,0:T(8,128)(2,1)S(1)} collective-permute-done((bf16[128,3200]{1,0:T(8,128)(2,1)S(1)}, bf16[128,3200]{1,0:T(8,128)(2,1)S(1)}, u32[]{:S(2)}, u32[]{:S(2)}) %collective-permute-start.10) | collective-permute-done | bytes 819232 | tf_op jit(solution)/shard_map/ppermute | solution.py:496
  68.3 2.2 collective-permute-done.9.refs_11_
  70.4 13.1 %collective-permute-done.6.refs_0_ = bf16[256,3200]{1,0:T(8,128)(2,1)} collective-permute-done((bf16[256,3200]{1,0:T(8,128)(2,1)}, bf16[256,3200]{1,0:T(8,128)(2,1)}, u32[]{:S(2)}, u32[]{:S(2)}) %collective-permute-start.6) | collective-permute-done | bytes 1638432 | tf_op jit(solution)/shard_map/ppermute | solution.py:490
  87.3 2.5 collective-permute-start.17
  89.9 11.9 %qkv.6 = (f32[256,1536]{1,0:T(8,128)}, f32[256,1536]{1,0:T(8,128)}, f32[2,256]{1,0:T(2,128)}, f32[2,256]{1,0:T(2,128)}) custom-call(bf16[256,3200]{1,0:T(8,128)(2,1)} %collective-permute-done.6.refs_0_, bf16[256,3200]{1,0:T(8,128)(2,1)} %collective-permute-done.13.refs_1_, f32[1,3200]{1,0:T(1,128)} %reshape.49.refs_2_, bf16[3200,1536]{1,0:T(8,128)(2,1)} %refs_3_.9), custom_call_target="tpu_custom_call" | custom-call | flops 1 | bytes 1 | tf_op jit(solution)/shard_map/qkv/pallas_call | solution.py:96
  101.8 5.9 %collective-permute-done.17.refs_6_ = bf16[1,64,3200]{2,1,0:T(8,128)(2,1)S(1)} collective-permute-done((bf16[1,64,3200]{2,1,0:T(8,128)(2,1)S(1)}, bf16[1,64,3200]{2,1,0:T(8,128)(2,1)S(1)}, u32[]{:S(2)}, u32[]{:S(2)}) %collective-permute-start.17) | collective-permute-done | bytes 409632 | tf_op jit(solution)/shard_map/ppermute | solution.py:493
  109.0 1.7 collective-permute-done.18.refs_1_
  111.7 7.9 %qkv.7 = (f32[128,1536]{1,0:T(8,128)}, f32[128,1536]{1,0:T(8,128)}, f32[2,128]{1,0:T(2,128)}, f32[2,128]{1,0:T(2,128)}) custom-call(bf16[128,3200]{1,0:T(8,128)(2,1)} %collective-permute-done.12.refs_0_, bf16[128,3200]{1,0:T(8,128)(2,1)} %copy-done.36, f32[1,3200]{1,0:T(1,128)} %reshape.49.refs_2_, bf16[3200,1536]{1,0:T(8,128)(2,1)} %refs_3_.9), custom_call_target="tpu_custom_call" | custom-call | flops 1 | bytes 1 | tf_op jit(solution)/shard_map/qkv/pallas_call | solution.py:96
  124.3 2.2 collective-permute-done.20
  128.5 12.1 %attend.2 = (bf16[256,512]{1,0:T(8,128)(2,1)}, bf16[256,512]{1,0:T(8,128)(2,1)}, bf16[256,512]{1,0:T(8,128)(2,1)}, bf16[256,512]{1,0:T(8,128)(2,1)}) custom-call(s32[1]{0:T(128)} %bitcast.4.refs_0_, s32[1]{0:T(128)} %collective-permute-done.refs_1_, f32[2,2048]{1,0:T(2,128)} %bitcast.32, f32[2,512]{1,0:T(2,128)} %refs_3_.11, ...), custom_call_target="tpu_custom_call" | custom-call | flops 1 | bytes 1 | tf_op jit(solution)/shard_map/attend/pallas_call | solution.py:205
  140.6 6.7 %collective-permute-done.23.refs_7_ = bf16[1,64,3200]{2,1,0:T(8,128)(2,1)S(1)} collective-permute-done((bf16[1,64,3200]{2,1,0:T(8,128)(2,1)S(1)}, bf16[1,64,3200]{2,1,0:T(8,128)(2,1)S(1)}, u32[]{:S(2)}, u32[]{:S(2)}) %collective-permute-start.23) | collective-permute-done | bytes 409632 | tf_op jit(solution)/shard_map/ppermute | solution.py:493
  149.9 12.5 %attend.3 = (bf16[256,512]{1,0:T(8,128)(2,1)}, bf16[256,512]{1,0:T(8,128)(2,1)}, bf16[256,512]{1,0:T(8,128)(2,1)}, bf16[256,512]{1,0:T(8,128)(2,1)}) custom-call(s32[1]{0:T(128)} %bitcast.4.refs_0_, s32[1]{0:T(128)} %collective-permute-done.refs_1_, f32[2,2048]{1,0:T(2,128)} %bitcast.33, f32[2,512]{1,0:T(2,128)} %refs_3_.11, ...), custom_call_target="tpu_custom_call" | custom-call | flops 1 | bytes 1 | tf_op jit(solution)/shard_map/attend/pallas_call | solution.py:205
  164.5 7.8 %collective-permute-start.27 = (bf16[64,2048]{1,0:T(8,128)(2,1)S(1)}, bf16[64,2048]{1,0:T(8,128)(2,1)S(1)}, u32[]{:S(2)}, u32[]{:S(2)}) collective-permute-start(bf16[64,2048]{1,0:T(8,128)(2,1)S(1)} %get-tuple-element.328), channel_id=1, source_target_pairs={{0,8},{4,12},{8,0},{12,4},{16,24},{20,28},{24,16},{28,20},{1,9},{5... | collective-permute-start | bytes 786440 | tf_op jit(solution)/shard_map/ppermute | solution.py:493
  177.4 2.3 collective-permute-done.27.refs_1_
  179.7 10.3 %collective-permute-done.28.refs_2_ = bf16[64,2048]{1,0:T(8,128)(2,1)S(1)} collective-permute-done((bf16[64,2048]{1,0:T(8,128)(2,1)S(1)}, bf16[64,2048]{1,0:T(8,128)(2,1)S(1)}, u32[]{:S(2)}, u32[]{:S(2)}) %collective-permute-start.28) | collective-permute-done | bytes 262176 | tf_op jit(solution)/shard_map/ppermute | solution.py:493
  190.0 7.5 %collective-permute-done.29.refs_3_ = bf16[64,2048]{1,0:T(8,128)(2,1)S(1)} collective-permute-done((bf16[64,2048]{1,0:T(8,128)(2,1)S(1)}, bf16[64,2048]{1,0:T(8,128)(2,1)S(1)}, u32[]{:S(2)}, u32[]{:S(2)}) %collective-permute-start.29) | collective-permute-done | bytes 262176 | tf_op jit(solution)/shard_map/ppermute | solution.py:493
  197.5 1.9 collective-permute-start.35
  201.0 11.1 %hidden.2 = (f32[256,3200]{1,0:T(8,128)}, f32[3,256]{1,0:T(4,128)}) custom-call(s32[1]{0:T(128)} %bitcast.1.strip_ref, s32[1]{0:T(128)} %bitcast.2.mask_ref, bf16[64,2048]{1,0:T(8,128)(2,1)S(1)} %get-tuple-element.339.refs_0_, bf16[64,2048]{1,0:T(8,128)(2,1)S(1)} %collective-permute-done.27.refs_1_, bf16[64,2048]{1,0:T(8,128)(2,1)S(1)} %collective-permute-done.28.refs_2_, ...), custom_call_target="tpu_custom_call" | custom-call | flops 3355443200 | bytes 18022400 | tf_op jit(solution)/shard_map/hidden/pallas_call | solution.py:309
  212.8 4.6 %collective-permute-done.35.refs_2_ = bf16[64,2048]{1,0:T(8,128)(2,1)S(1)} collective-permute-done((bf16[64,2048]{1,0:T(8,128)(2,1)S(1)}, bf16[64,2048]{1,0:T(8,128)(2,1)S(1)}, u32[]{:S(2)}, u32[]{:S(2)}) %collective-permute-start.35) | collective-permute-done | bytes 262176 | tf_op jit(solution)/shard_map/ppermute | solution.py:493
  218.1 5.5 %collective-permute-done.36.refs_3_ = bf16[64,2048]{1,0:T(8,128)(2,1)S(1)} collective-permute-done((bf16[64,2048]{1,0:T(8,128)(2,1)S(1)}, bf16[64,2048]{1,0:T(8,128)(2,1)S(1)}, u32[]{:S(2)}, u32[]{:S(2)}) %collective-permute-start.36) | collective-permute-done | bytes 262176 | tf_op jit(solution)/shard_map/ppermute | solution.py:493
  224.3 1.9 collective-permute-start.38
  230.1 1.9 copy-done.3
  232.0 2.7 norm.2
  234.9 11.2 %hidden.3 = (f32[256,3200]{1,0:T(8,128)}, f32[3,256]{1,0:T(4,128)S(1)}) custom-call(s32[1]{0:T(128)} %bitcast.1.strip_ref, s32[1]{0:T(128)} %bitcast.2.mask_ref, bf16[64,2048]{1,0:T(8,128)(2,1)S(1)} %get-tuple-element.376.refs_0_, bf16[64,2048]{1,0:T(8,128)(2,1)S(1)} %copy-done.20, bf16[64,2048]{1,0:T(8,128)(2,1)S(1)} %copy-done.22, ...), custom_call_target="tpu_custom_call" | custom-call | flops 3355443200 | bytes 18022400 | tf_op jit(solution)/shard_map/hidden/pallas_call | solution.py:309
  246.1 1.9 collective-permute-start.41
  249.7 2.8 collective-permute-done.42.refs_2_
  252.8 1.9 copy-done.4
  254.7 1.9 norm.3
  256.6 2.1 collective-permute-start.44
  258.7 15.8 %shares.2 = (bf16[128,6144]{1,0:T(8,128)(2,1)S(1)}, bf16[128,6144]{1,0:T(8,128)(2,1)S(1)}, bf16[128,6144]{1,0:T(8,128)(2,1)}, bf16[128,6144]{1,0:T(8,128)(2,1)}) custom-call(s32[2]{0:T(128)S(1)} %pad_add_fusion.place_ref, s32[8]{0:T(128)S(1)} %copy-done.26, bf16[256,1664]{1,0:T(8,128)(2,1)S(1)} %get-tuple-element.388.refs_0_, ...), custom_call_target="tpu_custom_call" | custom-call | flops 10066329600 | bytes 27590656 | tf_op jit(solution)/shard_map/shares/pallas_call | solution.py:414
  274.9 2.5 collective-permute-start.45
  277.4 15.8 %shares.3 = (bf16[128,6144]{1,0:T(8,128)(2,1)S(1)}, bf16[128,6144]{1,0:T(8,128)(2,1)S(1)}, bf16[128,6144]{1,0:T(8,128)(2,1)}, bf16[128,6144]{1,0:T(8,128)(2,1)}) custom-call(s32[2]{0:T(128)S(1)} %pad_add_fusion.place_ref, s32[8]{0:T(128)S(1)} %copy-done.26, bf16[256,1664]{1,0:T(8,128)(2,1)S(1)} %get-tuple-element.400.refs_0_, ...), custom_call_target="tpu_custom_call" | custom-call | flops 10066329600 | bytes 27590656 | tf_op jit(solution)/shard_map/shares/pallas_call | solution.py:414
  293.2 16.8 %collective-permute-done.45.refs_1_ = bf16[128,6144]{1,0:T(8,128)(2,1)S(1)} collective-permute-done((bf16[128,6144]{1,0:T(8,128)(2,1)S(1)}, bf16[128,6144]{1,0:T(8,128)(2,1)S(1)}, u32[]{:S(2)}, u32[]{:S(2)}) %collective-permute-start.45) | collective-permute-done | bytes 1572896 | tf_op jit(solution)/shard_map/ppermute | solution.py:496
  310.0 2.0 collective-permute-start.46
  312.8 3.2 collective-permute-start.47
  322.3 2.5 pad_maximum_fusion
  324.8 16.1 %collective-permute-done.50 = f32[4]{0:T(128)S(1)} collective-permute-done((f32[4]{0:T(128)S(1)}, f32[4]{0:T(128)S(1)}, u32[]{:S(2)}, u32[]{:S(2)}) %collective-permute-start.50) | collective-permute-done | bytes 48 | tf_op jit(solution)/shard_map/ppermute | solution.py:496
  340.9 1.8 collective-permute-done.49
  349.0 2.4 fusion.3
  351.4 5.1 %collective-permute-done.52 = bf16[32,6144]{1,0:T(8,128)(2,1)S(1)} collective-permute-done((bf16[32,6144]{1,0:T(8,128)(2,1)S(1)}, bf16[32,6144]{1,0:T(8,128)(2,1)S(1)}, u32[]{:S(2)}, u32[]{:S(2)}) %collective-permute-start.52) | collective-permute-done | bytes 393248 | tf_op jit(solution)/shard_map/ppermute | solution.py:493
  356.5 14.3 %collective-permute-done.53 = bf16[32,6144]{1,0:T(8,128)(2,1)S(1)} collective-permute-done((bf16[32,6144]{1,0:T(8,128)(2,1)S(1)}, bf16[32,6144]{1,0:T(8,128)(2,1)S(1)}, u32[]{:S(2)}, u32[]{:S(2)}) %collective-permute-start.53) | collective-permute-done | bytes 393248 | tf_op jit(solution)/shard_map/ppermute | solution.py:493
  370.9 6.6 %collective-permute-done.54 = bf16[32,6144]{1,0:T(8,128)(2,1)S(1)} collective-permute-done((bf16[32,6144]{1,0:T(8,128)(2,1)S(1)}, bf16[32,6144]{1,0:T(8,128)(2,1)S(1)}, u32[]{:S(2)}, u32[]{:S(2)}) %collective-permute-start.54) | collective-permute-done | bytes 393248 | tf_op jit(solution)/shard_map/ppermute | solution.py:493
  377.5 3.3 collective-permute-done.51.refs_1_
  382.2 3.8 collective-permute-start.56
  387.6 2.4 fusion.7
  390.0 7.2 %collective-permute-done.56 = bf16[32,6144]{1,0:T(8,128)(2,1)S(1)} collective-permute-done((bf16[32,6144]{1,0:T(8,128)(2,1)S(1)}, bf16[32,6144]{1,0:T(8,128)(2,1)S(1)}, u32[]{:S(2)}, u32[]{:S(2)}) %collective-permute-start.56) | collective-permute-done | bytes 393248 | tf_op jit(solution)/shard_map/ppermute | solution.py:493
  397.2 9.0 %collective-permute-done.57 = bf16[32,6144]{1,0:T(8,128)(2,1)S(1)} collective-permute-done((bf16[32,6144]{1,0:T(8,128)(2,1)S(1)}, bf16[32,6144]{1,0:T(8,128)(2,1)S(1)}, u32[]{:S(2)}, u32[]{:S(2)}) %collective-permute-start.57) | collective-permute-done | bytes 393248 | tf_op jit(solution)/shard_map/ppermute | solution.py:493
  406.2 7.2 %collective-permute-done.58 = bf16[32,6144]{1,0:T(8,128)(2,1)S(1)} collective-permute-done((bf16[32,6144]{1,0:T(8,128)(2,1)S(1)}, bf16[32,6144]{1,0:T(8,128)(2,1)S(1)}, u32[]{:S(2)}, u32[]{:S(2)}) %collective-permute-start.58) | collective-permute-done | bytes 393248 | tf_op jit(solution)/shard_map/ppermute | solution.py:493
  415.4 2.5 collective-permute-start.61
  417.9 2.4 fusion.11
  420.4 6.6 %collective-permute-done.59 = bf16[32,6144]{1,0:T(8,128)(2,1)S(1)} collective-permute-done((bf16[32,6144]{1,0:T(8,128)(2,1)S(1)}, bf16[32,6144]{1,0:T(8,128)(2,1)S(1)}, u32[]{:S(2)}, u32[]{:S(2)}) %collective-permute-start.59) | collective-permute-done | bytes 393248 | tf_op jit(solution)/shard_map/ppermute | solution.py:493
  426.9 14.9 %collective-permute-done.60 = bf16[32,6144]{1,0:T(8,128)(2,1)S(1)} collective-permute-done((bf16[32,6144]{1,0:T(8,128)(2,1)S(1)}, bf16[32,6144]{1,0:T(8,128)(2,1)S(1)}, u32[]{:S(2)}, u32[]{:S(2)}) %collective-permute-start.60) | collective-permute-done | bytes 393248 | tf_op jit(solution)/shard_map/ppermute | solution.py:493
  441.9 7.4 %collective-permute-done.61 = bf16[32,6144]{1,0:T(8,128)(2,1)S(1)} collective-permute-done((bf16[32,6144]{1,0:T(8,128)(2,1)S(1)}, bf16[32,6144]{1,0:T(8,128)(2,1)S(1)}, u32[]{:S(2)}, u32[]{:S(2)}) %collective-permute-start.61) | collective-permute-done | bytes 393248 | tf_op jit(solution)/shard_map/ppermute | solution.py:493
  449.3 2.4 fusion.15
  (220 shorter events, 64.9 us)
Async XLA Ops:
  4.1 12.7 %collective-permute-start.5 = (bf16[512,3200]{1,0:T(8,128)(2,1)S(1)}, bf16[512,3200]{1,0:T(8,128)(2,1)}, u32[]{:S(2)}, u32[]{:S(2)}) collective-permute-start(bf16[512,3200]{1,0:T(8,128)(2,1)S(1)} %reorder.1.refs_0_), channel_id=1, source_target_pairs={{0,1},{1,0},{2,3},{3,2},{4,5},{5,4},{6,7},{7,6},{8,9},{9,8},{10,11... | collective-permute-start | bytes 9830408 | tf_op jit(solution)/shard_map/ppermute | solution.py:490
  6.2 39.7 %collective-permute-start.3 = (bf16[2,64,3200]{2,1,0:T(8,128)(2,1)}, bf16[2,64,3200]{2,1,0:T(8,128)(2,1)}, u32[]{:S(2)}, u32[]{:S(2)}) collective-permute-start(bf16[2,64,3200]{2,1,0:T(8,128)(2,1)} %get-tuple-element.487), channel_id=1, source_target_pairs={{0,8},{4,12},{8,0},{12,4},{16,24},{20,28},{24,16},{28,20},{1,9},{5... | collective-permute-start | bytes 2457608 | tf_op jit(solution)/shard_map/ppermute | solution.py:493
  7.4 38.4 %collective-permute-start.1 = (bf16[128,3200]{1,0:T(8,128)(2,1)S(1)}, bf16[128,3200]{1,0:T(8,128)(2,1)S(1)}, u32[]{:S(2)}, u32[]{:S(2)}) collective-permute-start(bf16[128,3200]{1,0:T(8,128)(2,1)S(1)} %constant_dynamic-slice_fusion), channel_id=1, source_target_pairs={{0,2},{1,3},{2,0},{3,1},{4,6},{5,7},{6,4},{7,5},{8,10},{9,11},{10,... | collective-permute-start | bytes 2457608 | tf_op jit(solution)/shard_map/ppermute | solution.py:490
  10.4 35.5 %collective-permute-start.2 = (bf16[128,3200]{1,0:T(8,128)(2,1)S(1)}, bf16[128,3200]{1,0:T(8,128)(2,1)S(1)}, u32[]{:S(2)}, u32[]{:S(2)}) collective-permute-start(bf16[128,3200]{1,0:T(8,128)(2,1)S(1)} %get-tuple-element.484), channel_id=1, source_target_pairs={{0,2},{1,3},{2,0},{3,1},{4,6},{5,7},{6,4},{7,5},{8,10},{9,11},{10,... | collective-permute-start | bytes 2457608 | tf_op jit(solution)/shard_map/ppermute | solution.py:490
  10.6 35.3 %collective-permute-start.4 = (bf16[1,64,3200]{2,1,0:T(8,128)(2,1)S(1)}, bf16[1,64,3200]{2,1,0:T(8,128)(2,1)S(1)}, u32[]{:S(2)}, u32[]{:S(2)}) collective-permute-start(bf16[1,64,3200]{2,1,0:T(8,128)(2,1)S(1)} %dynamic-slice_bitcast_fusion.4), channel_id=1, source_target_pairs={{0,16},{4,20},{8,24},{12,28},{16,0},{20,4},{24,8},{28,12},{1,17},{... | collective-permute-start | bytes 1228808 | tf_op jit(solution)/shard_map/ppermute | solution.py:493
  16.8 29.1 %collective-permute-start = (s32[1]{0:T(128)}, s32[1]{0:T(128)}, u32[]{:S(2)}, u32[]{:S(2)}) collective-permute-start(s32[1]{0:T(128)} %bitcast.4.refs_0_), channel_id=1, source_target_pairs={{0,2},{1,3},{2,0},{3,1},{4,6},{5,7},{6,4},{7,5},{8,10},{9,11},{10,... | collective-permute-start | bytes 20 | tf_op jit(solution)/shard_map/ppermute | solution.py:490
  45.9 37.6 %collective-permute-start.6 = (bf16[256,3200]{1,0:T(8,128)(2,1)}, bf16[256,3200]{1,0:T(8,128)(2,1)}, u32[]{:S(2)}, u32[]{:S(2)}) collective-permute-start(bf16[256,3200]{1,0:T(8,128)(2,1)} %slice.102), channel_id=1, source_target_pairs={{0,2},{1,3},{2,0},{3,1},{4,6},{5,7},{6,4},{7,5},{8,10},{9,11},{10,... | collective-permute-start | bytes 4915208 | tf_op jit(solution)/shard_map/ppermute | solution.py:490
  47.6 3.4 collective-permute-start.8
  47.6 20.7 %collective-permute-start.10 = (bf16[128,3200]{1,0:T(8,128)(2,1)S(1)}, bf16[128,3200]{1,0:T(8,128)(2,1)S(1)}, u32[]{:S(2)}, u32[]{:S(2)}) collective-permute-start(bf16[128,3200]{1,0:T(8,128)(2,1)S(1)} %collective-permute-done.1.refs_10_), channel_id=1, source_target_pairs={{0,4},{4,0},{8,12},{12,8},{16,20},{20,16},{24,28},{28,24},{1,5},{5... | collective-permute-start | bytes 2457608 | tf_op jit(solution)/shard_map/ppermute | solution.py:496
  49.1 19.1 %collective-permute-start.11 = (bf16[128,3200]{1,0:T(8,128)(2,1)S(1)}, bf16[128,3200]{1,0:T(8,128)(2,1)S(1)}, u32[]{:S(2)}, u32[]{:S(2)}) collective-permute-start(bf16[128,3200]{1,0:T(8,128)(2,1)S(1)} %collective-permute-done.1.refs_10_), channel_id=1, source_target_pairs={{0,1},{1,0},{2,3},{3,2},{4,5},{5,4},{6,7},{7,6},{8,9},{9,8},{10,11... | collective-permute-start | bytes 2457608 | tf_op jit(solution)/shard_map/ppermute | solution.py:490
  49.4 21.1 %collective-permute-start.9 = (bf16[128,3200]{1,0:T(8,128)(2,1)S(1)}, bf16[128,3200]{1,0:T(8,128)(2,1)S(1)}, u32[]{:S(2)}, u32[]{:S(2)}) collective-permute-start(bf16[128,3200]{1,0:T(8,128)(2,1)S(1)} %collective-permute-done.1.refs_10_), channel_id=1, source_target_pairs={{0,8},{4,12},{8,0},{12,4},{16,24},{20,28},{24,16},{28,20},{1,9},{5... | collective-permute-start | bytes 2457608 | tf_op jit(solution)/shard_map/ppermute | solution.py:493
  51.0 11.4 %collective-permute-start.7 = (bf16[1,64,3200]{2,1,0:T(8,128)(2,1)S(1)}, bf16[1,64,3200]{2,1,0:T(8,128)(2,1)S(1)}, u32[]{:S(2)}, u32[]{:S(2)}) collective-permute-start(bf16[1,64,3200]{2,1,0:T(8,128)(2,1)S(1)} %slice.84), channel_id=1, source_target_pairs={{0,24},{4,28},{8,16},{12,20},{16,8},{20,12},{24,0},{28,4},{1,25},{... | collective-permute-start | bytes 1228808 | tf_op jit(solution)/shard_map/ppermute | solution.py:493
  83.5 3.8 collective-permute-start.13
  83.5 24.2 %collective-permute-start.12 = (bf16[128,3200]{1,0:T(8,128)(2,1)}, bf16[128,3200]{1,0:T(8,128)(2,1)}, u32[]{:S(2)}, u32[]{:S(2)}) collective-permute-start(bf16[128,3200]{1,0:T(8,128)(2,1)} %get-tuple-element.262), channel_id=1, source_target_pairs={{0,2},{1,3},{2,0},{3,1},{4,6},{5,7},{6,4},{7,5},{8,10},{9,11},{10,... | collective-permute-start | bytes 2457608 | tf_op jit(solution)/shard_map/ppermute | solution.py:490
  84.9 22.8 %collective-permute-start.14 = (bf16[128,3200]{1,0:T(8,128)(2,1)S(1)}, bf16[128,3200]{1,0:T(8,128)(2,1)S(1)}, u32[]{:S(2)}, u32[]{:S(2)}) collective-permute-start(bf16[128,3200]{1,0:T(8,128)(2,1)S(1)} %collective-permute-done.9.refs_11_), channel_id=1, source_target_pairs={{0,4},{4,0},{8,12},{12,8},{16,20},{20,16},{24,28},{28,24},{1,5},{5... | collective-permute-start | bytes 2457608 | tf_op jit(solution)/shard_map/ppermute | solution.py:496
  86.4 21.3 %collective-permute-start.15 = (bf16[128,3200]{1,0:T(8,128)(2,1)S(1)}, bf16[128,3200]{1,0:T(8,128)(2,1)S(1)}, u32[]{:S(2)}, u32[]{:S(2)}) collective-permute-start(bf16[128,3200]{1,0:T(8,128)(2,1)S(1)} %collective-permute-done.9.refs_11_), channel_id=1, source_target_pairs={{0,1},{1,0},{2,3},{3,2},{4,5},{5,4},{6,7},{7,6},{8,9},{9,8},{10,11... | collective-permute-start | bytes 2457608 | tf_op jit(solution)/shard_map/ppermute | solution.py:490
  86.4 21.3 %collective-permute-start.16 = (bf16[128,3200]{1,0:T(8,128)(2,1)S(1)}, bf16[128,3200]{1,0:T(8,128)(2,1)S(1)}, u32[]{:S(2)}, u32[]{:S(2)}) collective-permute-start(bf16[128,3200]{1,0:T(8,128)(2,1)S(1)} %collective-permute-done.10.refs_12_), channel_id=1, source_target_pairs={{0,1},{1,0},{2,3},{3,2},{4,5},{5,4},{6,7},{7,6},{8,9},{9,8},{10,11... | collective-permute-start | bytes 2457608 | tf_op jit(solution)/shard_map/ppermute | solution.py:490
  87.3 20.3 %collective-permute-start.17 = (bf16[1,64,3200]{2,1,0:T(8,128)(2,1)S(1)}, bf16[1,64,3200]{2,1,0:T(8,128)(2,1)S(1)}, u32[]{:S(2)}, u32[]{:S(2)}) collective-permute-start(bf16[1,64,3200]{2,1,0:T(8,128)(2,1)S(1)} %slice.85), channel_id=1, source_target_pairs={{0,16},{4,20},{8,24},{12,28},{16,0},{20,4},{24,8},{28,12},{1,17},{... | collective-permute-start | bytes 1228808 | tf_op jit(solution)/shard_map/ppermute | solution.py:493
  107.7 3.0 collective-permute-start.18
  107.8 93.2 %collective-permute-start.33 = (bf16[512,3200]{1,0:T(8,128)(2,1)}, bf16[512,3200]{1,0:T(8,128)(2,1)}, u32[]{:S(2)}, u32[]{:S(2)}) collective-permute-start(bf16[512,3200]{1,0:T(8,128)(2,1)} %refs_8_.1), channel_id=1, source_target_pairs={{0,1},{1,0},{2,3},{3,2},{4,5},{5,4},{6,7},{7,6},{8,9},{9,8},{10,11... | collective-permute-start | bytes 9830408 | tf_op jit(solution)/shard_map/ppermute | solution.py:490
  121.1 3.2 collective-permute-start.21
  122.3 4.8 %collective-permute-start.22 = (bf16[128,3200]{1,0:T(8,128)(2,1)S(1)}, bf16[128,3200]{1,0:T(8,128)(2,1)S(1)}, u32[]{:S(2)}, u32[]{:S(2)}) collective-permute-start(bf16[128,3200]{1,0:T(8,128)(2,1)S(1)} %collective-permute-done.14.refs_13_), channel_id=1, source_target_pairs={{0,1},{1,0},{2,3},{3,2},{4,5},{5,4},{6,7},{7,6},{8,9},{9,8},{10,11... | collective-permute-start | bytes 2457608 | tf_op jit(solution)/shard_map/ppermute | solution.py:490
  122.7 3.7 collective-permute-start.20
  123.3 3.2 collective-permute-start.19
  128.1 19.2 %collective-permute-start.23 = (bf16[1,64,3200]{2,1,0:T(8,128)(2,1)S(1)}, bf16[1,64,3200]{2,1,0:T(8,128)(2,1)S(1)}, u32[]{:S(2)}, u32[]{:S(2)}) collective-permute-start(bf16[1,64,3200]{2,1,0:T(8,128)(2,1)S(1)} %slice.96), channel_id=1, source_target_pairs={{0,24},{4,28},{8,16},{12,20},{16,8},{20,12},{24,0},{28,4},{1,25},{... | collective-permute-start | bytes 1228808 | tf_op jit(solution)/shard_map/ppermute | solution.py:493
  148.1 14.4 %collective-permute-start.24 = (bf16[256,512]{1,0:T(8,128)(2,1)}, bf16[256,512]{1,0:T(8,128)(2,1)S(1)}, u32[]{:S(2)}, u32[]{:S(2)}) collective-permute-start(bf16[256,512]{1,0:T(8,128)(2,1)} %get-tuple-element.320), channel_id=1, source_target_pairs={{0,1},{1,0},{2,3},{3,2},{4,5},{5,4},{6,7},{7,6},{8,9},{9,8},{10,11... | collective-permute-start | bytes 786440 | tf_op jit(solution)/shard_map/ppermute | solution.py:490
  148.1 14.4 %collective-permute-start.25 = (bf16[256,512]{1,0:T(8,128)(2,1)}, bf16[256,512]{1,0:T(8,128)(2,1)S(1)}, u32[]{:S(2)}, u32[]{:S(2)}) collective-permute-start(bf16[256,512]{1,0:T(8,128)(2,1)} %get-tuple-element.321), channel_id=1, source_target_pairs={{0,2},{1,3},{2,0},{3,1},{4,6},{5,7},{6,4},{7,5},{8,10},{9,11},{10,... | collective-permute-start | bytes 786440 | tf_op jit(solution)/shard_map/ppermute | solution.py:490
  148.7 13.8 %collective-permute-start.26 = (bf16[256,512]{1,0:T(8,128)(2,1)}, bf16[256,512]{1,0:T(8,128)(2,1)S(1)}, u32[]{:S(2)}, u32[]{:S(2)}) collective-permute-start(bf16[256,512]{1,0:T(8,128)(2,1)} %get-tuple-element.322), channel_id=1, source_target_pairs={{0,3},{1,2},{2,1},{3,0},{4,7},{5,6},{6,5},{7,4},{8,11},{9,10},{10,... | collective-permute-start | bytes 786440 | tf_op jit(solution)/shard_map/ppermute | solution.py:490
  149.9 51.1 %copy-start.14 = (bf16[1,64,3200]{2,1,0:T(8,128)(2,1)S(1)}, bf16[1,64,3200]{2,1,0:T(8,128)(2,1)}, u32[]{:S(2)}) copy-start(bf16[1,64,3200]{2,1,0:T(8,128)(2,1)} %copy-done.13) | copy-start | bytes 1228804
  162.5 9.8 %collective-permute-start.30 = (bf16[256,512]{1,0:T(8,128)(2,1)}, bf16[256,512]{1,0:T(8,128)(2,1)S(1)}, u32[]{:S(2)}, u32[]{:S(2)}) collective-permute-start(bf16[256,512]{1,0:T(8,128)(2,1)} %get-tuple-element.332), channel_id=1, source_target_pairs={{0,1},{1,0},{2,3},{3,2},{4,5},{5,4},{6,7},{7,6},{8,9},{9,8},{10,11... | collective-permute-start | bytes 786440 | tf_op jit(solution)/shard_map/ppermute | solution.py:490
  162.8 9.5 %collective-permute-start.31 = (bf16[256,512]{1,0:T(8,128)(2,1)}, bf16[256,512]{1,0:T(8,128)(2,1)S(1)}, u32[]{:S(2)}, u32[]{:S(2)}) collective-permute-start(bf16[256,512]{1,0:T(8,128)(2,1)} %get-tuple-element.333), channel_id=1, source_target_pairs={{0,2},{1,3},{2,0},{3,1},{4,6},{5,7},{6,4},{7,5},{8,10},{9,11},{10,... | collective-permute-start | bytes 786440 | tf_op jit(solution)/shard_map/ppermute | solution.py:490
  163.5 12.9 %collective-permute-start.32 = (bf16[256,512]{1,0:T(8,128)(2,1)}, bf16[256,512]{1,0:T(8,128)(2,1)S(1)}, u32[]{:S(2)}, u32[]{:S(2)}) collective-permute-start(bf16[256,512]{1,0:T(8,128)(2,1)} %get-tuple-element.334), channel_id=1, source_target_pairs={{0,3},{1,2},{2,1},{3,0},{4,7},{5,6},{6,5},{7,4},{8,11},{9,10},{10,... | collective-permute-start | bytes 786440 | tf_op jit(solution)/shard_map/ppermute | solution.py:490
  164.5 15.2 %collective-permute-start.27 = (bf16[64,2048]{1,0:T(8,128)(2,1)S(1)}, bf16[64,2048]{1,0:T(8,128)(2,1)S(1)}, u32[]{:S(2)}, u32[]{:S(2)}) collective-permute-start(bf16[64,2048]{1,0:T(8,128)(2,1)S(1)} %get-tuple-element.328), channel_id=1, source_target_pairs={{0,8},{4,12},{8,0},{12,4},{16,24},{20,28},{24,16},{28,20},{1,9},{5... | collective-permute-start | bytes 786440 | tf_op jit(solution)/shard_map/ppermute | solution.py:493
  172.3 17.7 %collective-permute-start.28 = (bf16[64,2048]{1,0:T(8,128)(2,1)S(1)}, bf16[64,2048]{1,0:T(8,128)(2,1)S(1)}, u32[]{:S(2)}, u32[]{:S(2)}) collective-permute-start(bf16[64,2048]{1,0:T(8,128)(2,1)S(1)} %get-tuple-element.329), channel_id=1, source_target_pairs={{0,16},{4,20},{8,24},{12,28},{16,0},{20,4},{24,8},{28,12},{1,17},{... | collective-permute-start | bytes 786440 | tf_op jit(solution)/shard_map/ppermute | solution.py:493
  172.3 25.2 %collective-permute-start.29 = (bf16[64,2048]{1,0:T(8,128)(2,1)S(1)}, bf16[64,2048]{1,0:T(8,128)(2,1)S(1)}, u32[]{:S(2)}, u32[]{:S(2)}) collective-permute-start(bf16[64,2048]{1,0:T(8,128)(2,1)S(1)} %get-tuple-element.330), channel_id=1, source_target_pairs={{0,24},{4,28},{8,16},{12,20},{16,8},{20,12},{24,0},{28,4},{1,25},{... | collective-permute-start | bytes 786440 | tf_op jit(solution)/shard_map/ppermute | solution.py:493
  197.5 14.6 %collective-permute-start.34 = (bf16[64,2048]{1,0:T(8,128)(2,1)S(1)}, bf16[64,2048]{1,0:T(8,128)(2,1)S(1)}, u32[]{:S(2)}, u32[]{:S(2)}) collective-permute-start(bf16[64,2048]{1,0:T(8,128)(2,1)S(1)} %get-tuple-element.359), channel_id=1, source_target_pairs={{0,8},{4,12},{8,0},{12,4},{16,24},{20,28},{24,16},{28,20},{1,9},{5... | collective-permute-start | bytes 786440 | tf_op jit(solution)/shard_map/ppermute | solution.py:493
  197.5 19.9 %collective-permute-start.35 = (bf16[64,2048]{1,0:T(8,128)(2,1)S(1)}, bf16[64,2048]{1,0:T(8,128)(2,1)S(1)}, u32[]{:S(2)}, u32[]{:S(2)}) collective-permute-start(bf16[64,2048]{1,0:T(8,128)(2,1)S(1)} %get-tuple-element.360), channel_id=1, source_target_pairs={{0,16},{4,20},{8,24},{12,28},{16,0},{20,4},{24,8},{28,12},{1,17},{... | collective-permute-start | bytes 786440 | tf_op jit(solution)/shard_map/ppermute | solution.py:493
  199.4 24.2 %collective-permute-start.36 = (bf16[64,2048]{1,0:T(8,128)(2,1)S(1)}, bf16[64,2048]{1,0:T(8,128)(2,1)S(1)}, u32[]{:S(2)}, u32[]{:S(2)}) collective-permute-start(bf16[64,2048]{1,0:T(8,128)(2,1)S(1)} %get-tuple-element.361), channel_id=1, source_target_pairs={{0,24},{4,28},{8,16},{12,20},{16,8},{20,12},{24,0},{28,4},{1,25},{... | collective-permute-start | bytes 786440 | tf_op jit(solution)/shard_map/ppermute | solution.py:493
  224.3 5.1 %collective-permute-start.37 = (f32[3,256]{1,0:T(4,128)}, f32[3,256]{1,0:T(4,128)}, u32[]{:S(2)}, u32[]{:S(2)}) collective-permute-start(f32[3,256]{1,0:T(4,128)} %get-tuple-element.424.refs_0_), channel_id=1, source_target_pairs={{0,8},{4,12},{8,0},{12,4},{16,24},{20,28},{24,16},{28,20},{1,9},{5... | collective-permute-start | bytes 9224 | tf_op jit(solution)/shard_map/ppermute | solution.py:493
  224.3 5.1 %collective-permute-start.38 = (f32[3,256]{1,0:T(4,128)}, f32[3,256]{1,0:T(4,128)}, u32[]{:S(2)}, u32[]{:S(2)}) collective-permute-start(f32[3,256]{1,0:T(4,128)} %get-tuple-element.424.refs_0_), channel_id=1, source_target_pairs={{0,16},{4,20},{8,24},{12,28},{16,0},{20,4},{24,8},{28,12},{1,17},{... | collective-permute-start | bytes 9224 | tf_op jit(solution)/shard_map/ppermute | solution.py:493
  226.2 3.9 collective-permute-start.39
  234.7 21.9 %collective-permute-start.40 = (bf16[256,1664]{1,0:T(8,128)(2,1)S(1)}, bf16[256,1664]{1,0:T(8,128)(2,1)S(1)}, u32[]{:S(2)}, u32[]{:S(2)}) collective-permute-start(bf16[256,1664]{1,0:T(8,128)(2,1)S(1)} %get-tuple-element.371), channel_id=1, source_target_pairs={{0,4},{4,0},{8,12},{12,8},{16,20},{20,16},{24,28},{28,24},{1,5},{5... | collective-permute-start | bytes 2555912 | tf_op jit(solution)/shard_map/ppermute | solution.py:496
  246.1 3.6 collective-permute-start.41
  248.0 4.5 collective-permute-start.42
  249.2 3.6 collective-permute-start.43
  256.6 18.3 %collective-permute-start.44 = (bf16[256,1664]{1,0:T(8,128)(2,1)S(1)}, bf16[256,1664]{1,0:T(8,128)(2,1)S(1)}, u32[]{:S(2)}, u32[]{:S(2)}) collective-permute-start(bf16[256,1664]{1,0:T(8,128)(2,1)S(1)} %get-tuple-element.387), channel_id=1, source_target_pairs={{0,4},{4,0},{8,12},{12,8},{16,20},{20,16},{24,28},{28,24},{1,5},{5... | collective-permute-start | bytes 2555912 | tf_op jit(solution)/shard_map/ppermute | solution.py:496
  274.9 35.0 %collective-permute-start.45 = (bf16[128,6144]{1,0:T(8,128)(2,1)S(1)}, bf16[128,6144]{1,0:T(8,128)(2,1)S(1)}, u32[]{:S(2)}, u32[]{:S(2)}) collective-permute-start(bf16[128,6144]{1,0:T(8,128)(2,1)S(1)} %get-tuple-element.407), channel_id=1, source_target_pairs={{0,4},{4,0},{8,12},{12,8},{16,20},{20,16},{24,28},{28,24},{1,5},{5... | collective-permute-start | bytes 4718600 | tf_op jit(solution)/shard_map/ppermute | solution.py:496
  293.2 49.5 %copy-start.8 = (bf16[128,6144]{1,0:T(8,128)(2,1)S(1)}, bf16[128,6144]{1,0:T(8,128)(2,1)}, u32[]{:S(2)}) copy-start(bf16[128,6144]{1,0:T(8,128)(2,1)} %get-tuple-element.432.refs_0_) | copy-start | bytes 4718596
  310.0 32.8 %collective-permute-start.46 = (bf16[128,6144]{1,0:T(8,128)(2,1)S(1)}, bf16[128,6144]{1,0:T(8,128)(2,1)S(1)}, u32[]{:S(2)}, u32[]{:S(2)}) collective-permute-start(bf16[128,6144]{1,0:T(8,128)(2,1)S(1)} %copy-done.46), channel_id=1, source_target_pairs={{0,4},{4,0},{8,12},{12,8},{16,20},{20,16},{24,28},{28,24},{1,5},{5... | collective-permute-start | bytes 4718600 | tf_op jit(solution)/shard_map/ppermute | solution.py:496
  312.8 28.1 %collective-permute-start.47 = (bf16[32,6144]{1,0:T(8,128)(2,1)S(1)}, bf16[32,6144]{1,0:T(8,128)(2,1)S(1)}, u32[]{:S(2)}, u32[]{:S(2)}) collective-permute-start(bf16[32,6144]{1,0:T(8,128)(2,1)S(1)} %get-tuple-element.421), channel_id=1, source_target_pairs={{0,8},{4,12},{8,0},{12,4},{16,24},{20,28},{24,16},{28,20},{1,9},{5... | collective-permute-start | bytes 1179656 | tf_op jit(solution)/shard_map/ppermute | solution.py:493
  316.0 24.9 %collective-permute-start.48 = (bf16[32,6144]{1,0:T(8,128)(2,1)S(1)}, bf16[32,6144]{1,0:T(8,128)(2,1)S(1)}, u32[]{:S(2)}, u32[]{:S(2)}) collective-permute-start(bf16[32,6144]{1,0:T(8,128)(2,1)S(1)} %get-tuple-element.422), channel_id=1, source_target_pairs={{0,16},{4,20},{8,24},{12,28},{16,0},{20,4},{24,8},{28,12},{1,17},{... | collective-permute-start | bytes 1179656 | tf_op jit(solution)/shard_map/ppermute | solution.py:493
  316.1 26.6 %collective-permute-start.49 = (bf16[32,6144]{1,0:T(8,128)(2,1)S(1)}, bf16[32,6144]{1,0:T(8,128)(2,1)S(1)}, u32[]{:S(2)}, u32[]{:S(2)}) collective-permute-start(bf16[32,6144]{1,0:T(8,128)(2,1)S(1)} %get-tuple-element.423), channel_id=1, source_target_pairs={{0,24},{4,28},{8,16},{12,20},{16,8},{20,12},{24,0},{28,4},{1,25},{... | collective-permute-start | bytes 1179656 | tf_op jit(solution)/shard_map/ppermute | solution.py:493
  324.8 16.1 %collective-permute-start.50 = (f32[4]{0:T(128)S(1)}, f32[4]{0:T(128)S(1)}, u32[]{:S(2)}, u32[]{:S(2)}) collective-permute-start(f32[4]{0:T(128)S(1)} %pad_maximum_fusion), channel_id=1, source_target_pairs={{0,4},{4,0},{8,12},{12,8},{16,20},{20,16},{24,28},{28,24},{1,5},{5... | collective-permute-start | bytes 56 | tf_op jit(solution)/shard_map/ppermute | solution.py:496
  343.5 13.0 %collective-permute-start.52 = (bf16[32,6144]{1,0:T(8,128)(2,1)S(1)}, bf16[32,6144]{1,0:T(8,128)(2,1)S(1)}, u32[]{:S(2)}, u32[]{:S(2)}) collective-permute-start(bf16[32,6144]{1,0:T(8,128)(2,1)S(1)} %get-tuple-element.435), channel_id=1, source_target_pairs={{0,8},{4,12},{8,0},{12,4},{16,24},{20,28},{24,16},{28,20},{1,9},{5... | collective-permute-start | bytes 1179656 | tf_op jit(solution)/shard_map/ppermute | solution.py:493
  345.0 25.9 %collective-permute-start.53 = (bf16[32,6144]{1,0:T(8,128)(2,1)S(1)}, bf16[32,6144]{1,0:T(8,128)(2,1)S(1)}, u32[]{:S(2)}, u32[]{:S(2)}) collective-permute-start(bf16[32,6144]{1,0:T(8,128)(2,1)S(1)} %get-tuple-element.436), channel_id=1, source_target_pairs={{0,16},{4,20},{8,24},{12,28},{16,0},{20,4},{24,8},{28,12},{1,17},{... | collective-permute-start | bytes 1179656 | tf_op jit(solution)/shard_map/ppermute | solution.py:493
  345.6 31.9 %collective-permute-start.54 = (bf16[32,6144]{1,0:T(8,128)(2,1)S(1)}, bf16[32,6144]{1,0:T(8,128)(2,1)S(1)}, u32[]{:S(2)}, u32[]{:S(2)}) collective-permute-start(bf16[32,6144]{1,0:T(8,128)(2,1)S(1)} %get-tuple-element.437), channel_id=1, source_target_pairs={{0,24},{4,28},{8,16},{12,20},{16,8},{20,12},{24,0},{28,4},{1,25},{... | collective-permute-start | bytes 1179656 | tf_op jit(solution)/shard_map/ppermute | solution.py:493
  347.1 33.7 %collective-permute-start.51 = (bf16[128,6144]{1,0:T(8,128)(2,1)S(1)}, bf16[128,6144]{1,0:T(8,128)(2,1)S(1)}, u32[]{:S(2)}, u32[]{:S(2)}) collective-permute-start(bf16[128,6144]{1,0:T(8,128)(2,1)S(1)} %get-tuple-element.431), channel_id=1, source_target_pairs={{0,4},{4,0},{8,12},{12,8},{16,20},{20,16},{24,28},{28,24},{1,5},{5... | collective-permute-start | bytes 4718600 | tf_op jit(solution)/shard_map/ppermute | solution.py:496
  380.8 32.6 %collective-permute-start.55 = (bf16[128,6144]{1,0:T(8,128)(2,1)S(1)}, bf16[128,6144]{1,0:T(8,128)(2,1)S(1)}, u32[]{:S(2)}, u32[]{:S(2)}) collective-permute-start(bf16[128,6144]{1,0:T(8,128)(2,1)S(1)} %copy-done.45), channel_id=1, source_target_pairs={{0,4},{4,0},{8,12},{12,8},{16,20},{20,16},{24,28},{28,24},{1,5},{5... | collective-permute-start | bytes 4718600 | tf_op jit(solution)/shard_map/ppermute | solution.py:496
  382.2 15.0 %collective-permute-start.56 = (bf16[32,6144]{1,0:T(8,128)(2,1)S(1)}, bf16[32,6144]{1,0:T(8,128)(2,1)S(1)}, u32[]{:S(2)}, u32[]{:S(2)}) collective-permute-start(bf16[32,6144]{1,0:T(8,128)(2,1)S(1)} %get-tuple-element.449), channel_id=1, source_target_pairs={{0,8},{4,12},{8,0},{12,4},{16,24},{20,28},{24,16},{28,20},{1,9},{5... | collective-permute-start | bytes 1179656 | tf_op jit(solution)/shard_map/ppermute | solution.py:493
  386.0 20.1 %collective-permute-start.57 = (bf16[32,6144]{1,0:T(8,128)(2,1)S(1)}, bf16[32,6144]{1,0:T(8,128)(2,1)S(1)}, u32[]{:S(2)}, u32[]{:S(2)}) collective-permute-start(bf16[32,6144]{1,0:T(8,128)(2,1)S(1)} %get-tuple-element.450), channel_id=1, source_target_pairs={{0,16},{4,20},{8,24},{12,28},{16,0},{20,4},{24,8},{28,12},{1,17},{... | collective-permute-start | bytes 1179656 | tf_op jit(solution)/shard_map/ppermute | solution.py:493
  386.1 27.3 %collective-permute-start.58 = (bf16[32,6144]{1,0:T(8,128)(2,1)S(1)}, bf16[32,6144]{1,0:T(8,128)(2,1)S(1)}, u32[]{:S(2)}, u32[]{:S(2)}) collective-permute-start(bf16[32,6144]{1,0:T(8,128)(2,1)S(1)} %get-tuple-element.451), channel_id=1, source_target_pairs={{0,24},{4,28},{8,16},{12,20},{16,8},{20,12},{24,0},{28,4},{1,25},{... | collective-permute-start | bytes 1179656 | tf_op jit(solution)/shard_map/ppermute | solution.py:493
  414.4 12.6 %collective-permute-start.59 = (bf16[32,6144]{1,0:T(8,128)(2,1)S(1)}, bf16[32,6144]{1,0:T(8,128)(2,1)S(1)}, u32[]{:S(2)}, u32[]{:S(2)}) collective-permute-start(bf16[32,6144]{1,0:T(8,128)(2,1)S(1)} %get-tuple-element.461), channel_id=1, source_target_pairs={{0,8},{4,12},{8,0},{12,4},{16,24},{20,28},{24,16},{28,20},{1,9},{5... | collective-permute-start | bytes 1179656 | tf_op jit(solution)/shard_map/ppermute | solution.py:493
  414.9 26.9 %collective-permute-start.60 = (bf16[32,6144]{1,0:T(8,128)(2,1)S(1)}, bf16[32,6144]{1,0:T(8,128)(2,1)S(1)}, u32[]{:S(2)}, u32[]{:S(2)}) collective-permute-start(bf16[32,6144]{1,0:T(8,128)(2,1)S(1)} %get-tuple-element.462), channel_id=1, source_target_pairs={{0,16},{4,20},{8,24},{12,28},{16,0},{20,4},{24,8},{28,12},{1,17},{... | collective-permute-start | bytes 1179656 | tf_op jit(solution)/shard_map/ppermute | solution.py:493
  415.4 33.8 %collective-permute-start.61 = (bf16[32,6144]{1,0:T(8,128)(2,1)S(1)}, bf16[32,6144]{1,0:T(8,128)(2,1)S(1)}, u32[]{:S(2)}, u32[]{:S(2)}) collective-permute-start(bf16[32,6144]{1,0:T(8,128)(2,1)S(1)} %get-tuple-element.463), channel_id=1, source_target_pairs={{0,24},{4,28},{8,16},{12,20},{16,8},{20,12},{24,0},{28,4},{1,25},{... | collective-permute-start | bytes 1179656 | tf_op jit(solution)/shard_map/ppermute | solution.py:493
  (46 other events, 683.7 us)
